TPU v7x, 32 devices: a whole 2x2x4 slice. The times are simulated.
32 devices in a mesh: rep: 2 (over x), seq: 16 (over z, y, core).
Axes of the slice: x: 2, y: 2, z: 4, core: 2. Of those that a mesh axis runs over, the one named last changes fastest.
Arguments:
- q_stream: bfloat16 [4096, 8192], P(('rep', 'seq')), parts along dimension 0, may hold values from -6 to 6
- k_stream: bfloat16 [4096, 8192], P(('rep', 'seq')), parts along dimension 0, may hold values from -6 to 6
- v_stream: bfloat16 [4096, 8192], P(('rep', 'seq')), parts along dimension 0, may hold values from -6 to 6
- feat_filter: float32 [3, 3, 8192], replicated, may hold values from -3.5 to 3.5
- long_filter: bfloat16 [512, 128], replicated, may hold values from -0.5 to 0.5
- skip_gain: float32 [8192], replicated, may hold values from -3 to 3
Outputs:
- mixed: bfloat16 [4096, 8192], P(('rep', 'seq')), parts along dimension 0
There are 2 independent parts, one for each index of `rep`. A program takes and returns all parts, laid end to end along the dimension named above; an argument that names none is the same for every part. Nothing has to cross between parts.
All inputs are finite; a program needn't handle non-finite values.
Results may differ from a plain program's by a relative error of at most 0.005.
Values may be sent and summed in bfloat16 or wider, within the bound.
No kernel may reach another device: no remote copies, remote signals or barrier semaphores. Data moves between devices by JAX's collectives and lax.ppermute only.
A program may use at most 128 MiB of HBM per device.

v0:
```python
import jax
import jax.numpy as jnp
from jax import lax
from jax.sharding import PartitionSpec as P

GROUP_CH = 16
FILT = 128
FEAT = 3


def passed_along(shard, axis, by):
    length = lax.axis_size(axis)
    pairs = [(i, i + by) for i in range(length) if 0 <= i + by < length]
    return lax.ppermute(shard, axis, pairs)


def featurize(rim, local, taps):
    length = local.shape[0]
    extended = jnp.concatenate([rim, local], axis=0).astype(jnp.float32)
    total = taps[0] * extended[FEAT - 1 : FEAT - 1 + length]
    for j in range(1, FEAT):
        total = total + taps[j] * extended[FEAT - 1 - j : FEAT - 1 - j + length]
    return total


def causal_blocks(current, earlier, filters):
    length, width = current.shape
    count = length // FILT
    groups = filters.shape[0]
    blocks = current.reshape(count, FILT, groups, GROUP_CH)
    before = jnp.concatenate([earlier.reshape(1, FILT, groups, GROUP_CH), blocks[:-1]], axis=0)
    window = jnp.concatenate([before, blocks], axis=1)
    rows = lax.broadcasted_iota(jnp.int32, (FILT, 2 * FILT), 0)
    cols = lax.broadcasted_iota(jnp.int32, (FILT, 2 * FILT), 1)
    lags = FILT + rows - cols
    picks = jnp.arange(FILT, dtype=jnp.int32)
    onehot = (lags[None, :, :] == picks[:, None, None]).astype(jnp.bfloat16)
    toeplitz = jnp.einsum(
        "gk,kts->gts", filters, onehot, preferred_element_type=jnp.float32
    ).astype(jnp.bfloat16)
    result = jnp.einsum("gts,bsgc->btgc", toeplitz, window, preferred_element_type=jnp.float32)
    return result.reshape(length, width)


def shards(q_stream, k_stream, v_stream, feat_filter, long_filter, skip_gain):
    rows, width = q_stream.shape
    edge = FEAT - 1
    rims = passed_along(
        (q_stream[rows - edge :], k_stream[rows - edge :], v_stream[rows - edge :]), "seq", 1
    )
    q_feat = featurize(rims[0], q_stream, feat_filter[0])
    k_feat = featurize(rims[1], k_stream, feat_filter[1])
    v_feat = featurize(rims[2], v_stream, feat_filter[2])
    gated = (k_feat * v_feat).astype(jnp.bfloat16)
    trailing = passed_along(gated[rows - FILT + 1 :], "seq", 1)
    earlier = jnp.concatenate([jnp.zeros((1, width), jnp.bfloat16), trailing], axis=0)
    conv = causal_blocks(gated, earlier, long_filter)
    mixed = q_feat * (conv + skip_gain * gated.astype(jnp.float32))
    return mixed.astype(jnp.bfloat16)


def solution(mesh):
    in_specs = (
        P(("rep", "seq"), None),
        P(("rep", "seq"), None),
        P(("rep", "seq"), None),
        P(),
        P(),
        P(),
    )
    out_specs = P(("rep", "seq"), None)
    return jax.shard_map(shards, mesh=mesh, in_specs=in_specs, out_specs=out_specs, check_vma=False)
```

profile of v0, /device:TPU:0, one launch (start us, length us, event | category | flops | bytes accessed | tf_op | source)
XLA Modules:
  0.0 137.5 jit_solution(12762081072262178950)
XLA Ops:
  0.0 0.0 copy-start
  0.0 1.1 slice.88
  1.1 2.4 %collective-permute-start = (bf16[2,8192]{1,0:T(2,128)(2,1)S(1)}, bf16[2,8192]{1,0:T(2,128)(2,1)S(1)}, u32[]{:S(2)}, u32[]{:S(2)}) collective-permute-start(bf16[2,8192]{1,0:T(2,128)(2,1)S(1)} %slice.88), channel_id=1, source_target_pairs={{0,1},{1,2},{2,3},{3,4},{4,5},{5,6},{6,7},{7,8},{8,9},{9,10},{10,1... | collective-permute-start | bytes 98312 | tf_op jit(solution)/shard_map/ppermute | solution.py:14
  3.5 0.9 slice.102
  4.4 4.5 %collective-permute-start.2 = (bf16[2,8192]{1,0:T(2,128)(2,1)S(1)}, bf16[2,8192]{1,0:T(2,128)(2,1)S(1)}, u32[]{:S(2)}, u32[]{:S(2)}) collective-permute-start(bf16[2,8192]{1,0:T(2,128)(2,1)S(1)} %slice.102), channel_id=1, source_target_pairs={{0,1},{1,2},{2,3},{3,4},{4,5},{5,6},{6,7},{7,8},{8,9},{9,10},{10,1... | collective-permute-start | bytes 98312 | tf_op jit(solution)/shard_map/ppermute | solution.py:14
  9.0 0.9 slice.95
  9.9 1.9 %collective-permute-start.1 = (bf16[2,8192]{1,0:T(2,128)(2,1)S(1)}, bf16[2,8192]{1,0:T(2,128)(2,1)S(1)}, u32[]{:S(2)}, u32[]{:S(2)}) collective-permute-start(bf16[2,8192]{1,0:T(2,128)(2,1)S(1)} %slice.95), channel_id=1, source_target_pairs={{0,1},{1,2},{2,3},{3,4},{4,5},{5,6},{6,7},{7,8},{8,9},{9,10},{10,1... | collective-permute-start | bytes 98312 | tf_op jit(solution)/shard_map/ppermute | solution.py:14
  11.8 0.1 iota_subtract_fusion
  11.9 1.7 %fusion.19 = (f32[1,1,8192]{2,1,0:T(1,128)S(1)}, f32[1,1,8192]{2,1,0:T(1,128)S(1)}, f32[1,1,8192]{2,1,0:T(1,128)S(1)}, f32[1,1,8192]{2,1,0:T(1,128)S(1)}, f32[1,...) fusion(f32[3,3,8192]{2,1,0:T(4,128)} %param.9), kind=kLoop, calls=%fused_computation.35 | loop fusion | bytes 589824 | tf_op jit(solution)/shard_map/slice | solution.py:20
  13.6 4.4 %iota_compare_fusion = pred[128,128,256]{2,1,0:T(32,128)(4,1)} fusion(s32[128,256]{1,0:T(8,128)S(1)} %iota_subtract_fusion), kind=kLoop, calls=%fused_computation.3 | loop fusion | flops 4194304 | bytes 4325376 | tf_op jit(solution)/shard_map/eq | solution.py:37
  18.1 0.0 collective-permute-done.2
  18.1 0.0 copy-done.2
  18.1 0.6 maximum_convert_fusion.2
  18.7 0.0 collective-permute-done.1
  18.7 1.0 copy-done.3
  19.7 0.6 maximum_convert_fusion.1
  20.3 2.7 %fusion.7 = bf16[128,8192]{1,0:T(8,128)(2,1)S(1)} fusion(f32[130,8192]{1,0:T(8,128)S(1)} %maximum_convert_fusion.2, f32[130,8192]{1,0:T(8,128)S(1)} %maximum_convert_fusion.1, f32[8192]{0:T(1024)S(1)} %bitcast.35, f32[8192]{0:T(1024)S(1)} %bitcast.36, f32[8192]{0:T(1024)S(1)} %bitcast.31, f32[8192]{0:T(1024)S(1)} %bitcast.32, f32[8192]{0:T(1024)S(1)} %bitcast.33, ...), kind=kLoop, calls=%fused_computation.9 | loop fusion | flops 12582912 | bytes 27459584 | tf_op jit(solution)/shard_map/convert_element_type | solution.py:54
  23.0 1.9 %slice.118 = bf16[127,8192]{1,0:T(8,128)(2,1)} slice(bf16[128,8192]{1,0:T(8,128)(2,1)S(1)} %fusion.7), slice={[1:128], [0:8192]} | slice | bytes 4161536 | tf_op jit(solution)/shard_map/slice | solution.py:55
  24.8 4.8 %collective-permute-start.3 = (bf16[127,8192]{1,0:T(8,128)(2,1)}, bf16[127,8192]{1,0:T(8,128)(2,1)}, u32[]{:S(2)}, u32[]{:S(2)}) collective-permute-start(bf16[127,8192]{1,0:T(8,128)(2,1)} %slice.118), channel_id=1, source_target_pairs={{0,1},{1,2},{2,3},{3,4},{4,5},{5,6},{6,7},{7,8},{8,9},{9,10},{10,1... | collective-permute-start | bytes 6242312 | tf_op jit(solution)/shard_map/ppermute | solution.py:14
  29.7 0.0 copy-done
  29.7 16.1 %fusion.3 = bf16[128,256,512]{2,1,0:T(8,128)(2,1)} fusion(pred[128,128,256]{2,1,0:T(32,128)(4,1)} %iota_compare_fusion, bf16[512,128]{1,0:T(8,128)(2,1)S(1)} %copy-done), kind=kOutput, calls=%fused_computation.4 | convolution fusion | flops 4294967296 | bytes 37879808 | tf_op jit(solution)/shard_map/gk,kts->gts/dot_general | solution.py:38
  45.8 45.5 %copy.11 = bf16[128,256,512]{1,0,2:T(8,128)(2,1)} copy(bf16[128,256,512]{2,1,0:T(8,128)(2,1)} %fusion.3) | data formatting | bytes 67108864 | tf_op jit(solution)/shard_map/gk,kts->gts/dot_general | solution.py:38
  91.3 2.4 %copy.8 = bf16[128,8192]{0,1:T(8,128)(2,1)} copy(bf16[128,8192]{1,0:T(8,128)(2,1)S(1)} %fusion.7) | data formatting | bytes 4194304 | tf_op jit(solution)/shard_map/convert_element_type | solution.py:54
  93.7 0.0 collective-permute-done
  93.7 4.4 %maximum_convert_fusion = f32[130,8192]{1,0:T(8,128)} fusion(bf16[128,8192]{1,0:T(8,128)(2,1)} %param.6, bf16[2,8192]{1,0:T(2,128)(2,1)S(1)} %collective-permute-done), kind=kLoop, calls=%fused_computation.28 | loop fusion | flops 4259840 | bytes 6389760 | tf_op jit(solution)/shard_map/convert_element_type | solution.py:19
  98.1 0.0 collective-permute-done.3
  98.1 4.1 %copy.12 = bf16[127,8192]{0,1:T(8,128)(2,1)} copy(bf16[127,8192]{1,0:T(8,128)(2,1)} %collective-permute-done.3) | data formatting | bytes 4161536
  102.2 3.7 %concatenate.18.clone = bf16[128,8192]{0,1:T(8,128)(2,1)} pad(bf16[127,8192]{0,1:T(8,128)(2,1)} %copy.12, bf16[]{:T(256)} %constant.0.clone.1), padding=1_0x0_0 | pad | bytes 4177922 | tf_op jit(solution)/shard_map/concatenate | solution.py:56
  105.9 17.6 %fusion = f32[512,16,128]{2,1,0:T(8,128)} fusion(bf16[128,256,512]{1,0,2:T(8,128)(2,1)} %copy.11, bf16[1,128,512,16]{1,3,2,0:T(8,128)(2,1)} %bitcast.26, bf16[1,128,512,16]{1,3,2,0:T(8,128)(2,1)} %bitcast.27), kind=kOutput, calls=%fused_computation | convolution fusion | flops 545259520 | bytes 41943040 | tf_op jit(solution)/shard_map/gts,bsgc->btgc/dot_general | solution.py:41
  123.5 5.6 %copy.9 = f32[128,8192]{1,0:T(8,128)} copy(f32[128,8192]{0,1:T(8,128)} %bitcast.25) | data formatting | bytes 8388608 | tf_op jit(solution)/shard_map/reshape | solution.py:42
  129.1 8.4 %fusion.13 = bf16[128,8192]{1,0:T(8,128)(2,1)} fusion(f32[130,8192]{1,0:T(8,128)} %maximum_convert_fusion, f32[128,8192]{1,0:T(8,128)} %copy.9, bf16[128,8192]{1,0:T(8,128)(2,1)S(1)} %fusion.7, f32[8192]{0:T(1024)S(1)} %copy-done.4, f32[8192]{0:T(1024)S(1)} %bitcast.29, f32[8192]{0:T(1024)S(1)} %bitcast.30, f32[8192]{0:T(1024)S(1)} %bitcast.28), kind=kLoop, calls=%fused_computation.21 | loop fusion | flops 10485760 | bytes 21102592 | tf_op jit(solution)/shard_map/convert_element_type | solution.py:59
  137.5 0.0 copy-done.1
  (6 shorter events, 0.0 us)
Async XLA Ops:
  0.0 29.7 %copy-start = (bf16[512,128]{1,0:T(8,128)(2,1)S(1)}, bf16[512,128]{1,0:T(8,128)(2,1)}, u32[]{:S(2)}) copy-start(bf16[512,128]{1,0:T(8,128)(2,1)} %param.10) | copy-start | bytes 393220
  0.0 18.1 %copy-start.2 = (bf16[128,8192]{1,0:T(8,128)(2,1)S(1)}, bf16[128,8192]{1,0:T(8,128)(2,1)}, u32[]{:S(2)}) copy-start(bf16[128,8192]{1,0:T(8,128)(2,1)} %param.8) | copy-start | bytes 6291460
  1.1 92.6 %collective-permute-start = (bf16[2,8192]{1,0:T(2,128)(2,1)S(1)}, bf16[2,8192]{1,0:T(2,128)(2,1)S(1)}, u32[]{:S(2)}, u32[]{:S(2)}) collective-permute-start(bf16[2,8192]{1,0:T(2,128)(2,1)S(1)} %slice.88), channel_id=1, source_target_pairs={{0,1},{1,2},{2,3},{3,4},{4,5},{5,6},{6,7},{7,8},{8,9},{9,10},{10,1... | collective-permute-start | bytes 98312 | tf_op jit(solution)/shard_map/ppermute | solution.py:14
  4.4 13.7 %collective-permute-start.2 = (bf16[2,8192]{1,0:T(2,128)(2,1)S(1)}, bf16[2,8192]{1,0:T(2,128)(2,1)S(1)}, u32[]{:S(2)}, u32[]{:S(2)}) collective-permute-start(bf16[2,8192]{1,0:T(2,128)(2,1)S(1)} %slice.102), channel_id=1, source_target_pairs={{0,1},{1,2},{2,3},{3,4},{4,5},{5,6},{6,7},{7,8},{8,9},{9,10},{10,1... | collective-permute-start | bytes 98312 | tf_op jit(solution)/shard_map/ppermute | solution.py:14
  9.9 8.8 %collective-permute-start.1 = (bf16[2,8192]{1,0:T(2,128)(2,1)S(1)}, bf16[2,8192]{1,0:T(2,128)(2,1)S(1)}, u32[]{:S(2)}, u32[]{:S(2)}) collective-permute-start(bf16[2,8192]{1,0:T(2,128)(2,1)S(1)} %slice.95), channel_id=1, source_target_pairs={{0,1},{1,2},{2,3},{3,4},{4,5},{5,6},{6,7},{7,8},{8,9},{9,10},{10,1... | collective-permute-start | bytes 98312 | tf_op jit(solution)/shard_map/ppermute | solution.py:14
  18.1 1.6 %copy-start.3 = (bf16[128,8192]{1,0:T(8,128)(2,1)S(1)}, bf16[128,8192]{1,0:T(8,128)(2,1)}, u32[]{:S(2)}) copy-start(bf16[128,8192]{1,0:T(8,128)(2,1)} %param.7) | copy-start | bytes 6291460
  24.8 73.2 %collective-permute-start.3 = (bf16[127,8192]{1,0:T(8,128)(2,1)}, bf16[127,8192]{1,0:T(8,128)(2,1)}, u32[]{:S(2)}, u32[]{:S(2)}) collective-permute-start(bf16[127,8192]{1,0:T(8,128)(2,1)} %slice.118), channel_id=1, source_target_pairs={{0,1},{1,2},{2,3},{3,4},{4,5},{5,6},{6,7},{7,8},{8,9},{9,10},{10,1... | collective-permute-start | bytes 6242312 | tf_op jit(solution)/shard_map/ppermute | solution.py:14
  123.5 5.6 %copy-start.4 = (f32[8192]{0:T(1024)S(1)}, f32[8192]{0:T(1024)}, u32[]{:S(2)}) copy-start(f32[8192]{0:T(1024)} %param.11) | copy-start | bytes 98308
  129.1 8.4 %copy-start.1 = (bf16[512,128]{1,0:T(8,128)(2,1)S(1)}, bf16[512,128]{1,0:T(8,128)(2,1)}, u32[]{:S(2)}) copy-start(bf16[512,128]{1,0:T(8,128)(2,1)} %param.10) | copy-start | bytes 393220
where the time goes:
time: 139 us; the launch traced here: 137 us
  local copies, waits for them, and re-layouts  68.9 us (50%)
  matrix products  33.7 us (24%)
  other arithmetic  21.1 us (15%)
  starting transfers between devices  13.7 us (10%)
    dot_general x1, local copies, waits for them, and re-layouts, causal_blocks(): jnp.einsum('gk,kts->gts', filters, onehot, preferred_element_type=jnp.flo...  45.5 us
    dot_general x1, matrix products, causal_blocks(): jnp.einsum('gts,bsgc->btgc', toeplitz, window, preferred_element_type=jnp...  17.6 us
    dot_general x1, matrix products, causal_blocks(): jnp.einsum('gk,kts->gts', filters, onehot, preferred_element_type=jnp.flo...  16.1 us
    ppermute x4, starting transfers between devices, passed_along(): return lax.ppermute(shard, axis, pairs)  13.7 us
    convert_element_type x1, other arithmetic, shards(): return mixed.astype(jnp.bfloat16)  8.38 us
    reshape x1, local copies, waits for them, and re-layouts, causal_blocks(): return result.reshape(length, width)  5.63 us
    convert_element_type x3, other arithmetic, featurize(): extended = jnp.concatenate([rim, local], axis=0).astype(jnp.float32)  5.52 us
    unnamed x11, local copies, waits for them, and re-layouts  5.13 us
  transfers between devices with their start and end apart: 4, of which 0 were waited for; matrix products, arithmetic and copies ran while one was open for 60% of the time, Pallas kernels for 0%

commit v1 on v0

v1 whole, which is shorter than its diff:
```python
import functools

import jax
import jax.numpy as jnp
from jax import lax
from jax.experimental import pallas as pl
from jax.experimental.pallas import tpu as pltpu
from jax.sharding import PartitionSpec as P

GROUP_CH = 16
FILT = 128
FEAT = 3
LANES = 128
SUB = 16
STEP = 512
F32 = jnp.float32
BF16 = jnp.bfloat16


def passed_along(shard):
    length = lax.axis_size("seq")
    return lax.ppermute(shard, "seq", [(i, i + 1) for i in range(length - 1)])


def delayed(x, by):
    return pltpu.roll(x, by, 0)


def feature(x, taps):
    total = taps[0:1] * x
    for j in range(1, FEAT):
        total = total + taps[j : j + 1] * delayed(x, j)
    return total


def rows_iota(shape):
    return lax.broadcasted_iota(jnp.int32, shape, 0)


def gate_kernel(rims, *refs):
    if rims:
        k_ref, v_ref, qt_ref, taps_ref, kt_ref, vt_ref, out_ref = refs
    else:
        k_ref, v_ref, qt_ref, taps_ref, out_ref = refs
    rows, width = k_ref.shape
    for c in range(width // LANES):
        at = slice(c * LANES, (c + 1) * LANES)
        k = k_ref[:, at].astype(F32)
        v = v_ref[:, at].astype(F32)
        gated = feature(k, taps_ref[1, :, at]) * feature(v, taps_ref[2, :, at])
        qt = delayed(qt_ref[:, at].astype(F32), FEAT - 1)
        head = jnp.where(rows_iota((SUB, LANES)) < FEAT - 1, qt, gated[:SUB])
        out_ref[:SUB, at] = head.astype(BF16)
        out_ref[SUB:rows, at] = gated[SUB:].astype(BF16)
    if rims:
        parts = kt_ref.shape[1] // width
        for c in range(width // LANES):
            tail = jnp.zeros((SUB, LANES), F32)
            iota = rows_iota((SUB, LANES))
            for b in range(parts):
                at = slice(b * width + c * LANES, b * width + (c + 1) * LANES)
                kt = kt_ref[:, at].astype(F32)
                vt = vt_ref[:, at].astype(F32)
                low = 2 * (FEAT - 1) * b
                kt = pltpu.roll(kt, (low + FEAT - 1) % SUB, 0)
                vt = pltpu.roll(vt, (low + 2 * (FEAT - 1)) % SUB, 0)
                tail = jnp.where((iota >= low) & (iota < low + FEAT - 1), kt, tail)
                tail = jnp.where((iota >= low + FEAT - 1) & (iota < low + 2 * (FEAT - 1)), vt, tail)
            out_ref[rows:, c * LANES : (c + 1) * LANES] = tail.astype(BF16)


def gate(k, v, q, taps, first, width, rims=False):
    rows, full = k.shape
    steps = width // STEP
    base = first // STEP
    last = rows // SUB - 1
    big = pl.BlockSpec((rows, STEP), lambda s: (0, base + s))
    in_specs = [
        big,
        big,
        pl.BlockSpec((SUB, STEP), lambda s: (last, base + s)),
        pl.BlockSpec((3, FEAT, STEP), lambda s: (0, 0, base + s)),
    ]
    args = [k, v, q, taps]
    out_rows = rows
    if rims:
        wide = full // steps
        in_specs += [pl.BlockSpec((SUB, wide), lambda s: (last, s))] * 2
        args += [k, v]
        out_rows += SUB
    return pl.pallas_call(
        functools.partial(gate_kernel, rims),
        grid=(steps,),
        in_specs=in_specs,
        out_specs=pl.BlockSpec((out_rows, STEP), lambda s: (0, s)),
        out_shape=jax.ShapeDtypeStruct((out_rows, width), BF16),
        cost_estimate=pl.CostEstimate(flops=12 * rows * width, bytes_accessed=6 * rows * width, transcendentals=0),
        name="gate",
    )(*args)


def edge_kernel(k_ref, v_ref, rim_ref, taps_ref, out_ref):
    width = rim_ref.shape[1]
    parts = k_ref.shape[1] // width
    iota = rows_iota((SUB, LANES))
    for b in range(parts):
        low = 2 * (FEAT - 1) * b
        for c in range(width // LANES):
            at = slice(b * width + c * LANES, b * width + (c + 1) * LANES)
            rim = rim_ref[:, c * LANES : (c + 1) * LANES].astype(F32)
            feats = []
            for i, ref in ((0, k_ref), (1, v_ref)):
                moved = pltpu.roll(rim, (SUB - (FEAT - 1) * (i + 1) - low) % SUB, 0)
                x = jnp.where(iota >= SUB - (FEAT - 1), moved, ref[:, at].astype(F32))
                feats.append(feature(x, taps_ref[i + 1, :, at]))
            out_ref[:, at] = (feats[0] * feats[1]).astype(BF16)[: out_ref.shape[0]]


def edge(k, v, rims, taps):
    rows, full = k.shape
    steps = rims.shape[1] // STEP
    wide = full // steps
    at_rim = rows // SUB
    return pl.pallas_call(
        edge_kernel,
        grid=(steps,),
        in_specs=[
            pl.BlockSpec((SUB, wide), lambda s: (0, s)),
            pl.BlockSpec((SUB, wide), lambda s: (0, s)),
            pl.BlockSpec((SUB, STEP), lambda s: (at_rim, s)),
            pl.BlockSpec((3, FEAT, wide), lambda s: (0, 0, s)),
        ],
        out_specs=pl.BlockSpec((FEAT - 1, wide), lambda s: (0, s)),
        out_shape=jax.ShapeDtypeStruct((FEAT - 1, full), BF16),
        cost_estimate=pl.CostEstimate(flops=12 * SUB * full, bytes_accessed=6 * SUB * full, transcendentals=0),
        name="edge",
    )(k, v, rims, taps)


def mix_kernel(h_ref, own_ref, got_ref, edge_ref, before_ref, q_ref, taps_ref, skip_ref, _, out_ref, lhs_ref):
    rows, width = q_ref.shape
    half = rows // 2
    per = LANES // GROUP_CH
    i = rows_iota((FILT, FILT))
    j = lax.broadcasted_iota(jnp.int32, (FILT, FILT), 1)
    flip = (i + j == FILT) | ((i == 0) & (j == 0))
    turned = jnp.dot(h_ref[...], flip.astype(BF16), preferred_element_type=F32)
    iota = rows_iota((SUB, LANES))
    b = rows_iota((half, FILT))
    m = lax.broadcasted_iota(jnp.int32, (half, FILT), 1)
    lane_group = lax.broadcasted_iota(jnp.int32, (half, 2 * LANES), 1) % LANES // GROUP_CH
    for c in range(width // LANES):
        at = slice(c * LANES, (c + 1) * LANES)
        for g in range(per):
            row = jnp.broadcast_to(turned[c * per + g : c * per + g + 1], (half, FILT))
            ring = pltpu.roll(row, 0, 1, stride=1, stride_axis=0)
            lhs_ref[g * half : (g + 1) * half, :FILT] = jnp.where(m > b, ring, 0.0).astype(BF16)
            lhs_ref[g * half : (g + 1) * half, FILT:] = jnp.where(m <= b, ring, 0.0).astype(BF16)
        edges = edge_ref[:, at].astype(F32)
        own_head = own_ref[:SUB, at].astype(F32)
        own_head = jnp.where(iota == 0, edges[0:1], own_head)
        own_head = jnp.where(iota == 1, edges[1:2], own_head)
        got_head = got_ref[:SUB, at].astype(F32)
        q_rim = got_head
        got_head = jnp.where(iota == 1, before_ref[1:2, at].astype(F32), got_head)
        cur0 = jnp.concatenate([own_head.astype(BF16), own_ref[SUB:half, at]], axis=0)
        cur1 = own_ref[half:, at]
        prev0 = jnp.concatenate([got_head.astype(BF16), got_ref[SUB:half, at]], axis=0)
        prev1 = got_ref[half:rows, at]
        rhs = jnp.concatenate(
            [
                jnp.concatenate([prev0, prev1], axis=1),
                jnp.concatenate([prev1, cur0], axis=1),
                jnp.concatenate([cur0, cur1], axis=1),
                jnp.concatenate([cur1, cur1], axis=1),
            ],
            axis=0,
        )
        res = jnp.dot(lhs_ref[...], rhs, preferred_element_type=F32)
        total = res[:half]
        for g in range(1, per):
            total = jnp.where(lane_group == g, res[g * half : (g + 1) * half], total)
        conv = jnp.concatenate([total[:, :LANES], total[:, LANES:]], axis=0)
        cur = jnp.concatenate([cur0, cur1], axis=0).astype(F32)
        q = q_ref[:, at].astype(F32)
        taps = taps_ref[0, :, at]
        q_feat = taps[0:1] * q
        rim = jnp.concatenate([q_rim[:8], jnp.zeros((rows - 8, LANES), F32)], axis=0)
        full_iota = rows_iota((rows, LANES))
        for d in range(1, FEAT):
            moved = delayed(q, d)
            shifted = pltpu.roll(rim, (d - (FEAT - 1)) % rows, 0)
            q_feat = q_feat + taps[d : d + 1] * jnp.where(full_iota < d, shifted, moved)
        out_ref[:, at] = (q_feat * (conv + skip_ref[:, at] * cur)).astype(BF16)


def mix(filters, own, got, edges, before, q, taps, skip, out, first):
    rows, full = q.shape
    width = own.shape[1]
    steps = width // STEP
    base = first // STEP
    mine = lambda s: (0, s)
    abs_ = lambda s: (0, base + s)
    in_specs = [
        pl.BlockSpec((STEP // GROUP_CH, FILT), lambda s: (base + s, 0)),
        pl.BlockSpec((rows, STEP), mine),
        pl.BlockSpec((rows, STEP), mine),
        pl.BlockSpec((FEAT - 1, STEP), abs_),
        pl.BlockSpec((FEAT - 1, STEP), abs_),
        pl.BlockSpec((rows, STEP), abs_),
        pl.BlockSpec((3, FEAT, STEP), lambda s: (0, 0, base + s)),
        pl.BlockSpec((1, STEP), abs_),
    ]
    args = [filters, own, got, edges, before, q, taps, skip]
    aliases = {}
    kernel = mix_kernel
    if out is not None:
        in_specs.append(pl.BlockSpec(memory_space=pl.ANY))
        args.append(out)
        aliases = {len(args) - 1: 0}
    else:
        kernel = lambda *refs: mix_kernel(*refs[:8], None, *refs[8:])
    return pl.pallas_call(
        kernel,
        grid=(steps,),
        in_specs=in_specs,
        out_specs=pl.BlockSpec((rows, STEP), abs_),
        out_shape=jax.ShapeDtypeStruct((rows, full), BF16),
        scratch_shapes=[pltpu.VMEM((LANES // GROUP_CH * rows // 2, 2 * FILT), BF16)],
        input_output_aliases=aliases,
        cost_estimate=pl.CostEstimate(
            flops=4 * rows * FILT * width, bytes_accessed=8 * rows * width, transcendentals=0
        ),
        name="mix",
    )(*args)


def shards(q_stream, k_stream, v_stream, feat_filter, long_filter, skip_gain):
    rows, width = q_stream.shape
    skip = skip_gain.reshape(1, width)
    quarter = width // 4
    sizes = [quarter, quarter, quarter, quarter - STEP, STEP]
    starts = [sum(sizes[:i]) for i in range(len(sizes))]
    own = []
    got = []
    for i, (first, size) in enumerate(zip(starts, sizes)):
        own.append(gate(k_stream, v_stream, q_stream, feat_filter, first, size, rims=i == 0))
        got.append(passed_along(own[-1]))
    edges = edge(k_stream, v_stream, got[0], feat_filter)
    before = passed_along(edges)
    out = None
    for first, a, b in zip(starts, own, got):
        out = mix(long_filter, a, b, edges, before, q_stream, feat_filter, skip, out, first)
    return out


def solution(mesh):
    in_specs = (
        P(("rep", "seq"), None),
        P(("rep", "seq"), None),
        P(("rep", "seq"), None),
        P(),
        P(),
        P(),
    )
    out_specs = P(("rep", "seq"), None)
    return jax.shard_map(shards, mesh=mesh, in_specs=in_specs, out_specs=out_specs, check_vma=False)
```

time: 139 us -> 66.4 us (0.48)
  the two profiles are of different devices: /device:TPU:0 before, /device:TPU:16 now
where the time goes in v1:
time: 66.4 us; the launch traced here: 65.5 us
  Pallas kernels  41.9 us (63%)
  starting transfers between devices  16.3 us (25%)
  local copies, waits for them, and re-layouts  4.34 us (7%)
  waiting for transfers between devices  2.82 us (4%)
    pallas_call x5, Pallas kernels, mix(): pl.pallas_call(kernel, grid=(steps,), in_specs=in_specs, out_specs=pl.Blo...  22.3 us
    ppermute x6, starting transfers between devices, passed_along(): return lax.ppermute(shard, 'seq', [(i, i + 1) for i in range(length - 1)])  16.3 us
    pallas_call x5, Pallas kernels, gate(): pl.pallas_call(functools.partial(gate_kernel, rims), grid=(steps,), in_sp...  16.3 us
    unnamed x12, local copies, waits for them, and re-layouts  4.34 us
    pallas_call x1, Pallas kernels, edge(): pl.pallas_call(edge_kernel, grid=(steps,), in_specs=[pl.BlockSpec((SUB, w...  3.4 us
    ppermute x6, waiting for transfers between devices, passed_along(): return lax.ppermute(shard, 'seq', [(i, i + 1) for i in range(length - 1)])  2.82 us
  transfers between devices with their start and end apart: 6, of which 1 were waited for; matrix products, arithmetic and copies ran while one was open for 0% of the time, Pallas kernels for 54%

profile of v1, /device:TPU:16, one launch (start us, length us, event | category | flops | bytes accessed | tf_op | source)
XLA Modules:
  0.0 65.5 jit_solution(4693945299393341630)
XLA Ops:
  0.0 3.9 %gate.6.refs_1_ = bf16[144,2048]{1,0:T(8,128)(2,1)} custom-call(bf16[128,8192]{1,0:T(8,128)(2,1)} %refs_0_.10, bf16[128,8192]{1,0:T(8,128)(2,1)} %refs_1_.9, bf16[128,8192]{1,0:T(8,128)(2,1)} %q_ref.7, f32[3,3,8192]{2,1,0:T(4,128)} %taps_ref.9, bf16[128,8192]{1,0:T(8,128)(2,1)} %refs_0_.10, bf16[128,8192]{1,0:T(8,128)(2,1)} %refs_1_.9), custom_call_target="tpu_custom_call" | custom-call | flops 3145728 | bytes 1572864 | tf_op jit(solution)/shard_map/gate/pallas_call | solution.py:91
  3.9 1.9 %collective-permute-start.1 = (bf16[144,2048]{1,0:T(8,128)(2,1)}, bf16[144,2048]{1,0:T(8,128)(2,1)S(1)}, u32[]{:S(2)}, u32[]{:S(2)}) collective-permute-start(bf16[144,2048]{1,0:T(8,128)(2,1)} %gate.6.refs_1_), channel_id=1, source_target_pairs={{0,1},{1,2},{2,3},{3,4},{4,5},{5,6},{6,7},{7,8},{8,9},{9,10},{10,1... | collective-permute-start | bytes 1769480 | tf_op jit(solution)/shard_map/ppermute | solution.py:22
  5.8 3.7 %gate.9.own_ref = bf16[128,2048]{1,0:T(8,128)(2,1)} custom-call(bf16[128,8192]{1,0:T(8,128)(2,1)} %refs_0_.10, bf16[128,8192]{1,0:T(8,128)(2,1)} %refs_1_.9, bf16[128,8192]{1,0:T(8,128)(2,1)} %q_ref.7, f32[3,3,8192]{2,1,0:T(4,128)} %taps_ref.9), custom_call_target="tpu_custom_call" | custom-call | flops 3145728 | bytes 1572864 | tf_op jit(solution)/shard_map/gate/pallas_call | solution.py:91
  9.5 3.5 %collective-permute-start.5 = (bf16[128,2048]{1,0:T(8,128)(2,1)}, bf16[128,2048]{1,0:T(8,128)(2,1)S(1)}, u32[]{:S(2)}, u32[]{:S(2)}) collective-permute-start(bf16[128,2048]{1,0:T(8,128)(2,1)} %gate.9.own_ref), channel_id=1, source_target_pairs={{0,1},{1,2},{2,3},{3,4},{4,5},{5,6},{6,7},{7,8},{8,9},{9,10},{10,1... | collective-permute-start | bytes 1572872 | tf_op jit(solution)/shard_map/ppermute | solution.py:22
  13.1 3.7 %gate.8.own_ref = bf16[128,2048]{1,0:T(8,128)(2,1)} custom-call(bf16[128,8192]{1,0:T(8,128)(2,1)} %refs_0_.10, bf16[128,8192]{1,0:T(8,128)(2,1)} %refs_1_.9, bf16[128,8192]{1,0:T(8,128)(2,1)} %q_ref.7, f32[3,3,8192]{2,1,0:T(4,128)} %taps_ref.9), custom_call_target="tpu_custom_call" | custom-call | flops 3145728 | bytes 1572864 | tf_op jit(solution)/shard_map/gate/pallas_call | solution.py:91
  16.8 1.9 %collective-permute-start.4 = (bf16[128,2048]{1,0:T(8,128)(2,1)}, bf16[128,2048]{1,0:T(8,128)(2,1)S(1)}, u32[]{:S(2)}, u32[]{:S(2)}) collective-permute-start(bf16[128,2048]{1,0:T(8,128)(2,1)} %gate.8.own_ref), channel_id=1, source_target_pairs={{0,1},{1,2},{2,3},{3,4},{4,5},{5,6},{6,7},{7,8},{8,9},{9,10},{10,1... | collective-permute-start | bytes 1572872 | tf_op jit(solution)/shard_map/ppermute | solution.py:22
  18.7 3.1 %gate.7.own_ref = bf16[128,1536]{1,0:T(8,128)(2,1)} custom-call(bf16[128,8192]{1,0:T(8,128)(2,1)} %refs_0_.10, bf16[128,8192]{1,0:T(8,128)(2,1)} %refs_1_.9, bf16[128,8192]{1,0:T(8,128)(2,1)} %q_ref.7, f32[3,3,8192]{2,1,0:T(4,128)} %taps_ref.9), custom_call_target="tpu_custom_call" | custom-call | flops 2359296 | bytes 1179648 | tf_op jit(solution)/shard_map/gate/pallas_call | solution.py:91
  21.8 3.5 %collective-permute-start.3 = (bf16[128,1536]{1,0:T(8,128)(2,1)}, bf16[128,1536]{1,0:T(8,128)(2,1)S(1)}, u32[]{:S(2)}, u32[]{:S(2)}) collective-permute-start(bf16[128,1536]{1,0:T(8,128)(2,1)} %gate.7.own_ref), channel_id=1, source_target_pairs={{0,1},{1,2},{2,3},{3,4},{4,5},{5,6},{6,7},{7,8},{8,9},{9,10},{10,1... | collective-permute-start | bytes 1179656 | tf_op jit(solution)/shard_map/ppermute | solution.py:22
  25.3 1.8 %gate.5.own_ref = bf16[128,512]{1,0:T(8,128)(2,1)} custom-call(bf16[128,8192]{1,0:T(8,128)(2,1)} %refs_0_.10, bf16[128,8192]{1,0:T(8,128)(2,1)} %refs_1_.9, bf16[128,8192]{1,0:T(8,128)(2,1)} %q_ref.7, f32[3,3,8192]{2,1,0:T(4,128)} %taps_ref.9), custom_call_target="tpu_custom_call" | custom-call | flops 786432 | bytes 393216 | tf_op jit(solution)/shard_map/gate/pallas_call | solution.py:91
  27.2 1.9 %collective-permute-start = (bf16[128,512]{1,0:T(8,128)(2,1)}, bf16[128,512]{1,0:T(8,128)(2,1)S(1)}, u32[]{:S(2)}, u32[]{:S(2)}) collective-permute-start(bf16[128,512]{1,0:T(8,128)(2,1)} %gate.5.own_ref), channel_id=1, source_target_pairs={{0,1},{1,2},{2,3},{3,4},{4,5},{5,6},{6,7},{7,8},{8,9},{9,10},{10,1... | collective-permute-start | bytes 393224 | tf_op jit(solution)/shard_map/ppermute | solution.py:22
  29.1 0.0 collective-permute-done.1.rim_ref.refs_2_
  29.1 0.0 copy-start
  29.1 0.8 %copy-done = bf16[144,2048]{1,0:T(8,128)(2,1)} copy-done((bf16[144,2048]{1,0:T(8,128)(2,1)}, bf16[144,2048]{1,0:T(8,128)(2,1)S(1)}, u32[]{:S(2)}) %copy-start) | copy-done | bytes 589848
  29.9 3.4 %edge.1.refs_3_.edge_ref = bf16[2,8192]{1,0:T(2,128)(2,1)} custom-call(bf16[128,8192]{1,0:T(8,128)(2,1)} %refs_0_.10, bf16[128,8192]{1,0:T(8,128)(2,1)} %refs_1_.9, bf16[144,2048]{1,0:T(8,128)(2,1)} %copy-done, f32[3,3,8192]{2,1,0:T(4,128)} %taps_ref.9), custom_call_target="tpu_custom_call" | custom-call | flops 1572864 | bytes 786432 | tf_op jit(solution)/shard_map/edge/pallas_call | solution.py:124
  33.3 3.5 %collective-permute-start.2 = (bf16[2,8192]{1,0:T(2,128)(2,1)}, bf16[2,8192]{1,0:T(2,128)(2,1)S(1)}, u32[]{:S(2)}, u32[]{:S(2)}) collective-permute-start(bf16[2,8192]{1,0:T(2,128)(2,1)} %edge.1.refs_3_.edge_ref), channel_id=1, source_target_pairs={{0,1},{1,2},{2,3},{3,4},{4,5},{5,6},{6,7},{7,8},{8,9},{9,10},{10,1... | collective-permute-start | bytes 98312 | tf_op jit(solution)/shard_map/ppermute | solution.py:22
  36.8 2.8 %collective-permute-done.2.refs_4_.before_ref = bf16[2,8192]{1,0:T(2,128)(2,1)S(1)} collective-permute-done((bf16[2,8192]{1,0:T(2,128)(2,1)}, bf16[2,8192]{1,0:T(2,128)(2,1)S(1)}, u32[]{:S(2)}, u32[]{:S(2)}) %collective-permute-start.2) | collective-permute-done | bytes 32800 | tf_op jit(solution)/shard_map/ppermute | solution.py:22
  39.6 0.6 copy-done.1
  40.2 5.2 %mix.5._ = bf16[128,8192]{1,0:T(8,128)(2,1)} custom-call(bf16[512,128]{1,0:T(8,128)(2,1)} %h_ref.7, bf16[144,2048]{1,0:T(8,128)(2,1)} %gate.6.refs_1_, bf16[144,2048]{1,0:T(8,128)(2,1)} %copy-done, bf16[2,8192]{1,0:T(2,128)(2,1)} %edge.1.refs_3_.edge_ref, bf16[2,8192]{1,0:T(2,128)(2,1)} %copy-done.1, bf16[128,8192]{1,0:T(8,128)(2,1)} %q_ref.7, ...), custom_call_target="tpu_custom_call" | custom-call | flops 134217728 | bytes 2097152 | tf_op jit(solution)/shard_map/mix/pallas_call | solution.py:223
  45.4 0.0 collective-permute-done.5.got_ref
  45.4 0.8 %copy-done.3 = bf16[128,2048]{1,0:T(8,128)(2,1)} copy-done((bf16[128,2048]{1,0:T(8,128)(2,1)}, bf16[128,2048]{1,0:T(8,128)(2,1)S(1)}, u32[]{:S(2)}) %copy-start.3) | copy-done | bytes 524312
  46.2 5.2 %mix.6._ = bf16[128,8192]{1,0:T(8,128)(2,1)} custom-call(bf16[512,128]{1,0:T(8,128)(2,1)} %h_ref.7, bf16[128,2048]{1,0:T(8,128)(2,1)} %gate.9.own_ref, bf16[128,2048]{1,0:T(8,128)(2,1)} %copy-done.3, bf16[2,8192]{1,0:T(2,128)(2,1)} %edge.1.refs_3_.edge_ref, bf16[2,8192]{1,0:T(2,128)(2,1)} %copy-done.1, ...), custom_call_target="tpu_custom_call", output_to_operand_aliasing={{}: (8, {})} | custom-call | flops 134217728 | bytes 2097152 | tf_op jit(solution)/shard_map/mix/pallas_call | solution.py:223
  51.3 0.0 collective-permute-done.4.got_ref
  51.4 0.8 %copy-done.2 = bf16[128,2048]{1,0:T(8,128)(2,1)} copy-done((bf16[128,2048]{1,0:T(8,128)(2,1)}, bf16[128,2048]{1,0:T(8,128)(2,1)S(1)}, u32[]{:S(2)}) %copy-start.2) | copy-done | bytes 524312
  52.1 5.2 %mix.7._ = bf16[128,8192]{1,0:T(8,128)(2,1)} custom-call(bf16[512,128]{1,0:T(8,128)(2,1)} %h_ref.7, bf16[128,2048]{1,0:T(8,128)(2,1)} %gate.8.own_ref, bf16[128,2048]{1,0:T(8,128)(2,1)} %copy-done.2, bf16[2,8192]{1,0:T(2,128)(2,1)} %edge.1.refs_3_.edge_ref, bf16[2,8192]{1,0:T(2,128)(2,1)} %copy-done.1, ...), custom_call_target="tpu_custom_call", output_to_operand_aliasing={{}: (8, {})} | custom-call | flops 134217728 | bytes 2097152 | tf_op jit(solution)/shard_map/mix/pallas_call | solution.py:223
  57.3 0.0 collective-permute-done.3.got_ref
  57.3 0.0 copy-start.4
  57.3 0.7 %copy-done.4 = bf16[128,1536]{1,0:T(8,128)(2,1)} copy-done((bf16[128,1536]{1,0:T(8,128)(2,1)}, bf16[128,1536]{1,0:T(8,128)(2,1)S(1)}, u32[]{:S(2)}) %copy-start.4) | copy-done | bytes 393240
  58.1 4.3 %mix.8._ = bf16[128,8192]{1,0:T(8,128)(2,1)} custom-call(bf16[512,128]{1,0:T(8,128)(2,1)} %h_ref.7, bf16[128,1536]{1,0:T(8,128)(2,1)} %gate.7.own_ref, bf16[128,1536]{1,0:T(8,128)(2,1)} %copy-done.4, bf16[2,8192]{1,0:T(2,128)(2,1)} %edge.1.refs_3_.edge_ref, bf16[2,8192]{1,0:T(2,128)(2,1)} %copy-done.1, ...), custom_call_target="tpu_custom_call", output_to_operand_aliasing={{}: (8, {})} | custom-call | flops 100663296 | bytes 1572864 | tf_op jit(solution)/shard_map/mix/pallas_call | solution.py:223
  62.4 0.0 collective-permute-done.got_ref
  62.4 0.0 copy-start.5
  62.4 0.6 copy-done.5
  63.0 2.5 %mix.9 = bf16[128,8192]{1,0:T(8,128)(2,1)} custom-call(bf16[512,128]{1,0:T(8,128)(2,1)} %h_ref.7, bf16[128,512]{1,0:T(8,128)(2,1)} %gate.5.own_ref, bf16[128,512]{1,0:T(8,128)(2,1)} %copy-done.5, bf16[2,8192]{1,0:T(2,128)(2,1)} %edge.1.refs_3_.edge_ref, bf16[2,8192]{1,0:T(2,128)(2,1)} %copy-done.1, ...), custom_call_target="tpu_custom_call", output_to_operand_aliasing={{}: (8, {})} | custom-call | flops 33554432 | bytes 524288 | tf_op jit(solution)/shard_map/mix/pallas_call | solution.py:223
  (3 shorter events, 0.0 us)
Async XLA Ops:
  3.9 25.2 %collective-permute-start.1 = (bf16[144,2048]{1,0:T(8,128)(2,1)}, bf16[144,2048]{1,0:T(8,128)(2,1)S(1)}, u32[]{:S(2)}, u32[]{:S(2)}) collective-permute-start(bf16[144,2048]{1,0:T(8,128)(2,1)} %gate.6.refs_1_), channel_id=1, source_target_pairs={{0,1},{1,2},{2,3},{3,4},{4,5},{5,6},{6,7},{7,8},{8,9},{9,10},{10,1... | collective-permute-start | bytes 1769480 | tf_op jit(solution)/shard_map/ppermute | solution.py:22
  9.5 35.9 %collective-permute-start.5 = (bf16[128,2048]{1,0:T(8,128)(2,1)}, bf16[128,2048]{1,0:T(8,128)(2,1)S(1)}, u32[]{:S(2)}, u32[]{:S(2)}) collective-permute-start(bf16[128,2048]{1,0:T(8,128)(2,1)} %gate.9.own_ref), channel_id=1, source_target_pairs={{0,1},{1,2},{2,3},{3,4},{4,5},{5,6},{6,7},{7,8},{8,9},{9,10},{10,1... | collective-permute-start | bytes 1572872 | tf_op jit(solution)/shard_map/ppermute | solution.py:22
  16.8 34.6 %collective-permute-start.4 = (bf16[128,2048]{1,0:T(8,128)(2,1)}, bf16[128,2048]{1,0:T(8,128)(2,1)S(1)}, u32[]{:S(2)}, u32[]{:S(2)}) collective-permute-start(bf16[128,2048]{1,0:T(8,128)(2,1)} %gate.8.own_ref), channel_id=1, source_target_pairs={{0,1},{1,2},{2,3},{3,4},{4,5},{5,6},{6,7},{7,8},{8,9},{9,10},{10,1... | collective-permute-start | bytes 1572872 | tf_op jit(solution)/shard_map/ppermute | solution.py:22
  21.8 35.5 %collective-permute-start.3 = (bf16[128,1536]{1,0:T(8,128)(2,1)}, bf16[128,1536]{1,0:T(8,128)(2,1)S(1)}, u32[]{:S(2)}, u32[]{:S(2)}) collective-permute-start(bf16[128,1536]{1,0:T(8,128)(2,1)} %gate.7.own_ref), channel_id=1, source_target_pairs={{0,1},{1,2},{2,3},{3,4},{4,5},{5,6},{6,7},{7,8},{8,9},{9,10},{10,1... | collective-permute-start | bytes 1179656 | tf_op jit(solution)/shard_map/ppermute | solution.py:22
  27.2 35.2 %collective-permute-start = (bf16[128,512]{1,0:T(8,128)(2,1)}, bf16[128,512]{1,0:T(8,128)(2,1)S(1)}, u32[]{:S(2)}, u32[]{:S(2)}) collective-permute-start(bf16[128,512]{1,0:T(8,128)(2,1)} %gate.5.own_ref), channel_id=1, source_target_pairs={{0,1},{1,2},{2,3},{3,4},{4,5},{5,6},{6,7},{7,8},{8,9},{9,10},{10,1... | collective-permute-start | bytes 393224 | tf_op jit(solution)/shard_map/ppermute | solution.py:22
  29.1 0.8 %copy-start = (bf16[144,2048]{1,0:T(8,128)(2,1)}, bf16[144,2048]{1,0:T(8,128)(2,1)S(1)}, u32[]{:S(2)}) copy-start(bf16[144,2048]{1,0:T(8,128)(2,1)S(1)} %collective-permute-done.1.rim_ref.refs_2_) | copy-start | bytes 1769476
  33.3 6.3 %collective-permute-start.2 = (bf16[2,8192]{1,0:T(2,128)(2,1)}, bf16[2,8192]{1,0:T(2,128)(2,1)S(1)}, u32[]{:S(2)}, u32[]{:S(2)}) collective-permute-start(bf16[2,8192]{1,0:T(2,128)(2,1)} %edge.1.refs_3_.edge_ref), channel_id=1, source_target_pairs={{0,1},{1,2},{2,3},{3,4},{4,5},{5,6},{6,7},{7,8},{8,9},{9,10},{10,1... | collective-permute-start | bytes 98312 | tf_op jit(solution)/shard_map/ppermute | solution.py:22
  39.6 0.6 copy-start.1
  45.4 0.8 %copy-start.3 = (bf16[128,2048]{1,0:T(8,128)(2,1)}, bf16[128,2048]{1,0:T(8,128)(2,1)S(1)}, u32[]{:S(2)}) copy-start(bf16[128,2048]{1,0:T(8,128)(2,1)S(1)} %collective-permute-done.5.got_ref) | copy-start | bytes 1572868
  51.4 0.8 %copy-start.2 = (bf16[128,2048]{1,0:T(8,128)(2,1)}, bf16[128,2048]{1,0:T(8,128)(2,1)S(1)}, u32[]{:S(2)}) copy-start(bf16[128,2048]{1,0:T(8,128)(2,1)S(1)} %collective-permute-done.4.got_ref) | copy-start | bytes 1572868
  57.3 0.7 %copy-start.4 = (bf16[128,1536]{1,0:T(8,128)(2,1)}, bf16[128,1536]{1,0:T(8,128)(2,1)S(1)}, u32[]{:S(2)}) copy-start(bf16[128,1536]{1,0:T(8,128)(2,1)S(1)} %collective-permute-done.3.got_ref) | copy-start | bytes 1179652
  62.4 0.6 copy-start.5

commit v2 on v0

v2 whole, which is shorter than its diff:
```python
import functools

import jax
import jax.numpy as jnp
from jax import lax
from jax.experimental import pallas as pl
from jax.experimental.pallas import tpu as pltpu
from jax.sharding import PartitionSpec as P

GROUP_CH = 16
FILT = 128
FEAT = 3
LANES = 128
SUB = 16
PIECE = 512
MIB = 1 << 20
F32 = jnp.float32
BF16 = jnp.bfloat16
VMEM = pl.BlockSpec(memory_space=pltpu.VMEM)
HBM = pl.BlockSpec(memory_space=pltpu.HBM)
COST = pl.CostEstimate(flops=1000, bytes_accessed=1000, transcendentals=0)
LONG = pl.CostEstimate(flops=1000, bytes_accessed=64 * MIB, transcendentals=0)


def passed_along(shard):
    length = lax.axis_size("seq")
    return lax.ppermute(shard, "seq", [(i, i + 1) for i in range(length - 1)])


def feature(x, taps):
    total = taps[0:1] * x
    for j in range(1, FEAT):
        total = total + taps[j : j + 1] * pltpu.roll(x, j, 0)
    return total


def rows_iota(shape):
    return lax.broadcasted_iota(jnp.int32, shape, 0)


def lanes_at(c):
    return pl.ds(c * LANES if isinstance(c, int) else pl.multiple_of(c * LANES, LANES), LANES)


def in_hbm(x):
    return pltpu.with_memory_space_constraint(x, pltpu.HBM)


def run_of(tiles, most=8):
    return max(n for n in range(1, most + 1) if tiles % n == 0)


def params(mib):
    return pltpu.CompilerParams(vmem_limit_bytes=mib * MIB)


def gate_tile(k, v, taps, at):
    return feature(k.astype(F32), taps[1, :, at]) * feature(v.astype(F32), taps[2, :, at])


def gate_piece(k_ref, v_ref, q_tail, taps_ref, out_ref, src, dst, at):
    rows = k_ref.shape[0]
    gated = gate_tile(k_ref[:, src], v_ref[:, src], taps_ref, at)
    tail = pltpu.roll(q_tail.astype(F32), FEAT - 1, 0)
    head = jnp.where(rows_iota((SUB, LANES)) < FEAT - 1, tail, gated[:SUB])
    out_ref[:SUB, dst] = head.astype(BF16)
    out_ref[SUB:rows, dst] = gated[SUB:].astype(BF16)


def first_gate_kernel(k_hbm, v_hbm, q_hbm, taps_hbm, out_ref, k_ref, v_ref, taps_ref, qt_ref, kt_ref, vt_ref, sems):
    rows, width = k_ref.shape
    full = kt_ref.shape[1]
    pieces = width // PIECE
    last = pl.ds(rows - SUB, SUB)

    def load(p, ref, hbm, i):
        at = pl.ds(p * PIECE, PIECE)
        return pltpu.make_async_copy(hbm.at[:, at], ref.at[:, at], sems.at[2 * p + i])

    rest = [
        pltpu.make_async_copy(taps_hbm.at[:, :, pl.ds(0, width)], taps_ref, sems.at[2 * pieces]),
        pltpu.make_async_copy(q_hbm.at[last, pl.ds(0, width)], qt_ref, sems.at[2 * pieces + 1]),
        pltpu.make_async_copy(k_hbm.at[last], kt_ref, sems.at[2 * pieces + 2]),
        pltpu.make_async_copy(v_hbm.at[last], vt_ref, sems.at[2 * pieces + 3]),
    ]
    rest[0].start()
    rest[1].start()
    for p in range(pieces):
        load(p, k_ref, k_hbm, 0).start()
        load(p, v_ref, v_hbm, 1).start()
    rest[2].start()
    rest[3].start()
    rest[0].wait()
    rest[1].wait()
    for p in range(pieces):
        load(p, k_ref, k_hbm, 0).wait()
        load(p, v_ref, v_hbm, 1).wait()

        @pl.loop(0, PIECE // LANES)
        def _(c):
            at = lanes_at(c + p * (PIECE // LANES))
            gate_piece(k_ref, v_ref, qt_ref[:, at], taps_ref, out_ref, at, at, at)

    rest[2].wait()
    rest[3].wait()
    iota = rows_iota((SUB, LANES))

    @pl.loop(0, width // LANES)
    def _(c):
        tail = jnp.zeros((SUB, LANES), F32)
        for b in range(full // width):
            low = 2 * (FEAT - 1) * b
            at = lanes_at(c + b * (width // LANES))
            kt = pltpu.roll(kt_ref[:, at].astype(F32), (low + FEAT - 1) % SUB, 0)
            vt = pltpu.roll(vt_ref[:, at].astype(F32), (low + 2 * (FEAT - 1)) % SUB, 0)
            tail = jnp.where((iota >= low) & (iota < low + FEAT - 1), kt, tail)
            tail = jnp.where((iota >= low + FEAT - 1) & (iota < low + 2 * (FEAT - 1)), vt, tail)
        out_ref[rows:, lanes_at(c)] = tail.astype(BF16)


def first_gate(k, v, q, taps, width):
    rows, full = k.shape
    return pl.pallas_call(
        first_gate_kernel,
        in_specs=[HBM] * 4,
        out_specs=VMEM,
        out_shape=jax.ShapeDtypeStruct((rows + SUB, width), BF16),
        scratch_shapes=[
            pltpu.VMEM((rows, width), BF16),
            pltpu.VMEM((rows, width), BF16),
            pltpu.VMEM((3, FEAT, width), F32),
            pltpu.VMEM((SUB, width), BF16),
            pltpu.VMEM((SUB, full), BF16),
            pltpu.VMEM((SUB, full), BF16),
            pltpu.SemaphoreType.DMA((2 * (width // PIECE) + 4,)),
        ],
        compiler_params=params(12),
        cost_estimate=COST,
        name="gate_first",
    )(*(in_hbm(x) for x in (k, v, q, taps)))


def gate_kernel(firsts, k_ref, v_ref, q_ref, taps_ref, _, *out_refs):
    rows = k_ref.shape[0]
    for first, out_ref in zip(firsts, out_refs):

        @pl.loop(0, out_ref.shape[1] // LANES, unroll=2)
        def _(c):
            at = lanes_at(c + first // LANES)
            gate_piece(k_ref, v_ref, q_ref[rows - SUB :, at], taps_ref, out_ref, at, lanes_at(c), at)


def gate(k, v, q, taps, after, firsts, widths):
    rows = k.shape[0]
    return pl.pallas_call(
        functools.partial(gate_kernel, firsts),
        in_specs=[VMEM] * 4 + [pl.BlockSpec(memory_space=pl.ANY)],
        out_specs=[VMEM] * len(widths),
        out_shape=[jax.ShapeDtypeStruct((rows, w), BF16) for w in widths],
        compiler_params=params(12),
        cost_estimate=COST,
        name="gate",
    )(k, v, q, taps, after)


def last_gate_kernel(kh_ref, vh_ref, taps_ref, rim_ref, own_ref, out_ref, edge_ref):
    rows, width = own_ref.shape
    full = kh_ref.shape[1]
    wide = rim_ref.shape[1]
    iota = rows_iota((SUB, LANES))

    @pl.loop(0, wide // LANES)
    def _(c):
        rim = rim_ref[rows:, lanes_at(c)].astype(F32)
        for b in range(full // wide):
            low = 2 * (FEAT - 1) * b
            at = lanes_at(c + b * (wide // LANES))
            feats = []
            for i, ref in ((0, kh_ref), (1, vh_ref)):
                moved = pltpu.roll(rim, (SUB - (FEAT - 1) * (i + 1) - low) % SUB, 0)
                x = jnp.where(iota >= SUB - (FEAT - 1), moved, ref[:SUB, at].astype(F32))
                feats.append(feature(x, taps_ref[i + 1, :, at]))
            edge_ref[:, at] = (feats[0] * feats[1]).astype(BF16)

    @pl.loop(0, width // LANES)
    def _(c):
        out_ref[:rows, lanes_at(c)] = own_ref[:, lanes_at(c)]
        tail = jnp.zeros((SUB, LANES), F32)
        for b in range(pl.cdiv(full, width)):
            at = lanes_at(lax.rem(c + b * (width // LANES), full // LANES))
            one = jnp.broadcast_to(edge_ref[:, at].astype(F32)[1:2], (SUB, LANES))
            tail = jnp.where(iota == b, one, tail)
        out_ref[rows:, lanes_at(c)] = tail.astype(BF16)


def last_gate(k_head, v_head, taps, rims, own):
    rows, width = own.shape
    full = k_head.shape[1]
    return pl.pallas_call(
        last_gate_kernel,
        in_specs=[VMEM] * 5,
        out_specs=[VMEM] * 2,
        out_shape=[
            jax.ShapeDtypeStruct((rows + SUB, width), BF16),
            jax.ShapeDtypeStruct((SUB, full), BF16),
        ],
        compiler_params=params(12),
        cost_estimate=COST,
        name="gate_last",
    )(k_head, v_head, taps, rims, own)


def turned_filters(h):
    i = rows_iota((FILT, FILT))
    j = lax.broadcasted_iota(jnp.int32, (FILT, FILT), 1)
    flip = (i + j == FILT) | ((i == 0) & (j == 0))
    return jnp.dot(h, flip.astype(BF16), preferred_element_type=F32)


def fill_mask(mask_ref):
    rows, cols = mask_ref.shape
    i = rows_iota((rows, cols))
    b = i // SUB * 8 + i % 8
    m = lax.broadcasted_iota(jnp.int32, (rows, cols), 1)
    mask_ref[...] = jnp.where((m > b) & (m <= b + FILT), 1.0, 0.0).astype(BF16)


def mix_tile(turned_ref, mask_ref, lhs_ref, own_ref, got_ref, edge_ref, q_ref, taps_ref, skip_ref, before, src, dst, c):
    rows = q_ref.shape[0]
    half = rows // 2
    per = LANES // GROUP_CH
    iota = rows_iota((SUB, LANES))
    lane_group = lax.broadcasted_iota(jnp.int32, (8, 2 * LANES), 1) % LANES // GROUP_CH
    turned = turned_ref[pl.ds(c * per if isinstance(c, int) else pl.multiple_of(c * per, per), per), :]
    rings = []
    for g in range(per):
        row = jnp.broadcast_to(turned[g : g + 1], (half, FILT))
        rings.append(pltpu.roll(row, 0, 1, stride=1, stride_axis=0))
    for r in range(half // 8):
        mask = mask_ref[r * SUB : (r + 1) * SUB]
        for g in range(0, per, 2):
            pair = jnp.concatenate([rings[g][r * 8 : r * 8 + 8], rings[g + 1][r * 8 : r * 8 + 8]], axis=0)
            pair = pair.astype(BF16)
            low = (r * per + g) * 8
            lhs_ref[low : low + SUB, :] = jnp.concatenate([pair, pair], axis=1) * mask
    own_head = jnp.where(iota < FEAT - 1, edge_ref[:, src].astype(F32), own_ref[:SUB, dst].astype(F32))
    got_head = got_ref[:SUB, dst].astype(F32)
    q_rim = got_head
    if before is None:
        got_head = jnp.where(iota < FEAT - 1, 0.0, got_head)
    else:
        got_head = jnp.where(iota < FEAT - 1, before, got_head)
    cur0 = jnp.concatenate([own_head.astype(BF16), own_ref[SUB:half, dst]], axis=0)
    cur1 = own_ref[half:rows, dst]
    prev0 = jnp.concatenate([got_head.astype(BF16), got_ref[SUB:half, dst]], axis=0)
    prev1 = got_ref[half:rows, dst]
    rhs = jnp.concatenate(
        [
            jnp.concatenate([prev0, prev1], axis=1),
            jnp.concatenate([prev1, cur0], axis=1),
            jnp.concatenate([cur0, cur1], axis=1),
            jnp.concatenate([cur1, cur1], axis=1),
        ],
        axis=0,
    )
    res = jnp.dot(lhs_ref[...], rhs, preferred_element_type=F32)
    totals = []
    for r in range(half // 8):
        total = res[r * per * 8 : r * per * 8 + 8]
        for g in range(1, per):
            low = (r * per + g) * 8
            total = jnp.where(lane_group == g, res[low : low + 8], total)
        totals.append(total)
    conv = jnp.concatenate([t[:, :LANES] for t in totals] + [t[:, LANES:] for t in totals], axis=0)
    cur = jnp.concatenate([cur0, cur1], axis=0).astype(F32)
    q = q_ref[:, src].astype(F32)
    taps = taps_ref[0, :, src]
    q_feat = taps[0:1] * q
    for d in range(1, FEAT):
        moved = pltpu.roll(q, d, 0)
        shifted = pltpu.roll(q_rim, (d - (FEAT - 1)) % SUB, 0)
        head = jnp.where(iota < d, shifted, moved[:SUB])
        q_feat = q_feat + taps[d : d + 1] * jnp.concatenate([head, moved[SUB:]], axis=0)
    return q_feat * (conv + skip_ref[:, src] * cur), q_feat, turned


def mix_kernel(first, has_out, h_ref, own_ref, got_ref, edge_ref, q_ref, taps_ref, skip_ref, *refs):
    refs = refs[1:] if has_out else refs
    out_hbm, head_ref, slope_ref, res_ref, turned_ref, mask_ref, lhs_ref, sems = refs
    rows = q_ref.shape[0]
    width = res_ref.shape[1]
    per = LANES // GROUP_CH
    fill_mask(mask_ref)
    turned_ref[...] = turned_filters(h_ref[pl.ds(first // GROUP_CH, width // GROUP_CH), :])
    row_group = rows_iota((per, LANES))
    lane_group = lax.broadcasted_iota(jnp.int32, (per, LANES), 1) // GROUP_CH

    run = run_of(width // LANES)
    runs = width // LANES // run

    def store(p):
        here = pl.ds(pl.multiple_of(p * run * LANES, LANES), run * LANES)
        there = pl.ds(pl.multiple_of(first + p * run * LANES, LANES), run * LANES)
        return pltpu.make_async_copy(
            res_ref.at[:, here], out_hbm.at[pl.ds(SUB, rows - SUB), there], sems.at[p]
        )

    @pl.loop(0, runs)
    def _(p):
        for u in range(run):
            c = p * run + u
            dst = lanes_at(c)
            src = lanes_at(c + first // LANES)
            mixed, q_feat, turned = mix_tile(
                turned_ref, mask_ref, lhs_ref.at[u], own_ref, got_ref, edge_ref, q_ref, taps_ref, skip_ref, None, src, dst, c
            )
            res_ref[:, dst] = mixed[SUB:].astype(BF16)
            head_ref[:, dst] = mixed[:SUB]
            last_tap = jnp.where(row_group == lane_group, jnp.broadcast_to(turned[:, 1:2], (per, LANES)), 0.0)
            slope_ref[:, dst] = q_feat[:8] * jnp.sum(last_tap, axis=0, keepdims=True)
        store(p).start()

    @pl.loop(0, runs)
    def _(p):
        store(p).wait()


def mix(filters, own, got, edges, q, taps, skip, out, first):
    rows, full = q.shape
    width = own.shape[1]
    run = run_of(width // LANES)
    per = LANES // GROUP_CH
    args = [filters, own, got, edges, q, taps, skip]
    in_specs = [VMEM] * len(args)
    if out is not None:
        in_specs.append(HBM)
        args.append(out)
    return pl.pallas_call(
        functools.partial(mix_kernel, first, out is not None),
        in_specs=in_specs,
        out_specs=[HBM, VMEM, VMEM],
        out_shape=[
            jax.ShapeDtypeStruct((rows, full), BF16),
            jax.ShapeDtypeStruct((SUB, width), F32),
            jax.ShapeDtypeStruct((8, width), F32),
        ],
        scratch_shapes=[
            pltpu.VMEM((rows - SUB, width), BF16),
            pltpu.VMEM((width // GROUP_CH, FILT), F32),
            pltpu.VMEM((rows, 2 * FILT), BF16),
            pltpu.VMEM((run, per * rows // 2, 2 * FILT), BF16),
            pltpu.SemaphoreType.DMA((width // LANES // run,)),
        ],
        input_output_aliases={} if out is None else {len(args) - 1: 0},
        compiler_params=params(12),
        cost_estimate=LONG,
        name="mix",
    )(*args)


def last_mix_kernel(first, parts, h_ref, own_ref, got_ref, edge_ref, q_ref, taps_ref, skip_ref, *refs):
    heads, slopes = refs[:parts], refs[parts : 2 * parts]
    _, out_hbm, res_ref, top_ref, turned_ref, mask_ref, lhs_ref, sems, top_sem = refs[2 * parts :]
    rows, full = q_ref.shape
    width = res_ref.shape[1]
    fill_mask(mask_ref)
    turned_ref[...] = turned_filters(h_ref[pl.ds(first // GROUP_CH, width // GROUP_CH), :])
    iota = rows_iota((SUB, LANES))

    def before_at(c_all):
        tiles = width // LANES
        col = lax.rem(c_all, tiles)
        row = lax.div(c_all, tiles)
        x = got_ref[rows:, lanes_at(col)].astype(F32)
        return jnp.sum(jnp.where(iota == row, x, 0.0), axis=0, keepdims=True)

    at_first = 0
    for head_ref, slope_ref in zip(heads, slopes):
        wide = head_ref.shape[1]

        @pl.loop(0, wide // LANES, unroll=2)
        def _(c):
            c_all = c + at_first // LANES
            head = head_ref[:, lanes_at(c)]
            more = slope_ref[:, lanes_at(c)] * before_at(c_all)
            more = jnp.concatenate([more, jnp.zeros_like(more)], axis=0)
            top_ref[:, lanes_at(c_all)] = jnp.where(iota == 0, head + more, head).astype(BF16)

        at_first += wide
    top = pltpu.make_async_copy(top_ref, out_hbm.at[pl.ds(0, SUB), pl.ds(0, first)], top_sem)
    top.start()

    run = run_of(width // LANES)
    runs = width // LANES // run

    def store(p):
        here = pl.ds(pl.multiple_of(p * run * LANES, LANES), run * LANES)
        there = pl.ds(pl.multiple_of(first + p * run * LANES, LANES), run * LANES)
        return pltpu.make_async_copy(res_ref.at[:, here], out_hbm.at[:, there], sems.at[p])

    @pl.loop(0, runs)
    def _(p):
        for u in range(run):
            c = p * run + u
            dst = lanes_at(c)
            src = lanes_at(c + first // LANES)
            before = before_at(c + first // LANES)
            mixed, _, _ = mix_tile(
                turned_ref, mask_ref, lhs_ref.at[u], own_ref, got_ref, edge_ref, q_ref, taps_ref, skip_ref, before, src, dst, c
            )
            res_ref[:, dst] = mixed.astype(BF16)
        store(p).start()

    @pl.loop(0, runs)
    def _(p):
        store(p).wait()

    top.wait()


def last_mix(filters, own, got, edges, q, taps, skip, heads, slopes, out, first):
    rows, full = q.shape
    width = own.shape[1]
    run = run_of(width // LANES)
    per = LANES // GROUP_CH
    args = [filters, own, got, edges, q, taps, skip, *heads, *slopes, out]
    return pl.pallas_call(
        functools.partial(last_mix_kernel, first, len(heads)),
        in_specs=[VMEM] * (len(args) - 1) + [HBM],
        out_specs=HBM,
        out_shape=jax.ShapeDtypeStruct((rows, full), BF16),
        scratch_shapes=[
            pltpu.VMEM((rows, width), BF16),
            pltpu.VMEM((SUB, first), BF16),
            pltpu.VMEM((width // GROUP_CH, FILT), F32),
            pltpu.VMEM((rows, 2 * FILT), BF16),
            pltpu.VMEM((run, per * rows // 2, 2 * FILT), BF16),
            pltpu.SemaphoreType.DMA((width // LANES // run,)),
            pltpu.SemaphoreType.DMA,
        ],
        input_output_aliases={len(args) - 1: 0},
        compiler_params=params(12),
        cost_estimate=LONG,
        name="mix_last",
    )(*args)


def shards(q_stream, k_stream, v_stream, feat_filter, long_filter, skip_gain):
    rows, width = q_stream.shape
    skip = skip_gain.reshape(1, width)
    unit = width // 32
    sizes = [8 * unit, 9 * unit, 8 * unit, 7 * unit]
    starts = [sum(sizes[:i]) for i in range(len(sizes))]
    streams = (k_stream, v_stream, q_stream, feat_filter)
    own = [first_gate(*streams, sizes[0])]
    got = [passed_along(own[0])]
    more = gate(*streams, own[0], starts[1:], sizes[1:])
    own += more[:2]
    got += [passed_along(own[1]), passed_along(own[2])]
    last, edges = last_gate(k_stream, v_stream, feat_filter, got[0], more[2])
    own.append(last)
    got.append(passed_along(last))
    out = None
    heads = []
    slopes = []
    for first, a, b in zip(starts[:3], own, got):
        out, head, slope = mix(long_filter, a, b, edges, q_stream, feat_filter, skip, out, first)
        heads.append(head)
        slopes.append(slope)
    return last_mix(
        long_filter, own[3], got[3], edges, q_stream, feat_filter, skip, heads, slopes, out, starts[3]
    )


def solution(mesh):
    in_specs = (
        P(("rep", "seq"), None),
        P(("rep", "seq"), None),
        P(("rep", "seq"), None),
        P(),
        P(),
        P(),
    )
    out_specs = P(("rep", "seq"), None)
    return jax.shard_map(shards, mesh=mesh, in_specs=in_specs, out_specs=out_specs, check_vma=False)
```

time: 139 us -> 35.5 us (0.26)
  the two profiles are of different devices: /device:TPU:0 before, /device:TPU:16 now
where the time goes in v2:
time: 35.5 us; the launch traced here: 35.3 us
  Pallas kernels  17.3 us (49%)
  starting transfers between devices  9.42 us (27%)
  waiting for transfers between devices  8.4 us (24%)
    ppermute x4, starting transfers between devices, passed_along(): return lax.ppermute(shard, 'seq', [(i, i + 1) for i in range(length - 1)])  9.42 us
    ppermute x4, waiting for transfers between devices, passed_along(): return lax.ppermute(shard, 'seq', [(i, i + 1) for i in range(length - 1)])  8.4 us
    pallas_call x3, Pallas kernels, mix(): pl.pallas_call(functools.partial(mix_kernel, first, out is not None), in_...  8.02 us
    pallas_call x1, Pallas kernels, last_mix(): pl.pallas_call(functools.partial(last_mix_kernel, first, len(heads)), in_...  3.08 us
    pallas_call x1, Pallas kernels, gate(): pl.pallas_call(functools.partial(gate_kernel, firsts), in_specs=[VMEM] *...  2.81 us
    pallas_call x1, Pallas kernels, first_gate(): pl.pallas_call(first_gate_kernel, in_specs=[HBM] * 4, out_specs=VMEM, out...  2.45 us
    pallas_call x1, Pallas kernels, last_gate(): pl.pallas_call(last_gate_kernel, in_specs=[VMEM] * 5, out_specs=[VMEM] *...  0.91 us
  transfers between devices with their start and end apart: 4, of which 4 were waited for; matrix products, arithmetic and copies ran while one was open for 0% of the time, Pallas kernels for 33%

profile of v2, /device:TPU:16, one launch (start us, length us, event | category | flops | bytes accessed | tf_op | source)
XLA Modules:
  0.0 35.3 jit_solution(84231765093680231)
XLA Ops:
  0.0 0.0 copy-start
  0.0 0.0 copy-start.2
  0.0 0.0 copy-start.3
  0.0 0.0 copy-start.1
  0.0 2.5 %gate_first.1._.own_ref = bf16[144,2048]{1,0:T(8,128)(2,1)S(1)} custom-call(bf16[128,8192]{1,0:T(8,128)(2,1)} %kh_ref.1, bf16[128,8192]{1,0:T(8,128)(2,1)} %vh_ref.1, bf16[128,8192]{1,0:T(8,128)(2,1)} %q_ref.9, f32[3,3,8192]{2,1,0:T(4,128)} %taps_ref.11), custom_call_target="tpu_custom_call" | custom-call | flops 1000 | bytes 1000 | tf_op jit(solution)/shard_map/gate_first/pallas_call | solution.py:123
  2.5 2.1 %collective-permute-start = (bf16[144,2048]{1,0:T(8,128)(2,1)S(1)}, bf16[144,2048]{1,0:T(8,128)(2,1)S(1)}, u32[]{:S(2)}, u32[]{:S(2)}) collective-permute-start(bf16[144,2048]{1,0:T(8,128)(2,1)S(1)} %gate_first.1._.own_ref), channel_id=1, source_target_pairs={{0,1},{1,2},{2,3},{3,4},{4,5},{5,6},{6,7},{7,8},{8,9},{9,10},{10,1... | collective-permute-start | bytes 1769480 | tf_op jit(solution)/shard_map/ppermute | solution.py:27
  4.5 0.0 copy-done
  4.6 0.0 copy-done.2
  4.6 0.0 copy-done.3
  4.6 0.0 copy-done.1
  4.6 2.8 %gate.1 = (bf16[128,2304]{1,0:T(8,128)(2,1)S(1)}, bf16[128,2048]{1,0:T(8,128)(2,1)S(1)}, bf16[128,1792]{1,0:T(8,128)(2,1)S(1)}) custom-call(bf16[128,8192]{1,0:T(8,128)(2,1)S(1)} %copy-done.2, bf16[128,8192]{1,0:T(8,128)(2,1)S(1)} %copy-done.3, bf16[128,8192]{1,0:T(8,128)(2,1)S(1)} %copy-done, f32[3,3,8192]{2,1,0:T(4,128)S(1)} %copy-done.1, ...), custom_call_target="tpu_custom_call" | custom-call | flops 1000 | bytes 1000 | tf_op jit(solution)/shard_map/gate/pallas_call | solution.py:155
  7.4 3.5 %collective-permute-start.2 = (bf16[128,2304]{1,0:T(8,128)(2,1)S(1)}, bf16[128,2304]{1,0:T(8,128)(2,1)S(1)}, u32[]{:S(2)}, u32[]{:S(2)}) collective-permute-start(bf16[128,2304]{1,0:T(8,128)(2,1)S(1)} %get-tuple-element.23.own_ref), channel_id=1, source_target_pairs={{0,1},{1,2},{2,3},{3,4},{4,5},{5,6},{6,7},{7,8},{8,9},{9,10},{10,1... | collective-permute-start | bytes 1769480 | tf_op jit(solution)/shard_map/ppermute | solution.py:27
  10.9 1.9 %collective-permute-start.3 = (bf16[128,2048]{1,0:T(8,128)(2,1)S(1)}, bf16[128,2048]{1,0:T(8,128)(2,1)S(1)}, u32[]{:S(2)}, u32[]{:S(2)}) collective-permute-start(bf16[128,2048]{1,0:T(8,128)(2,1)S(1)} %get-tuple-element.26.own_ref), channel_id=1, source_target_pairs={{0,1},{1,2},{2,3},{3,4},{4,5},{5,6},{6,7},{7,8},{8,9},{9,10},{10,1... | collective-permute-start | bytes 1572872 | tf_op jit(solution)/shard_map/ppermute | solution.py:27
  12.9 1.9 %collective-permute-done.rim_ref.got_ref = bf16[144,2048]{1,0:T(8,128)(2,1)S(1)} collective-permute-done((bf16[144,2048]{1,0:T(8,128)(2,1)S(1)}, bf16[144,2048]{1,0:T(8,128)(2,1)S(1)}, u32[]{:S(2)}, u32[]{:S(2)}) %collective-permute-start) | collective-permute-done | bytes 589856 | tf_op jit(solution)/shard_map/ppermute | solution.py:27
  14.7 0.0 copy-start.4
  14.7 0.0 copy-start.5
  14.7 0.9 %gate_last.1 = (bf16[144,1792]{1,0:T(8,128)(2,1)S(1)}, bf16[16,8192]{1,0:T(8,128)(2,1)S(1)}) custom-call(bf16[128,8192]{1,0:T(8,128)(2,1)S(1)} %copy-done.2, bf16[128,8192]{1,0:T(8,128)(2,1)S(1)} %copy-done.3, f32[3,3,8192]{2,1,0:T(4,128)S(1)} %copy-done.1, bf16[144,2048]{1,0:T(8,128)(2,1)S(1)} %collective-permute-done.rim_ref.got_ref, ...), custom_call_target="tpu_custom_call" | custom-call | flops 1000 | bytes 1000 | tf_op jit(solution)/shard_map/gate_last/pallas_call | solution.py:199
  15.6 1.9 %collective-permute-start.1 = (bf16[144,1792]{1,0:T(8,128)(2,1)S(1)}, bf16[144,1792]{1,0:T(8,128)(2,1)S(1)}, u32[]{:S(2)}, u32[]{:S(2)}) collective-permute-start(bf16[144,1792]{1,0:T(8,128)(2,1)S(1)} %get-tuple-element.20.own_ref), channel_id=1, source_target_pairs={{0,1},{1,2},{2,3},{3,4},{4,5},{5,6},{6,7},{7,8},{8,9},{9,10},{10,1... | collective-permute-start | bytes 1548296 | tf_op jit(solution)/shard_map/ppermute | solution.py:27
  17.6 0.0 copy-done.4
  17.6 0.0 copy-done.5
  17.6 2.5 %mix.3 = (bf16[128,8192]{1,0:T(8,128)(2,1)}, f32[16,2048]{1,0:T(8,128)S(1)}, f32[8,2048]{1,0:T(8,128)S(1)}) custom-call(bf16[512,128]{1,0:T(8,128)(2,1)S(1)} %copy-done.4, bf16[144,2048]{1,0:T(8,128)(2,1)S(1)} %gate_first.1._.own_ref, bf16[144,2048]{1,0:T(8,128)(2,1)S(1)} %collective-permute-done.rim_ref.got_ref, ...), custom_call_target="tpu_custom_call" | custom-call | flops 1000 | bytes 67108864 | tf_op jit(solution)/shard_map/mix/pallas_call | solution.py:338
  20.1 0.9 %collective-permute-done.2.got_ref = bf16[128,2304]{1,0:T(8,128)(2,1)S(1)} collective-permute-done((bf16[128,2304]{1,0:T(8,128)(2,1)S(1)}, bf16[128,2304]{1,0:T(8,128)(2,1)S(1)}, u32[]{:S(2)}, u32[]{:S(2)}) %collective-permute-start.2) | collective-permute-done | bytes 589856 | tf_op jit(solution)/shard_map/ppermute | solution.py:27
  21.0 2.9 %mix.4 = (bf16[128,8192]{1,0:T(8,128)(2,1)}, f32[16,2304]{1,0:T(8,128)S(1)}, f32[8,2304]{1,0:T(8,128)S(1)}) custom-call(bf16[512,128]{1,0:T(8,128)(2,1)S(1)} %copy-done.4, bf16[128,2304]{1,0:T(8,128)(2,1)S(1)} %get-tuple-element.23.own_ref, bf16[128,2304]{1,0:T(8,128)(2,1)S(1)} %collective-permute-done.2.got_ref, ...), custom_call_target="tpu_custom_call", output_to_operand_aliasing={{0}: (7, {})} | custom-call | flops 1000 | bytes 67108864 | tf_op jit(solution)/shard_map/mix/pallas_call | solution.py:338
  23.9 2.7 %collective-permute-done.3.got_ref = bf16[128,2048]{1,0:T(8,128)(2,1)S(1)} collective-permute-done((bf16[128,2048]{1,0:T(8,128)(2,1)S(1)}, bf16[128,2048]{1,0:T(8,128)(2,1)S(1)}, u32[]{:S(2)}, u32[]{:S(2)}) %collective-permute-start.3) | collective-permute-done | bytes 524320 | tf_op jit(solution)/shard_map/ppermute | solution.py:27
  26.7 2.6 %mix.5 = (bf16[128,8192]{1,0:T(8,128)(2,1)}, f32[16,2048]{1,0:T(8,128)S(1)}, f32[8,2048]{1,0:T(8,128)S(1)}) custom-call(bf16[512,128]{1,0:T(8,128)(2,1)S(1)} %copy-done.4, bf16[128,2048]{1,0:T(8,128)(2,1)S(1)} %get-tuple-element.26.own_ref, bf16[128,2048]{1,0:T(8,128)(2,1)S(1)} %collective-permute-done.3.got_ref, ...), custom_call_target="tpu_custom_call", output_to_operand_aliasing={{0}: (7, {})} | custom-call | flops 1000 | bytes 67108864 | tf_op jit(solution)/shard_map/mix/pallas_call | solution.py:338
  29.3 2.9 %collective-permute-done.1.got_ref = bf16[144,1792]{1,0:T(8,128)(2,1)S(1)} collective-permute-done((bf16[144,1792]{1,0:T(8,128)(2,1)S(1)}, bf16[144,1792]{1,0:T(8,128)(2,1)S(1)}, u32[]{:S(2)}, u32[]{:S(2)}) %collective-permute-start.1) | collective-permute-done | bytes 516128 | tf_op jit(solution)/shard_map/ppermute | solution.py:27
  32.2 3.1 %mix_last.1 = bf16[128,8192]{1,0:T(8,128)(2,1)} custom-call(bf16[512,128]{1,0:T(8,128)(2,1)S(1)} %copy-done.4, bf16[144,1792]{1,0:T(8,128)(2,1)S(1)} %get-tuple-element.20.own_ref, bf16[144,1792]{1,0:T(8,128)(2,1)S(1)} %collective-permute-done.1.got_ref, bf16[16,8192]{1,0:T(8,128)(2,1)S(1)} %get-tuple-element.21.edge_ref, ...), custom_call_target="tpu_custom_call", output_to_operand_aliasing={{}: (13, {})} | custom-call | flops 1000 | bytes 67108864 | tf_op jit(solution)/shard_map/mix_last/pallas_call | solution.py:427
Async XLA Ops:
  0.0 4.5 %copy-start = (bf16[128,8192]{1,0:T(8,128)(2,1)S(1)}, bf16[128,8192]{1,0:T(8,128)(2,1)}, u32[]{:S(2)}) copy-start(bf16[128,8192]{1,0:T(8,128)(2,1)} %q_ref.9) | copy-start | bytes 6291460
  0.0 4.6 %copy-start.2 = (bf16[128,8192]{1,0:T(8,128)(2,1)S(1)}, bf16[128,8192]{1,0:T(8,128)(2,1)}, u32[]{:S(2)}) copy-start(bf16[128,8192]{1,0:T(8,128)(2,1)} %kh_ref.1) | copy-start | bytes 6291460
  0.0 4.6 %copy-start.3 = (bf16[128,8192]{1,0:T(8,128)(2,1)S(1)}, bf16[128,8192]{1,0:T(8,128)(2,1)}, u32[]{:S(2)}) copy-start(bf16[128,8192]{1,0:T(8,128)(2,1)} %vh_ref.1) | copy-start | bytes 6291460
  0.0 4.6 %copy-start.1 = (f32[3,3,8192]{2,1,0:T(4,128)S(1)}, f32[3,3,8192]{2,1,0:T(4,128)}, u32[]{:S(2)}) copy-start(f32[3,3,8192]{2,1,0:T(4,128)} %taps_ref.11) | copy-start | bytes 884740
  2.5 12.2 %collective-permute-start = (bf16[144,2048]{1,0:T(8,128)(2,1)S(1)}, bf16[144,2048]{1,0:T(8,128)(2,1)S(1)}, u32[]{:S(2)}, u32[]{:S(2)}) collective-permute-start(bf16[144,2048]{1,0:T(8,128)(2,1)S(1)} %gate_first.1._.own_ref), channel_id=1, source_target_pairs={{0,1},{1,2},{2,3},{3,4},{4,5},{5,6},{6,7},{7,8},{8,9},{9,10},{10,1... | collective-permute-start | bytes 1769480 | tf_op jit(solution)/shard_map/ppermute | solution.py:27
  7.4 13.6 %collective-permute-start.2 = (bf16[128,2304]{1,0:T(8,128)(2,1)S(1)}, bf16[128,2304]{1,0:T(8,128)(2,1)S(1)}, u32[]{:S(2)}, u32[]{:S(2)}) collective-permute-start(bf16[128,2304]{1,0:T(8,128)(2,1)S(1)} %get-tuple-element.23.own_ref), channel_id=1, source_target_pairs={{0,1},{1,2},{2,3},{3,4},{4,5},{5,6},{6,7},{7,8},{8,9},{9,10},{10,1... | collective-permute-start | bytes 1769480 | tf_op jit(solution)/shard_map/ppermute | solution.py:27
  10.9 15.7 %collective-permute-start.3 = (bf16[128,2048]{1,0:T(8,128)(2,1)S(1)}, bf16[128,2048]{1,0:T(8,128)(2,1)S(1)}, u32[]{:S(2)}, u32[]{:S(2)}) collective-permute-start(bf16[128,2048]{1,0:T(8,128)(2,1)S(1)} %get-tuple-element.26.own_ref), channel_id=1, source_target_pairs={{0,1},{1,2},{2,3},{3,4},{4,5},{5,6},{6,7},{7,8},{8,9},{9,10},{10,1... | collective-permute-start | bytes 1572872 | tf_op jit(solution)/shard_map/ppermute | solution.py:27
  14.7 2.9 %copy-start.4 = (bf16[512,128]{1,0:T(8,128)(2,1)S(1)}, bf16[512,128]{1,0:T(8,128)(2,1)}, u32[]{:S(2)}) copy-start(bf16[512,128]{1,0:T(8,128)(2,1)} %h_ref.7) | copy-start | bytes 393220
  14.7 2.9 %copy-start.5 = (f32[8192]{0:T(1024)S(1)}, f32[8192]{0:T(1024)}, u32[]{:S(2)}) copy-start(f32[8192]{0:T(1024)} %param.11) | copy-start | bytes 98308
  15.6 16.5 %collective-permute-start.1 = (bf16[144,1792]{1,0:T(8,128)(2,1)S(1)}, bf16[144,1792]{1,0:T(8,128)(2,1)S(1)}, u32[]{:S(2)}, u32[]{:S(2)}) collective-permute-start(bf16[144,1792]{1,0:T(8,128)(2,1)S(1)} %get-tuple-element.20.own_ref), channel_id=1, source_target_pairs={{0,1},{1,2},{2,3},{3,4},{4,5},{5,6},{6,7},{7,8},{8,9},{9,10},{10,1... | collective-permute-start | bytes 1548296 | tf_op jit(solution)/shard_map/ppermute | solution.py:27

commit v3 on v2

--- a/solution.py
+++ b/solution.py
@@ -22,9 +22,13 @@
 LONG = pl.CostEstimate(flops=1000, bytes_accessed=64 * MIB, transcendentals=0)
 
 
-def passed_along(shard):
+def passed_along(shard, first=0, step=1):
     length = lax.axis_size("seq")
-    return lax.ppermute(shard, "seq", [(i, i + 1) for i in range(length - 1)])
+    return lax.ppermute(shard, "seq", [(i, i + 1) for i in range(first, length - 1, step)])
+
+
+def sends_first():
+    return lax.rem(lax.axis_index("seq"), 2) == 1
 
 
 def feature(x, taps):
@@ -67,9 +71,33 @@
     out_ref[SUB:rows, dst] = gated[SUB:].astype(BF16)
 
 
-def first_gate_kernel(k_hbm, v_hbm, q_hbm, taps_hbm, out_ref, k_ref, v_ref, taps_ref, qt_ref, kt_ref, vt_ref, sems):
+def rim_rows(kt_ref, vt_ref, out_ref):
+    full = kt_ref.shape[1]
+    rows, width = out_ref.shape
+    last = kt_ref.shape[0] - SUB
+    iota = rows_iota((SUB, LANES))
+
+    @pl.loop(0, width // LANES, unroll=2)
+    def _(c):
+        tail = jnp.zeros((SUB, LANES), F32)
+        for b in range(pl.cdiv(full, width)):
+            low = 2 * (FEAT - 1) * b
+            at = lanes_at(lax.rem(c + b * (width // LANES), full // LANES))
+            kt = pltpu.roll(kt_ref[last:, at].astype(F32), (low + FEAT - 1) % SUB, 0)
+            vt = pltpu.roll(vt_ref[last:, at].astype(F32), (low + 2 * (FEAT - 1)) % SUB, 0)
+            tail = jnp.where((iota >= low) & (iota < low + FEAT - 1), kt, tail)
+            tail = jnp.where((iota >= low + FEAT - 1) & (iota < low + 2 * (FEAT - 1)), vt, tail)
+        out_ref[rows - SUB :, lanes_at(c)] = tail.astype(BF16)
+
+
+def first_gate_kernel(*refs):
+    @pl.when(sends_first())
+    def _():
+        first_gate_body(*refs)
+
+
+def first_gate_body(k_hbm, v_hbm, q_hbm, taps_hbm, out_ref, k_ref, v_ref, taps_ref, qt_ref, kt_ref, vt_ref, sems):
     rows, width = k_ref.shape
-    full = kt_ref.shape[1]
     pieces = width // PIECE
     last = pl.ds(rows - SUB, SUB)
 
@@ -103,19 +131,7 @@
 
     rest[2].wait()
     rest[3].wait()
-    iota = rows_iota((SUB, LANES))
-
-    @pl.loop(0, width // LANES)
-    def _(c):
-        tail = jnp.zeros((SUB, LANES), F32)
-        for b in range(full // width):
-            low = 2 * (FEAT - 1) * b
-            at = lanes_at(c + b * (width // LANES))
-            kt = pltpu.roll(kt_ref[:, at].astype(F32), (low + FEAT - 1) % SUB, 0)
-            vt = pltpu.roll(vt_ref[:, at].astype(F32), (low + 2 * (FEAT - 1)) % SUB, 0)
-            tail = jnp.where((iota >= low) & (iota < low + FEAT - 1), kt, tail)
-            tail = jnp.where((iota >= low + FEAT - 1) & (iota < low + 2 * (FEAT - 1)), vt, tail)
-        out_ref[rows:, lanes_at(c)] = tail.astype(BF16)
+    rim_rows(kt_ref, vt_ref, out_ref)
 
 
 def first_gate(k, v, q, taps, width):
@@ -140,74 +156,130 @@
     )(*(in_hbm(x) for x in (k, v, q, taps)))
 
 
+def gate_block(k_ref, v_ref, q_ref, taps_ref, out_ref, first):
+    rows = k_ref.shape[0]
+
+    @pl.loop(0, out_ref.shape[1] // LANES, unroll=2)
+    def _(c):
+        at = lanes_at(c + first // LANES)
+        gate_piece(k_ref, v_ref, q_ref[rows - SUB :, at], taps_ref, out_ref, at, lanes_at(c), at)
+
+
+def second_gate_kernel(first, k_ref, v_ref, q_ref, taps_ref, begun_ref, out_ref, more_ref):
+    begun = sends_first()
+
+    @pl.when(begun)
+    def _():
+        out_ref[...] = begun_ref[...]
+
+    @pl.when(jnp.logical_not(begun))
+    def _():
+        gate_block(k_ref, v_ref, q_ref, taps_ref, out_ref, 0)
+        rim_rows(k_ref, v_ref, out_ref)
+
+    gate_block(k_ref, v_ref, q_ref, taps_ref, more_ref, first)
+
+
+def second_gate(k, v, q, taps, begun, first, width):
+    return pl.pallas_call(
+        functools.partial(second_gate_kernel, first),
+        in_specs=[VMEM] * 5,
+        out_specs=[VMEM] * 2,
+        out_shape=[
+            jax.ShapeDtypeStruct(begun.shape, BF16),
+            jax.ShapeDtypeStruct((k.shape[0], width), BF16),
+        ],
+        compiler_params=params(12),
+        cost_estimate=COST,
+        name="gate_second",
+    )(k, v, q, taps, begun)
+
+
 def gate_kernel(firsts, k_ref, v_ref, q_ref, taps_ref, _, *out_refs):
-    rows = k_ref.shape[0]
     for first, out_ref in zip(firsts, out_refs):
-
-        @pl.loop(0, out_ref.shape[1] // LANES, unroll=2)
-        def _(c):
-            at = lanes_at(c + first // LANES)
-            gate_piece(k_ref, v_ref, q_ref[rows - SUB :, at], taps_ref, out_ref, at, lanes_at(c), at)
+        gate_block(k_ref, v_ref, q_ref, taps_ref, out_ref, first)
 
 
 def gate(k, v, q, taps, after, firsts, widths):
-    rows = k.shape[0]
     return pl.pallas_call(
         functools.partial(gate_kernel, firsts),
         in_specs=[VMEM] * 4 + [pl.BlockSpec(memory_space=pl.ANY)],
         out_specs=[VMEM] * len(widths),
-        out_shape=[jax.ShapeDtypeStruct((rows, w), BF16) for w in widths],
+        out_shape=[jax.ShapeDtypeStruct((k.shape[0], w), BF16) for w in widths],
         compiler_params=params(12),
         cost_estimate=COST,
         name="gate",
     )(k, v, q, taps, after)
 
 
-def last_gate_kernel(kh_ref, vh_ref, taps_ref, rim_ref, own_ref, out_ref, edge_ref):
+def settle_kernel(in_ref, out_ref):
+    out_ref[...] = in_ref[...]
+
+
+def settle(x):
+    return pl.pallas_call(
+        settle_kernel,
+        in_specs=[VMEM],
+        out_specs=VMEM,
+        out_shape=jax.ShapeDtypeStruct(x.shape, x.dtype),
+        compiler_params=params(12),
+        cost_estimate=COST,
+        name="settle",
+    )(x)
+
+
+def last_gate_kernel(k_ref, v_ref, taps_ref, crossed_ref, near_ref, own_ref, out_ref, edge_ref, got_ref):
     rows, width = own_ref.shape
-    full = kh_ref.shape[1]
-    wide = rim_ref.shape[1]
+    full = k_ref.shape[1]
+    wide = got_ref.shape[1]
     iota = rows_iota((SUB, LANES))
-
-    @pl.loop(0, wide // LANES)
-    def _(c):
-        rim = rim_ref[rows:, lanes_at(c)].astype(F32)
-        for b in range(full // wide):
-            low = 2 * (FEAT - 1) * b
+    got_ref[...] = crossed_ref[...] + near_ref[...]
+
+    for b in range(pl.cdiv(full, wide)):
+        low = 2 * (FEAT - 1) * b
+        count = min(wide, full - b * wide) // LANES
+
+        @pl.loop(0, count, unroll=2)
+        def _(c):
+            rim = got_ref[rows:, lanes_at(c)].astype(F32)
             at = lanes_at(c + b * (wide // LANES))
             feats = []
-            for i, ref in ((0, kh_ref), (1, vh_ref)):
+            for i, ref in ((0, k_ref), (1, v_ref)):
                 moved = pltpu.roll(rim, (SUB - (FEAT - 1) * (i + 1) - low) % SUB, 0)
                 x = jnp.where(iota >= SUB - (FEAT - 1), moved, ref[:SUB, at].astype(F32))
                 feats.append(feature(x, taps_ref[i + 1, :, at]))
             edge_ref[:, at] = (feats[0] * feats[1]).astype(BF16)
 
+    extra = out_ref.shape[0] - rows
+
     @pl.loop(0, width // LANES)
     def _(c):
         out_ref[:rows, lanes_at(c)] = own_ref[:, lanes_at(c)]
-        tail = jnp.zeros((SUB, LANES), F32)
+        tail = jnp.zeros((extra, LANES), F32)
         for b in range(pl.cdiv(full, width)):
             at = lanes_at(lax.rem(c + b * (width // LANES), full // LANES))
-            one = jnp.broadcast_to(edge_ref[:, at].astype(F32)[1:2], (SUB, LANES))
-            tail = jnp.where(iota == b, one, tail)
+            one = jnp.broadcast_to(edge_ref[:, at].astype(F32)[1:2], (extra, LANES))
+            tail = jnp.where(rows_iota((extra, LANES)) == b, one, tail)
         out_ref[rows:, lanes_at(c)] = tail.astype(BF16)
 
 
-def last_gate(k_head, v_head, taps, rims, own):
+def last_gate(k, v, taps, crossed, near, own):
     rows, width = own.shape
-    full = k_head.shape[1]
+    full = k.shape[1]
+    extra = pl.cdiv(pl.cdiv(full, width), 8) * 8
     return pl.pallas_call(
         last_gate_kernel,
-        in_specs=[VMEM] * 5,
-        out_specs=[VMEM] * 2,
+        in_specs=[VMEM] * 6,
+        out_specs=[VMEM] * 3,
         out_shape=[
-            jax.ShapeDtypeStruct((rows + SUB, width), BF16),
+            jax.ShapeDtypeStruct((rows + extra, width), BF16),
             jax.ShapeDtypeStruct((SUB, full), BF16),
+            jax.ShapeDtypeStruct(crossed.shape, BF16),
         ],
         compiler_params=params(12),
         cost_estimate=COST,
         name="gate_last",
-    )(k_head, v_head, taps, rims, own)
+    )(k, v, taps, crossed, near, own)
 
 
 def turned_filters(h):
@@ -372,7 +444,7 @@
         col = lax.rem(c_all, tiles)
         row = lax.div(c_all, tiles)
         x = got_ref[rows:, lanes_at(col)].astype(F32)
-        return jnp.sum(jnp.where(iota == row, x, 0.0), axis=0, keepdims=True)
+        return jnp.sum(jnp.where(rows_iota(x.shape) == row, x, 0.0), axis=0, keepdims=True)
 
     at_first = 0
     for head_ref, slope_ref in zip(heads, slopes):
@@ -452,12 +524,15 @@
     sizes = [8 * unit, 9 * unit, 8 * unit, 7 * unit]
     starts = [sum(sizes[:i]) for i in range(len(sizes))]
     streams = (k_stream, v_stream, q_stream, feat_filter)
-    own = [first_gate(*streams, sizes[0])]
-    got = [passed_along(own[0])]
-    more = gate(*streams, own[0], starts[1:], sizes[1:])
-    own += more[:2]
-    got += [passed_along(own[1]), passed_along(own[2])]
-    last, edges = last_gate(k_stream, v_stream, feat_filter, got[0], more[2])
+    begun = first_gate(*streams, sizes[0])
+    crossed = passed_along(begun, 1, 2)
+    own = list(second_gate(*streams, begun, starts[1], sizes[1]))
+    near = passed_along(own[0], 0, 2)
+    got = [None, passed_along(own[1])]
+    more, last = gate(*streams, own[1], starts[2:], sizes[2:])
+    own.append(more)
+    got.append(passed_along(more))
+    last, edges, got[0] = last_gate(k_stream, v_stream, feat_filter, settle(crossed), near, last)
     own.append(last)
     got.append(passed_along(last))
     out = None

time: 35.5 us -> 33.3 us (0.938)
  waiting for transfers between devices: 8.4 us -> 4.44 us
  starting transfers between devices: 9.42 us -> 10.9 us
  local copies, waits for them, and re-layouts: 0.02 us -> 1.16 us
  Pallas kernels: 17.3 us -> 16.4 us
    ppermute x4 -> x5, waiting for transfers between devices: 8.4 us -> 4.44 us  [passed_along(): lax.ppermute(shard, 'seq', [(i, i + 1) for i in range(first, length - 1,...]
    pallas_call x1 -> x3, Pallas kernels: 0.91 us -> 3.46 us  [the longest x1 2.27 us: second_gate(): pl.pallas_call(functools.partial(second_gate_kernel, first), in_specs=[VM...]
    pallas_call x1, Pallas kernels: 2.45 us -> 0.12 us  [first_gate(): pl.pallas_call(first_gate_kernel, in_specs=[HBM] * 4, out_specs=VMEM, out...]
    ppermute x4 -> x5, starting transfers between devices: 9.42 us -> 10.9 us  [passed_along(): lax.ppermute(shard, 'seq', [(i, i + 1) for i in range(first, length - 1,...]
    unnamed x12, local copies, waits for them, and re-layouts: 0.02 us -> 1.16 us
    pallas_call x1, Pallas kernels: 2.81 us -> 1.77 us  [gate(): pl.pallas_call(functools.partial(gate_kernel, firsts), in_specs=[VMEM] *...]
  transfers between devices with their start and end apart: 4 -> 5, of which waited for: 4 -> 2; matrix products, arithmetic and copies ran while one was open for 0% -> 0% of each run, Pallas kernels for 33% -> 40%
where the time goes in v3:
time: 33.3 us; the launch traced here: 33.1 us
  Pallas kernels  16.4 us (49%)
  starting transfers between devices  10.9 us (33%)
  waiting for transfers between devices  4.44 us (13%)
  local copies, waits for them, and re-layouts  1.16 us (3%)
    ppermute x5, starting transfers between devices, passed_along(): lax.ppermute(shard, 'seq', [(i, i + 1) for i in range(first, length - 1,...  10.9 us
    pallas_call x3, Pallas kernels, mix(): pl.pallas_call(functools.partial(mix_kernel, first, out is not None), in_...  8.04 us
    ppermute x5, waiting for transfers between devices, passed_along(): lax.ppermute(shard, 'seq', [(i, i + 1) for i in range(first, length - 1,...  4.44 us
    pallas_call x1, Pallas kernels, last_mix(): pl.pallas_call(functools.partial(last_mix_kernel, first, len(heads)), in_...  3.06 us
    pallas_call x1, Pallas kernels, second_gate(): pl.pallas_call(functools.partial(second_gate_kernel, first), in_specs=[VM...  2.27 us
    pallas_call x1, Pallas kernels, gate(): pl.pallas_call(functools.partial(gate_kernel, firsts), in_specs=[VMEM] *...  1.77 us
    unnamed x12, local copies, waits for them, and re-layouts  1.16 us
    pallas_call x1, Pallas kernels, last_gate(): pl.pallas_call(last_gate_kernel, in_specs=[VMEM] * 6, out_specs=[VMEM] *...  1.15 us
  transfers between devices with their start and end apart: 5, of which 2 were waited for; matrix products, arithmetic and copies ran while one was open for 0% of the time, Pallas kernels for 40%

profile of v3, /device:TPU:16, one launch (start us, length us, event | category | flops | bytes accessed | tf_op | source)
XLA Modules:
  0.0 33.1 jit_solution(4144863085509147156)
XLA Ops:
  0.0 0.0 copy-start
  0.0 0.0 copy-start.1
  0.0 0.0 copy-start.2
  0.0 0.0 copy-start.3
  0.0 0.1 gate_first.1.begun_ref
  0.2 1.6 %collective-permute-start = (bf16[144,2048]{1,0:T(8,128)(2,1)S(1)}, bf16[144,2048]{1,0:T(8,128)(2,1)S(1)}, u32[]{:S(2)}, u32[]{:S(2)}) collective-permute-start(bf16[144,2048]{1,0:T(8,128)(2,1)S(1)} %gate_first.1.begun_ref), channel_id=1, source_target_pairs={{1,2},{3,4},{5,6},{7,8},{9,10},{11,12},{13,14},{17,18},{19,20},{21... | collective-permute-start | bytes 1769480 | tf_op jit(solution)/shard_map/ppermute | solution.py:27
  1.7 0.0 copy-done
  1.7 0.5 %copy-done.1 = bf16[128,8192]{1,0:T(8,128)(2,1)S(1)} copy-done((bf16[128,8192]{1,0:T(8,128)(2,1)S(1)}, bf16[128,8192]{1,0:T(8,128)(2,1)}, u32[]{:S(2)}) %copy-start.1) | copy-done | bytes 2097176
  2.2 0.6 %copy-done.2 = bf16[128,8192]{1,0:T(8,128)(2,1)S(1)} copy-done((bf16[128,8192]{1,0:T(8,128)(2,1)S(1)}, bf16[128,8192]{1,0:T(8,128)(2,1)}, u32[]{:S(2)}) %copy-start.2) | copy-done | bytes 2097176
  2.9 0.0 copy-done.3
  2.9 2.3 %gate_second.1 = (bf16[144,2048]{1,0:T(8,128)(2,1)S(1)}, bf16[128,2304]{1,0:T(8,128)(2,1)S(1)}) custom-call(bf16[128,8192]{1,0:T(8,128)(2,1)S(1)} %copy-done.1, bf16[128,8192]{1,0:T(8,128)(2,1)S(1)} %copy-done.2, bf16[128,8192]{1,0:T(8,128)(2,1)S(1)} %copy-done, f32[3,3,8192]{2,1,0:T(4,128)S(1)} %copy-done.3, bf16[144,2048]{1,0:T(8,128)(2,1)S(1)} %gate_first.1.begun_ref), custom_call_target="tpu_custom_call" | custom-call | flops 1000 | bytes 1000 | tf_op jit(solution)/shard_map/gate_second/pallas_call | solution.py:184
  5.1 2.0 %collective-permute-start.1 = (bf16[144,2048]{1,0:T(8,128)(2,1)S(1)}, bf16[144,2048]{1,0:T(8,128)(2,1)S(1)}, u32[]{:S(2)}, u32[]{:S(2)}) collective-permute-start(bf16[144,2048]{1,0:T(8,128)(2,1)S(1)} %get-tuple-element.21.own_ref), channel_id=1, source_target_pairs={{0,1},{2,3},{4,5},{6,7},{8,9},{10,11},{12,13},{14,15},{16,17},{18,... | collective-permute-start | bytes 1769480 | tf_op jit(solution)/shard_map/ppermute | solution.py:27
  7.1 1.9 %collective-permute-start.3 = (bf16[128,2304]{1,0:T(8,128)(2,1)S(1)}, bf16[128,2304]{1,0:T(8,128)(2,1)S(1)}, u32[]{:S(2)}, u32[]{:S(2)}) collective-permute-start(bf16[128,2304]{1,0:T(8,128)(2,1)S(1)} %get-tuple-element.22._.own_ref), channel_id=1, source_target_pairs={{0,1},{1,2},{2,3},{3,4},{4,5},{5,6},{6,7},{7,8},{8,9},{9,10},{10,1... | collective-permute-start | bytes 1769480 | tf_op jit(solution)/shard_map/ppermute | solution.py:27
  9.0 1.8 %gate.1 = (bf16[128,2048]{1,0:T(8,128)(2,1)S(1)}, bf16[128,1792]{1,0:T(8,128)(2,1)S(1)}) custom-call(bf16[128,8192]{1,0:T(8,128)(2,1)S(1)} %copy-done.1, bf16[128,8192]{1,0:T(8,128)(2,1)S(1)} %copy-done.2, bf16[128,8192]{1,0:T(8,128)(2,1)S(1)} %copy-done, f32[3,3,8192]{2,1,0:T(4,128)S(1)} %copy-done.3, bf16[128,2304]{1,0:T(8,128)(2,1)S(1)} %get-tuple-element.22._.own_ref), custom_call_target="tpu_custom_call" | custom-call | flops 1000 | bytes 1000 | tf_op jit(solution)/shard_map/gate/pallas_call | solution.py:204
  10.8 3.5 %collective-permute-start.4 = (bf16[128,2048]{1,0:T(8,128)(2,1)S(1)}, bf16[128,2048]{1,0:T(8,128)(2,1)S(1)}, u32[]{:S(2)}, u32[]{:S(2)}) collective-permute-start(bf16[128,2048]{1,0:T(8,128)(2,1)S(1)} %get-tuple-element.30.own_ref), channel_id=1, source_target_pairs={{0,1},{1,2},{2,3},{3,4},{4,5},{5,6},{6,7},{7,8},{8,9},{9,10},{10,1... | collective-permute-start | bytes 1572872 | tf_op jit(solution)/shard_map/ppermute | solution.py:27
  14.3 0.0 collective-permute-done.in_ref
  14.4 0.0 collective-permute-done.1.near_ref
  14.4 0.0 copy-start.4
  14.4 0.0 copy-start.5
  14.4 1.1 %gate_last.1 = (bf16[136,1792]{1,0:T(8,128)(2,1)S(1)}, bf16[16,8192]{1,0:T(8,128)(2,1)S(1)}, bf16[144,2048]{1,0:T(8,128)(2,1)S(1)}) custom-call(bf16[128,8192]{1,0:T(8,128)(2,1)S(1)} %copy-done.1, bf16[128,8192]{1,0:T(8,128)(2,1)S(1)} %copy-done.2, f32[3,3,8192]{2,1,0:T(4,128)S(1)} %copy-done.3, bf16[144,2048]{1,0:T(8,128)(2,1)S(1)} %settle.1.crossed_ref, ...), custom_call_target="tpu_custom_call" | custom-call | flops 1000 | bytes 1000 | tf_op jit(solution)/shard_map/gate_last/pallas_call | solution.py:270
  15.6 1.9 %collective-permute-start.2 = (bf16[136,1792]{1,0:T(8,128)(2,1)S(1)}, bf16[136,1792]{1,0:T(8,128)(2,1)S(1)}, u32[]{:S(2)}, u32[]{:S(2)}) collective-permute-start(bf16[136,1792]{1,0:T(8,128)(2,1)S(1)} %get-tuple-element.24.own_ref), channel_id=1, source_target_pairs={{0,1},{1,2},{2,3},{3,4},{4,5},{5,6},{6,7},{7,8},{8,9},{9,10},{10,1... | collective-permute-start | bytes 1462280 | tf_op jit(solution)/shard_map/ppermute | solution.py:27
  17.5 0.0 copy-done.4
  17.5 0.0 copy-done.5
  17.5 2.6 %mix.3 = (bf16[128,8192]{1,0:T(8,128)(2,1)}, f32[16,2048]{1,0:T(8,128)S(1)}, f32[8,2048]{1,0:T(8,128)S(1)}) custom-call(bf16[512,128]{1,0:T(8,128)(2,1)S(1)} %copy-done.4, bf16[144,2048]{1,0:T(8,128)(2,1)S(1)} %get-tuple-element.21.own_ref, bf16[144,2048]{1,0:T(8,128)(2,1)S(1)} %get-tuple-element.26.got_ref, ...), custom_call_target="tpu_custom_call" | custom-call | flops 1000 | bytes 67108864 | tf_op jit(solution)/shard_map/mix/pallas_call | solution.py:410
  20.1 0.0 collective-permute-done.3.got_ref
  20.1 2.9 %mix.4 = (bf16[128,8192]{1,0:T(8,128)(2,1)}, f32[16,2304]{1,0:T(8,128)S(1)}, f32[8,2304]{1,0:T(8,128)S(1)}) custom-call(bf16[512,128]{1,0:T(8,128)(2,1)S(1)} %copy-done.4, bf16[128,2304]{1,0:T(8,128)(2,1)S(1)} %get-tuple-element.22._.own_ref, bf16[128,2304]{1,0:T(8,128)(2,1)S(1)} %collective-permute-done.3.got_ref, ...), custom_call_target="tpu_custom_call", output_to_operand_aliasing={{0}: (7, {})} | custom-call | flops 1000 | bytes 67108864 | tf_op jit(solution)/shard_map/mix/pallas_call | solution.py:410
  23.0 1.8 %collective-permute-done.4.got_ref = bf16[128,2048]{1,0:T(8,128)(2,1)S(1)} collective-permute-done((bf16[128,2048]{1,0:T(8,128)(2,1)S(1)}, bf16[128,2048]{1,0:T(8,128)(2,1)S(1)}, u32[]{:S(2)}, u32[]{:S(2)}) %collective-permute-start.4) | collective-permute-done | bytes 524320 | tf_op jit(solution)/shard_map/ppermute | solution.py:27
  24.8 2.6 %mix.5 = (bf16[128,8192]{1,0:T(8,128)(2,1)}, f32[16,2048]{1,0:T(8,128)S(1)}, f32[8,2048]{1,0:T(8,128)S(1)}) custom-call(bf16[512,128]{1,0:T(8,128)(2,1)S(1)} %copy-done.4, bf16[128,2048]{1,0:T(8,128)(2,1)S(1)} %get-tuple-element.30.own_ref, bf16[128,2048]{1,0:T(8,128)(2,1)S(1)} %collective-permute-done.4.got_ref, ...), custom_call_target="tpu_custom_call", output_to_operand_aliasing={{0}: (7, {})} | custom-call | flops 1000 | bytes 67108864 | tf_op jit(solution)/shard_map/mix/pallas_call | solution.py:410
  27.4 2.6 %collective-permute-done.2.got_ref = bf16[136,1792]{1,0:T(8,128)(2,1)S(1)} collective-permute-done((bf16[136,1792]{1,0:T(8,128)(2,1)S(1)}, bf16[136,1792]{1,0:T(8,128)(2,1)S(1)}, u32[]{:S(2)}, u32[]{:S(2)}) %collective-permute-start.2) | collective-permute-done | bytes 487456 | tf_op jit(solution)/shard_map/ppermute | solution.py:27
  30.0 3.1 %mix_last.1 = bf16[128,8192]{1,0:T(8,128)(2,1)} custom-call(bf16[512,128]{1,0:T(8,128)(2,1)S(1)} %copy-done.4, bf16[136,1792]{1,0:T(8,128)(2,1)S(1)} %get-tuple-element.24.own_ref, bf16[136,1792]{1,0:T(8,128)(2,1)S(1)} %collective-permute-done.2.got_ref, bf16[16,8192]{1,0:T(8,128)(2,1)S(1)} %get-tuple-element.25.edge_ref, ...), custom_call_target="tpu_custom_call", output_to_operand_aliasing={{}: (13, {})} | custom-call | flops 1000 | bytes 67108864 | tf_op jit(solution)/shard_map/mix_last/pallas_call | solution.py:499
  (1 shorter events, 0.0 us)
Async XLA Ops:
  0.0 1.7 %copy-start = (bf16[128,8192]{1,0:T(8,128)(2,1)S(1)}, bf16[128,8192]{1,0:T(8,128)(2,1)}, u32[]{:S(2)}) copy-start(bf16[128,8192]{1,0:T(8,128)(2,1)} %q_ref.11) | copy-start | bytes 6291460
  0.0 2.2 %copy-start.1 = (bf16[128,8192]{1,0:T(8,128)(2,1)S(1)}, bf16[128,8192]{1,0:T(8,128)(2,1)}, u32[]{:S(2)}) copy-start(bf16[128,8192]{1,0:T(8,128)(2,1)} %k_ref.5) | copy-start | bytes 6291460
  0.0 2.9 %copy-start.2 = (bf16[128,8192]{1,0:T(8,128)(2,1)S(1)}, bf16[128,8192]{1,0:T(8,128)(2,1)}, u32[]{:S(2)}) copy-start(bf16[128,8192]{1,0:T(8,128)(2,1)} %v_ref.5) | copy-start | bytes 6291460
  0.0 2.9 %copy-start.3 = (f32[3,3,8192]{2,1,0:T(4,128)S(1)}, f32[3,3,8192]{2,1,0:T(4,128)}, u32[]{:S(2)}) copy-start(f32[3,3,8192]{2,1,0:T(4,128)} %taps_ref.13) | copy-start | bytes 884740
  0.2 14.2 %collective-permute-start = (bf16[144,2048]{1,0:T(8,128)(2,1)S(1)}, bf16[144,2048]{1,0:T(8,128)(2,1)S(1)}, u32[]{:S(2)}, u32[]{:S(2)}) collective-permute-start(bf16[144,2048]{1,0:T(8,128)(2,1)S(1)} %gate_first.1.begun_ref), channel_id=1, source_target_pairs={{1,2},{3,4},{5,6},{7,8},{9,10},{11,12},{13,14},{17,18},{19,20},{21... | collective-permute-start | bytes 1769480 | tf_op jit(solution)/shard_map/ppermute | solution.py:27
  5.1 9.3 %collective-permute-start.1 = (bf16[144,2048]{1,0:T(8,128)(2,1)S(1)}, bf16[144,2048]{1,0:T(8,128)(2,1)S(1)}, u32[]{:S(2)}, u32[]{:S(2)}) collective-permute-start(bf16[144,2048]{1,0:T(8,128)(2,1)S(1)} %get-tuple-element.21.own_ref), channel_id=1, source_target_pairs={{0,1},{2,3},{4,5},{6,7},{8,9},{10,11},{12,13},{14,15},{16,17},{18,... | collective-permute-start | bytes 1769480 | tf_op jit(solution)/shard_map/ppermute | solution.py:27
  7.1 13.0 %collective-permute-start.3 = (bf16[128,2304]{1,0:T(8,128)(2,1)S(1)}, bf16[128,2304]{1,0:T(8,128)(2,1)S(1)}, u32[]{:S(2)}, u32[]{:S(2)}) collective-permute-start(bf16[128,2304]{1,0:T(8,128)(2,1)S(1)} %get-tuple-element.22._.own_ref), channel_id=1, source_target_pairs={{0,1},{1,2},{2,3},{3,4},{4,5},{5,6},{6,7},{7,8},{8,9},{9,10},{10,1... | collective-permute-start | bytes 1769480 | tf_op jit(solution)/shard_map/ppermute | solution.py:27
  10.8 14.0 %collective-permute-start.4 = (bf16[128,2048]{1,0:T(8,128)(2,1)S(1)}, bf16[128,2048]{1,0:T(8,128)(2,1)S(1)}, u32[]{:S(2)}, u32[]{:S(2)}) collective-permute-start(bf16[128,2048]{1,0:T(8,128)(2,1)S(1)} %get-tuple-element.30.own_ref), channel_id=1, source_target_pairs={{0,1},{1,2},{2,3},{3,4},{4,5},{5,6},{6,7},{7,8},{8,9},{9,10},{10,1... | collective-permute-start | bytes 1572872 | tf_op jit(solution)/shard_map/ppermute | solution.py:27
  14.4 3.1 %copy-start.4 = (bf16[512,128]{1,0:T(8,128)(2,1)S(1)}, bf16[512,128]{1,0:T(8,128)(2,1)}, u32[]{:S(2)}) copy-start(bf16[512,128]{1,0:T(8,128)(2,1)} %h_ref.7) | copy-start | bytes 393220
  14.4 3.1 %copy-start.5 = (f32[8192]{0:T(1024)S(1)}, f32[8192]{0:T(1024)}, u32[]{:S(2)}) copy-start(f32[8192]{0:T(1024)} %param.11) | copy-start | bytes 98308
  15.6 14.5 %collective-permute-start.2 = (bf16[136,1792]{1,0:T(8,128)(2,1)S(1)}, bf16[136,1792]{1,0:T(8,128)(2,1)S(1)}, u32[]{:S(2)}, u32[]{:S(2)}) collective-permute-start(bf16[136,1792]{1,0:T(8,128)(2,1)S(1)} %get-tuple-element.24.own_ref), channel_id=1, source_target_pairs={{0,1},{1,2},{2,3},{3,4},{4,5},{5,6},{6,7},{7,8},{8,9},{9,10},{10,1... | collective-permute-start | bytes 1462280 | tf_op jit(solution)/shard_map/ppermute | solution.py:27

commit v4 on v3

--- a/solution.py
+++ b/solution.py
@@ -12,14 +12,12 @@
 FEAT = 3
 LANES = 128
 SUB = 16
-PIECE = 512
 MIB = 1 << 20
 F32 = jnp.float32
 BF16 = jnp.bfloat16
 VMEM = pl.BlockSpec(memory_space=pltpu.VMEM)
 HBM = pl.BlockSpec(memory_space=pltpu.HBM)
 COST = pl.CostEstimate(flops=1000, bytes_accessed=1000, transcendentals=0)
-LONG = pl.CostEstimate(flops=1000, bytes_accessed=64 * MIB, transcendentals=0)
 
 
 def passed_along(shard, first=0, step=1):
@@ -98,11 +96,12 @@
 
 def first_gate_body(k_hbm, v_hbm, q_hbm, taps_hbm, out_ref, k_ref, v_ref, taps_ref, qt_ref, kt_ref, vt_ref, sems):
     rows, width = k_ref.shape
-    pieces = width // PIECE
+    run = run_of(width // LANES, 5)
+    pieces = width // LANES // run
     last = pl.ds(rows - SUB, SUB)
 
     def load(p, ref, hbm, i):
-        at = pl.ds(p * PIECE, PIECE)
+        at = pl.ds(p * run * LANES, run * LANES)
         return pltpu.make_async_copy(hbm.at[:, at], ref.at[:, at], sems.at[2 * p + i])
 
     rest = [
@@ -124,9 +123,9 @@
         load(p, k_ref, k_hbm, 0).wait()
         load(p, v_ref, v_hbm, 1).wait()
 
-        @pl.loop(0, PIECE // LANES)
+        @pl.loop(0, run, unroll=run)
         def _(c):
-            at = lanes_at(c + p * (PIECE // LANES))
+            at = lanes_at(c + p * run)
             gate_piece(k_ref, v_ref, qt_ref[:, at], taps_ref, out_ref, at, at, at)
 
     rest[2].wait()
@@ -148,7 +147,7 @@
             pltpu.VMEM((SUB, width), BF16),
             pltpu.VMEM((SUB, full), BF16),
             pltpu.VMEM((SUB, full), BF16),
-            pltpu.SemaphoreType.DMA((2 * (width // PIECE) + 4,)),
+            pltpu.SemaphoreType.DMA((2 * (width // LANES // run_of(width // LANES, 5)) + 4,)),
         ],
         compiler_params=params(12),
         cost_estimate=COST,
@@ -195,21 +194,25 @@
     )(k, v, q, taps, begun)
 
 
-def gate_kernel(firsts, k_ref, v_ref, q_ref, taps_ref, _, *out_refs):
+def gate_kernel(firsts, k_ref, v_ref, q_ref, taps_ref, h_ref, _, turned_ref, mask_ref, *out_refs):
     for first, out_ref in zip(firsts, out_refs):
         gate_block(k_ref, v_ref, q_ref, taps_ref, out_ref, first)
-
-
-def gate(k, v, q, taps, after, firsts, widths):
+    turned_ref[...] = turned_filters(h_ref[...])
+    fill_mask(mask_ref)
+
+
+def gate(k, v, q, taps, h, after, firsts, widths):
+    rows = k.shape[0]
     return pl.pallas_call(
         functools.partial(gate_kernel, firsts),
-        in_specs=[VMEM] * 4 + [pl.BlockSpec(memory_space=pl.ANY)],
-        out_specs=[VMEM] * len(widths),
-        out_shape=[jax.ShapeDtypeStruct((k.shape[0], w), BF16) for w in widths],
+        in_specs=[VMEM] * 5 + [pl.BlockSpec(memory_space=pl.ANY)],
+        out_specs=[VMEM] * (len(widths) + 2),
+        out_shape=[jax.ShapeDtypeStruct(h.shape, F32), jax.ShapeDtypeStruct((rows, 2 * FILT), BF16)]
+        + [jax.ShapeDtypeStruct((rows, w), BF16) for w in widths],
         compiler_params=params(12),
         cost_estimate=COST,
         name="gate",
-    )(k, v, q, taps, after)
+    )(k, v, q, taps, h, after)
 
 
 def settle_kernel(in_ref, out_ref):
@@ -303,7 +306,7 @@
     per = LANES // GROUP_CH
     iota = rows_iota((SUB, LANES))
     lane_group = lax.broadcasted_iota(jnp.int32, (8, 2 * LANES), 1) % LANES // GROUP_CH
-    turned = turned_ref[pl.ds(c * per if isinstance(c, int) else pl.multiple_of(c * per, per), per), :]
+    turned = turned_ref[pl.ds(pl.multiple_of(c * per, per), per), :]
     rings = []
     for g in range(per):
         row = jnp.broadcast_to(turned[g : g + 1], (half, FILT))
@@ -356,14 +359,12 @@
     return q_feat * (conv + skip_ref[:, src] * cur), q_feat, turned
 
 
-def mix_kernel(first, has_out, h_ref, own_ref, got_ref, edge_ref, q_ref, taps_ref, skip_ref, *refs):
+def mix_kernel(first, has_out, turned_ref, mask_ref, own_ref, got_ref, edge_ref, q_ref, taps_ref, skip_ref, *refs):
     refs = refs[1:] if has_out else refs
-    out_hbm, head_ref, slope_ref, res_ref, turned_ref, mask_ref, lhs_ref, sems = refs
+    out_hbm, head_ref, slope_ref, res_ref, lhs_ref, sems = refs
     rows = q_ref.shape[0]
     width = res_ref.shape[1]
     per = LANES // GROUP_CH
-    fill_mask(mask_ref)
-    turned_ref[...] = turned_filters(h_ref[pl.ds(first // GROUP_CH, width // GROUP_CH), :])
     row_group = rows_iota((per, LANES))
     lane_group = lax.broadcasted_iota(jnp.int32, (per, LANES), 1) // GROUP_CH
 
@@ -384,7 +385,7 @@
             dst = lanes_at(c)
             src = lanes_at(c + first // LANES)
             mixed, q_feat, turned = mix_tile(
-                turned_ref, mask_ref, lhs_ref.at[u], own_ref, got_ref, edge_ref, q_ref, taps_ref, skip_ref, None, src, dst, c
+                turned_ref, mask_ref, lhs_ref.at[u], own_ref, got_ref, edge_ref, q_ref, taps_ref, skip_ref, None, src, dst, c + first // LANES
             )
             res_ref[:, dst] = mixed[SUB:].astype(BF16)
             head_ref[:, dst] = mixed[:SUB]
@@ -397,12 +398,12 @@
         store(p).wait()
 
 
-def mix(filters, own, got, edges, q, taps, skip, out, first):
+def mix(turned, mask, own, got, edges, q, taps, skip, out, first):
     rows, full = q.shape
     width = own.shape[1]
     run = run_of(width // LANES)
     per = LANES // GROUP_CH
-    args = [filters, own, got, edges, q, taps, skip]
+    args = [turned, mask, own, got, edges, q, taps, skip]
     in_specs = [VMEM] * len(args)
     if out is not None:
         in_specs.append(HBM)
@@ -418,43 +419,36 @@
         ],
         scratch_shapes=[
             pltpu.VMEM((rows - SUB, width), BF16),
-            pltpu.VMEM((width // GROUP_CH, FILT), F32),
-            pltpu.VMEM((rows, 2 * FILT), BF16),
             pltpu.VMEM((run, per * rows // 2, 2 * FILT), BF16),
             pltpu.SemaphoreType.DMA((width // LANES // run,)),
         ],
         input_output_aliases={} if out is None else {len(args) - 1: 0},
         compiler_params=params(12),
-        cost_estimate=LONG,
+        cost_estimate=COST,
         name="mix",
     )(*args)
 
 
-def last_mix_kernel(first, parts, h_ref, own_ref, got_ref, edge_ref, q_ref, taps_ref, skip_ref, *refs):
+def last_mix_kernel(first, parts, turned_ref, mask_ref, own_ref, got_ref, edge_ref, q_ref, taps_ref, skip_ref, *refs):
     heads, slopes = refs[:parts], refs[parts : 2 * parts]
-    _, out_hbm, res_ref, top_ref, turned_ref, mask_ref, lhs_ref, sems, top_sem = refs[2 * parts :]
+    _, out_hbm, res_ref, top_ref, before_ref, lhs_ref, sems, top_sem = refs[2 * parts :]
     rows, full = q_ref.shape
     width = res_ref.shape[1]
-    fill_mask(mask_ref)
-    turned_ref[...] = turned_filters(h_ref[pl.ds(first // GROUP_CH, width // GROUP_CH), :])
     iota = rows_iota((SUB, LANES))
 
-    def before_at(c_all):
-        tiles = width // LANES
-        col = lax.rem(c_all, tiles)
-        row = lax.div(c_all, tiles)
-        x = got_ref[rows:, lanes_at(col)].astype(F32)
-        return jnp.sum(jnp.where(rows_iota(x.shape) == row, x, 0.0), axis=0, keepdims=True)
+    for b in range(pl.cdiv(full, width)):
+        count = min(width, full - b * width)
+        before_ref[:, b * width : b * width + count] = got_ref[rows:, :count].astype(F32)[b : b + 1]
 
     at_first = 0
     for head_ref, slope_ref in zip(heads, slopes):
         wide = head_ref.shape[1]
 
-        @pl.loop(0, wide // LANES, unroll=2)
+        @pl.loop(0, wide // LANES, unroll=run_of(wide // LANES))
         def _(c):
             c_all = c + at_first // LANES
             head = head_ref[:, lanes_at(c)]
-            more = slope_ref[:, lanes_at(c)] * before_at(c_all)
+            more = slope_ref[:, lanes_at(c)] * before_ref[:, lanes_at(c_all)]
             more = jnp.concatenate([more, jnp.zeros_like(more)], axis=0)
             top_ref[:, lanes_at(c_all)] = jnp.where(iota == 0, head + more, head).astype(BF16)
 
@@ -476,9 +470,9 @@
             c = p * run + u
             dst = lanes_at(c)
             src = lanes_at(c + first // LANES)
-            before = before_at(c + first // LANES)
+            before = before_ref[:, src]
             mixed, _, _ = mix_tile(
-                turned_ref, mask_ref, lhs_ref.at[u], own_ref, got_ref, edge_ref, q_ref, taps_ref, skip_ref, before, src, dst, c
+                turned_ref, mask_ref, lhs_ref.at[u], own_ref, got_ref, edge_ref, q_ref, taps_ref, skip_ref, before, src, dst, c + first // LANES
             )
             res_ref[:, dst] = mixed.astype(BF16)
         store(p).start()
@@ -490,12 +484,12 @@
     top.wait()
 
 
-def last_mix(filters, own, got, edges, q, taps, skip, heads, slopes, out, first):
+def last_mix(turned, mask, own, got, edges, q, taps, skip, heads, slopes, out, first):
     rows, full = q.shape
     width = own.shape[1]
     run = run_of(width // LANES)
     per = LANES // GROUP_CH
-    args = [filters, own, got, edges, q, taps, skip, *heads, *slopes, out]
+    args = [turned, mask, own, got, edges, q, taps, skip, *heads, *slopes, out]
     return pl.pallas_call(
         functools.partial(last_mix_kernel, first, len(heads)),
         in_specs=[VMEM] * (len(args) - 1) + [HBM],
@@ -504,15 +498,14 @@
         scratch_shapes=[
             pltpu.VMEM((rows, width), BF16),
             pltpu.VMEM((SUB, first), BF16),
-            pltpu.VMEM((width // GROUP_CH, FILT), F32),
-            pltpu.VMEM((rows, 2 * FILT), BF16),
+            pltpu.VMEM((1, full), F32),
             pltpu.VMEM((run, per * rows // 2, 2 * FILT), BF16),
             pltpu.SemaphoreType.DMA((width // LANES // run,)),
             pltpu.SemaphoreType.DMA,
         ],
         input_output_aliases={len(args) - 1: 0},
         compiler_params=params(12),
-        cost_estimate=LONG,
+        cost_estimate=COST,
         name="mix_last",
     )(*args)
 
@@ -521,7 +514,7 @@
     rows, width = q_stream.shape
     skip = skip_gain.reshape(1, width)
     unit = width // 32
-    sizes = [8 * unit, 9 * unit, 8 * unit, 7 * unit]
+    sizes = [9 * unit, 10 * unit, 9 * unit, 4 * unit]
     starts = [sum(sizes[:i]) for i in range(len(sizes))]
     streams = (k_stream, v_stream, q_stream, feat_filter)
     begun = first_gate(*streams, sizes[0])
@@ -529,7 +522,7 @@
     own = list(second_gate(*streams, begun, starts[1], sizes[1]))
     near = passed_along(own[0], 0, 2)
     got = [None, passed_along(own[1])]
-    more, last = gate(*streams, own[1], starts[2:], sizes[2:])
+    turned, mask, more, last = gate(*streams, long_filter, own[1], starts[2:], sizes[2:])
     own.append(more)
     got.append(passed_along(more))
     last, edges, got[0] = last_gate(k_stream, v_stream, feat_filter, settle(crossed), near, last)
@@ -539,11 +532,11 @@
     heads = []
     slopes = []
     for first, a, b in zip(starts[:3], own, got):
-        out, head, slope = mix(long_filter, a, b, edges, q_stream, feat_filter, skip, out, first)
+        out, head, slope = mix(turned, mask, a, b, edges, q_stream, feat_filter, skip, out, first)
         heads.append(head)
         slopes.append(slope)
     return last_mix(
-        long_filter, own[3], got[3], edges, q_stream, feat_filter, skip, heads, slopes, out, starts[3]
+        turned, mask, own[3], got[3], edges, q_stream, feat_filter, skip, heads, slopes, out, starts[3]
     )
 
 

time: 33.3 us -> 31.6 us (0.949)
  Pallas kernels: 16.4 us -> 15.6 us
  waiting for transfers between devices: 4.44 us -> 3.68 us
    pallas_call x1, Pallas kernels: 3.06 us -> 1.71 us  [last_mix(): pl.pallas_call(functools.partial(last_mix_kernel, first, len(heads)), in_...]
    ppermute x5, waiting for transfers between devices: 4.44 us -> 3.68 us  [passed_along(): lax.ppermute(shard, 'seq', [(i, i + 1) for i in range(first, length - 1,...]
    pallas_call x3, Pallas kernels: 8.04 us -> 8.46 us  [mix(): pl.pallas_call(functools.partial(mix_kernel, first, out is not None), in_...]
  transfers between devices with their start and end apart: 5 -> 5, of which waited for: 2 -> 3; matrix products, arithmetic and copies ran while one was open for 0% -> 0% of each run, Pallas kernels for 40% -> 44%
where the time goes in v4:
time: 31.6 us; the launch traced here: 31.4 us
  Pallas kernels  15.6 us (49%)
  starting transfers between devices  10.8 us (34%)
  waiting for transfers between devices  3.68 us (12%)
  local copies, waits for them, and re-layouts  1.11 us (4%)
    ppermute x5, starting transfers between devices, passed_along(): lax.ppermute(shard, 'seq', [(i, i + 1) for i in range(first, length - 1,...  10.8 us
    pallas_call x3, Pallas kernels, mix(): pl.pallas_call(functools.partial(mix_kernel, first, out is not None), in_...  8.46 us
    ppermute x5, waiting for transfers between devices, passed_along(): lax.ppermute(shard, 'seq', [(i, i + 1) for i in range(first, length - 1,...  3.68 us
    pallas_call x1, Pallas kernels, second_gate(): pl.pallas_call(functools.partial(second_gate_kernel, first), in_specs=[VM...  2.52 us
    pallas_call x1, Pallas kernels, last_mix(): pl.pallas_call(functools.partial(last_mix_kernel, first, len(heads)), in_...  1.71 us
    pallas_call x1, Pallas kernels, gate(): pl.pallas_call(functools.partial(gate_kernel, firsts), in_specs=[VMEM] *...  1.7 us
    unnamed x12, local copies, waits for them, and re-layouts  1.11 us
    pallas_call x1, Pallas kernels, last_gate(): pl.pallas_call(last_gate_kernel, in_specs=[VMEM] * 6, out_specs=[VMEM] *...  1.02 us
  transfers between devices with their start and end apart: 5, of which 3 were waited for; matrix products, arithmetic and copies ran while one was open for 0% of the time, Pallas kernels for 44%

profile of v4, /device:TPU:16, one launch (start us, length us, event | category | flops | bytes accessed | tf_op | source)
XLA Modules:
  0.0 31.4 jit_solution(8082985081115219036)
XLA Ops:
  0.0 0.0 copy-start
  0.0 0.0 copy-start.1
  0.0 0.0 copy-start.2
  0.0 0.0 copy-start.3
  0.0 0.2 gate_first.1.begun_ref
  0.2 0.0 copy-start.5
  0.2 1.6 %collective-permute-start = (bf16[144,2304]{1,0:T(8,128)(2,1)S(1)}, bf16[144,2304]{1,0:T(8,128)(2,1)S(1)}, u32[]{:S(2)}, u32[]{:S(2)}) collective-permute-start(bf16[144,2304]{1,0:T(8,128)(2,1)S(1)} %gate_first.1.begun_ref), channel_id=1, source_target_pairs={{1,2},{3,4},{5,6},{7,8},{9,10},{11,12},{13,14},{17,18},{19,20},{21... | collective-permute-start | bytes 1990664 | tf_op jit(solution)/shard_map/ppermute | solution.py:25
  1.8 0.0 copy-done
  1.8 0.5 %copy-done.1 = bf16[128,8192]{1,0:T(8,128)(2,1)S(1)} copy-done((bf16[128,8192]{1,0:T(8,128)(2,1)S(1)}, bf16[128,8192]{1,0:T(8,128)(2,1)}, u32[]{:S(2)}) %copy-start.1) | copy-done | bytes 2097176
  2.2 0.6 %copy-done.2 = bf16[128,8192]{1,0:T(8,128)(2,1)S(1)} copy-done((bf16[128,8192]{1,0:T(8,128)(2,1)S(1)}, bf16[128,8192]{1,0:T(8,128)(2,1)}, u32[]{:S(2)}) %copy-start.2) | copy-done | bytes 2097176
  2.9 0.0 copy-done.3
  2.9 2.5 %gate_second.1 = (bf16[144,2304]{1,0:T(8,128)(2,1)S(1)}, bf16[128,2560]{1,0:T(8,128)(2,1)S(1)}) custom-call(bf16[128,8192]{1,0:T(8,128)(2,1)S(1)} %copy-done.1, bf16[128,8192]{1,0:T(8,128)(2,1)S(1)} %copy-done.2, bf16[128,8192]{1,0:T(8,128)(2,1)S(1)} %copy-done, f32[3,3,8192]{2,1,0:T(4,128)S(1)} %copy-done.3, bf16[144,2304]{1,0:T(8,128)(2,1)S(1)} %gate_first.1.begun_ref), custom_call_target="tpu_custom_call" | custom-call | flops 1000 | bytes 1000 | tf_op jit(solution)/shard_map/gate_second/pallas_call | solution.py:183
  5.4 1.9 %collective-permute-start.1 = (bf16[144,2304]{1,0:T(8,128)(2,1)S(1)}, bf16[144,2304]{1,0:T(8,128)(2,1)S(1)}, u32[]{:S(2)}, u32[]{:S(2)}) collective-permute-start(bf16[144,2304]{1,0:T(8,128)(2,1)S(1)} %get-tuple-element.26.own_ref), channel_id=1, source_target_pairs={{0,1},{2,3},{4,5},{6,7},{8,9},{10,11},{12,13},{14,15},{16,17},{18,... | collective-permute-start | bytes 1990664 | tf_op jit(solution)/shard_map/ppermute | solution.py:25
  7.3 1.9 %collective-permute-start.3 = (bf16[128,2560]{1,0:T(8,128)(2,1)S(1)}, bf16[128,2560]{1,0:T(8,128)(2,1)S(1)}, u32[]{:S(2)}, u32[]{:S(2)}) collective-permute-start(bf16[128,2560]{1,0:T(8,128)(2,1)S(1)} %get-tuple-element.23._.own_ref), channel_id=1, source_target_pairs={{0,1},{1,2},{2,3},{3,4},{4,5},{5,6},{6,7},{7,8},{8,9},{9,10},{10,1... | collective-permute-start | bytes 1966088 | tf_op jit(solution)/shard_map/ppermute | solution.py:25
  9.2 0.0 copy-done.5
  9.2 1.7 %gate.1 = (f32[512,128]{1,0:T(8,128)S(1)}, bf16[128,256]{1,0:T(8,128)(2,1)S(1)}, bf16[128,2304]{1,0:T(8,128)(2,1)S(1)}, bf16[128,1024]{1,0:T(8,128)(2,1)S(1)}) custom-call(bf16[128,8192]{1,0:T(8,128)(2,1)S(1)} %copy-done.1, bf16[128,8192]{1,0:T(8,128)(2,1)S(1)} %copy-done.2, bf16[128,8192]{1,0:T(8,128)(2,1)S(1)} %copy-done, f32[3,3,8192]{2,1,0:T(4,128)S(1)} %copy-done.3, ...), custom_call_target="tpu_custom_call" | custom-call | flops 1000 | bytes 1000 | tf_op jit(solution)/shard_map/gate/pallas_call | solution.py:206
  10.9 3.5 %collective-permute-start.4 = (bf16[128,2304]{1,0:T(8,128)(2,1)S(1)}, bf16[128,2304]{1,0:T(8,128)(2,1)S(1)}, u32[]{:S(2)}, u32[]{:S(2)}) collective-permute-start(bf16[128,2304]{1,0:T(8,128)(2,1)S(1)} %get-tuple-element.34.own_ref), channel_id=1, source_target_pairs={{0,1},{1,2},{2,3},{3,4},{4,5},{5,6},{6,7},{7,8},{8,9},{9,10},{10,1... | collective-permute-start | bytes 1769480 | tf_op jit(solution)/shard_map/ppermute | solution.py:25
  14.5 0.0 collective-permute-done.in_ref
  14.5 0.0 collective-permute-done.1.near_ref
  14.5 0.0 copy-start.4
  14.6 1.0 %gate_last.1 = (bf16[136,1024]{1,0:T(8,128)(2,1)S(1)}, bf16[16,8192]{1,0:T(8,128)(2,1)S(1)}, bf16[144,2304]{1,0:T(8,128)(2,1)S(1)}) custom-call(bf16[128,8192]{1,0:T(8,128)(2,1)S(1)} %copy-done.1, bf16[128,8192]{1,0:T(8,128)(2,1)S(1)} %copy-done.2, f32[3,3,8192]{2,1,0:T(4,128)S(1)} %copy-done.3, bf16[144,2304]{1,0:T(8,128)(2,1)S(1)} %settle.1.crossed_ref, ...), custom_call_target="tpu_custom_call" | custom-call | flops 1000 | bytes 1000 | tf_op jit(solution)/shard_map/gate_last/pallas_call | solution.py:273
  15.6 1.9 %collective-permute-start.2 = (bf16[136,1024]{1,0:T(8,128)(2,1)S(1)}, bf16[136,1024]{1,0:T(8,128)(2,1)S(1)}, u32[]{:S(2)}, u32[]{:S(2)}) collective-permute-start(bf16[136,1024]{1,0:T(8,128)(2,1)S(1)} %get-tuple-element.28.own_ref), channel_id=1, source_target_pairs={{0,1},{1,2},{2,3},{3,4},{4,5},{5,6},{6,7},{7,8},{8,9},{9,10},{10,1... | collective-permute-start | bytes 835592 | tf_op jit(solution)/shard_map/ppermute | solution.py:25
  17.5 0.0 copy-done.4
  17.5 2.7 %mix.3 = (bf16[128,8192]{1,0:T(8,128)(2,1)}, f32[16,2304]{1,0:T(8,128)S(1)}, f32[8,2304]{1,0:T(8,128)S(1)}) custom-call(f32[512,128]{1,0:T(8,128)S(1)} %get-tuple-element.24.turned_ref, bf16[128,256]{1,0:T(8,128)(2,1)S(1)} %get-tuple-element.25.mask_ref, bf16[144,2304]{1,0:T(8,128)(2,1)S(1)} %get-tuple-element.26.own_ref, ...), custom_call_target="tpu_custom_call" | custom-call | flops 1000 | bytes 1000 | tf_op jit(solution)/shard_map/mix/pallas_call | solution.py:411
  20.2 0.1 collective-permute-done.3.got_ref
  20.4 3.1 %mix.4 = (bf16[128,8192]{1,0:T(8,128)(2,1)}, f32[16,2560]{1,0:T(8,128)S(1)}, f32[8,2560]{1,0:T(8,128)S(1)}) custom-call(f32[512,128]{1,0:T(8,128)S(1)} %get-tuple-element.24.turned_ref, bf16[128,256]{1,0:T(8,128)(2,1)S(1)} %get-tuple-element.25.mask_ref, bf16[128,2560]{1,0:T(8,128)(2,1)S(1)} %get-tuple-element.23._.own_ref, ...), custom_call_target="tpu_custom_call", output_to_operand_aliasing={{0}: (8, {})} | custom-call | flops 1000 | bytes 1000 | tf_op jit(solution)/shard_map/mix/pallas_call | solution.py:411
  23.4 3.3 %collective-permute-done.4.got_ref = bf16[128,2304]{1,0:T(8,128)(2,1)S(1)} collective-permute-done((bf16[128,2304]{1,0:T(8,128)(2,1)S(1)}, bf16[128,2304]{1,0:T(8,128)(2,1)S(1)}, u32[]{:S(2)}, u32[]{:S(2)}) %collective-permute-start.4) | collective-permute-done | bytes 589856 | tf_op jit(solution)/shard_map/ppermute | solution.py:25
  26.7 2.7 %mix.5 = (bf16[128,8192]{1,0:T(8,128)(2,1)}, f32[16,2304]{1,0:T(8,128)S(1)}, f32[8,2304]{1,0:T(8,128)S(1)}) custom-call(f32[512,128]{1,0:T(8,128)S(1)} %get-tuple-element.24.turned_ref, bf16[128,256]{1,0:T(8,128)(2,1)S(1)} %get-tuple-element.25.mask_ref, bf16[128,2304]{1,0:T(8,128)(2,1)S(1)} %get-tuple-element.34.own_ref, ...), custom_call_target="tpu_custom_call", output_to_operand_aliasing={{0}: (8, {})} | custom-call | flops 1000 | bytes 1000 | tf_op jit(solution)/shard_map/mix/pallas_call | solution.py:411
  29.4 0.3 collective-permute-done.2.got_ref
  29.7 1.7 %mix_last.1 = bf16[128,8192]{1,0:T(8,128)(2,1)} custom-call(f32[512,128]{1,0:T(8,128)S(1)} %get-tuple-element.24.turned_ref, bf16[128,256]{1,0:T(8,128)(2,1)S(1)} %get-tuple-element.25.mask_ref, bf16[136,1024]{1,0:T(8,128)(2,1)S(1)} %get-tuple-element.28.own_ref, ...), custom_call_target="tpu_custom_call", output_to_operand_aliasing={{}: (14, {})} | custom-call | flops 1000 | bytes 1000 | tf_op jit(solution)/shard_map/mix_last/pallas_call | solution.py:493
  (1 shorter events, 0.0 us)
Async XLA Ops:
  0.0 1.8 %copy-start = (bf16[128,8192]{1,0:T(8,128)(2,1)S(1)}, bf16[128,8192]{1,0:T(8,128)(2,1)}, u32[]{:S(2)}) copy-start(bf16[128,8192]{1,0:T(8,128)(2,1)} %q_ref.11) | copy-start | bytes 6291460
  0.0 2.2 %copy-start.1 = (bf16[128,8192]{1,0:T(8,128)(2,1)S(1)}, bf16[128,8192]{1,0:T(8,128)(2,1)}, u32[]{:S(2)}) copy-start(bf16[128,8192]{1,0:T(8,128)(2,1)} %k_ref.5) | copy-start | bytes 6291460
  0.0 2.9 %copy-start.2 = (bf16[128,8192]{1,0:T(8,128)(2,1)S(1)}, bf16[128,8192]{1,0:T(8,128)(2,1)}, u32[]{:S(2)}) copy-start(bf16[128,8192]{1,0:T(8,128)(2,1)} %v_ref.5) | copy-start | bytes 6291460
  0.0 2.9 %copy-start.3 = (f32[3,3,8192]{2,1,0:T(4,128)S(1)}, f32[3,3,8192]{2,1,0:T(4,128)}, u32[]{:S(2)}) copy-start(f32[3,3,8192]{2,1,0:T(4,128)} %taps_ref.13) | copy-start | bytes 884740
  0.2 9.0 %copy-start.5 = (bf16[512,128]{1,0:T(8,128)(2,1)S(1)}, bf16[512,128]{1,0:T(8,128)(2,1)}, u32[]{:S(2)}) copy-start(bf16[512,128]{1,0:T(8,128)(2,1)} %h_ref.1) | copy-start | bytes 393220
  0.2 14.3 %collective-permute-start = (bf16[144,2304]{1,0:T(8,128)(2,1)S(1)}, bf16[144,2304]{1,0:T(8,128)(2,1)S(1)}, u32[]{:S(2)}, u32[]{:S(2)}) collective-permute-start(bf16[144,2304]{1,0:T(8,128)(2,1)S(1)} %gate_first.1.begun_ref), channel_id=1, source_target_pairs={{1,2},{3,4},{5,6},{7,8},{9,10},{11,12},{13,14},{17,18},{19,20},{21... | collective-permute-start | bytes 1990664 | tf_op jit(solution)/shard_map/ppermute | solution.py:25
  5.4 9.1 %collective-permute-start.1 = (bf16[144,2304]{1,0:T(8,128)(2,1)S(1)}, bf16[144,2304]{1,0:T(8,128)(2,1)S(1)}, u32[]{:S(2)}, u32[]{:S(2)}) collective-permute-start(bf16[144,2304]{1,0:T(8,128)(2,1)S(1)} %get-tuple-element.26.own_ref), channel_id=1, source_target_pairs={{0,1},{2,3},{4,5},{6,7},{8,9},{10,11},{12,13},{14,15},{16,17},{18,... | collective-permute-start | bytes 1990664 | tf_op jit(solution)/shard_map/ppermute | solution.py:25
  7.3 13.1 %collective-permute-start.3 = (bf16[128,2560]{1,0:T(8,128)(2,1)S(1)}, bf16[128,2560]{1,0:T(8,128)(2,1)S(1)}, u32[]{:S(2)}, u32[]{:S(2)}) collective-permute-start(bf16[128,2560]{1,0:T(8,128)(2,1)S(1)} %get-tuple-element.23._.own_ref), channel_id=1, source_target_pairs={{0,1},{1,2},{2,3},{3,4},{4,5},{5,6},{6,7},{7,8},{8,9},{9,10},{10,1... | collective-permute-start | bytes 1966088 | tf_op jit(solution)/shard_map/ppermute | solution.py:25
  10.9 15.8 %collective-permute-start.4 = (bf16[128,2304]{1,0:T(8,128)(2,1)S(1)}, bf16[128,2304]{1,0:T(8,128)(2,1)S(1)}, u32[]{:S(2)}, u32[]{:S(2)}) collective-permute-start(bf16[128,2304]{1,0:T(8,128)(2,1)S(1)} %get-tuple-element.34.own_ref), channel_id=1, source_target_pairs={{0,1},{1,2},{2,3},{3,4},{4,5},{5,6},{6,7},{7,8},{8,9},{9,10},{10,1... | collective-permute-start | bytes 1769480 | tf_op jit(solution)/shard_map/ppermute | solution.py:25
  14.5 3.0 %copy-start.4 = (f32[8192]{0:T(1024)S(1)}, f32[8192]{0:T(1024)}, u32[]{:S(2)}) copy-start(f32[8192]{0:T(1024)} %param.11) | copy-start | bytes 98308
  15.6 14.1 %collective-permute-start.2 = (bf16[136,1024]{1,0:T(8,128)(2,1)S(1)}, bf16[136,1024]{1,0:T(8,128)(2,1)S(1)}, u32[]{:S(2)}, u32[]{:S(2)}) collective-permute-start(bf16[136,1024]{1,0:T(8,128)(2,1)S(1)} %get-tuple-element.28.own_ref), channel_id=1, source_target_pairs={{0,1},{1,2},{2,3},{3,4},{4,5},{5,6},{6,7},{7,8},{8,9},{9,10},{10,1... | collective-permute-start | bytes 835592 | tf_op jit(solution)/shard_map/ppermute | solution.py:25

commit v5 on v4

--- a/solution.py
+++ b/solution.py
@@ -12,6 +12,7 @@
 FEAT = 3
 LANES = 128
 SUB = 16
+WINDOWS = 4
 MIB = 1 << 20
 F32 = jnp.float32
 BF16 = jnp.bfloat16
@@ -48,7 +49,7 @@
     return pltpu.with_memory_space_constraint(x, pltpu.HBM)
 
 
-def run_of(tiles, most=8):
+def run_of(tiles, most=10):
     return max(n for n in range(1, most + 1) if tiles % n == 0)
 
 
@@ -207,7 +208,7 @@
         functools.partial(gate_kernel, firsts),
         in_specs=[VMEM] * 5 + [pl.BlockSpec(memory_space=pl.ANY)],
         out_specs=[VMEM] * (len(widths) + 2),
-        out_shape=[jax.ShapeDtypeStruct(h.shape, F32), jax.ShapeDtypeStruct((rows, 2 * FILT), BF16)]
+        out_shape=[jax.ShapeDtypeStruct(h.shape, F32), jax.ShapeDtypeStruct((2 * rows // WINDOWS, 2 * FILT), BF16)]
         + [jax.ShapeDtypeStruct((rows, w), BF16) for w in widths],
         compiler_params=params(12),
         cost_estimate=COST,
@@ -302,22 +303,25 @@
 
 def mix_tile(turned_ref, mask_ref, lhs_ref, own_ref, got_ref, edge_ref, q_ref, taps_ref, skip_ref, before, src, dst, c):
     rows = q_ref.shape[0]
-    half = rows // 2
+    span = rows // WINDOWS
     per = LANES // GROUP_CH
+    half = per // 2
     iota = rows_iota((SUB, LANES))
-    lane_group = lax.broadcasted_iota(jnp.int32, (8, 2 * LANES), 1) % LANES // GROUP_CH
+    lane_group = lax.broadcasted_iota(jnp.int32, (8, 2 * LANES), 1) % (LANES // 2) // GROUP_CH
     turned = turned_ref[pl.ds(pl.multiple_of(c * per, per), per), :]
     rings = []
     for g in range(per):
-        row = jnp.broadcast_to(turned[g : g + 1], (half, FILT))
+        row = jnp.broadcast_to(turned[g : g + 1], (span, FILT))
         rings.append(pltpu.roll(row, 0, 1, stride=1, stride_axis=0))
-    for r in range(half // 8):
-        mask = mask_ref[r * SUB : (r + 1) * SUB]
-        for g in range(0, per, 2):
-            pair = jnp.concatenate([rings[g][r * 8 : r * 8 + 8], rings[g + 1][r * 8 : r * 8 + 8]], axis=0)
-            pair = pair.astype(BF16)
-            low = (r * per + g) * 8
-            lhs_ref[low : low + SUB, :] = jnp.concatenate([pair, pair], axis=1) * mask
+    low = 0
+    for h in range(2):
+        for r in range(span // 8):
+            mask = mask_ref[r * SUB : (r + 1) * SUB]
+            for g in range(h * half, (h + 1) * half, 2):
+                pair = jnp.concatenate([rings[g][r * 8 : r * 8 + 8], rings[g + 1][r * 8 : r * 8 + 8]], axis=0)
+                pair = pair.astype(BF16)
+                lhs_ref[low : low + SUB, :] = jnp.concatenate([pair, pair], axis=1) * mask
+                low += SUB
     own_head = jnp.where(iota < FEAT - 1, edge_ref[:, src].astype(F32), own_ref[:SUB, dst].astype(F32))
     got_head = got_ref[:SUB, dst].astype(F32)
     q_rim = got_head
@@ -325,29 +329,38 @@
         got_head = jnp.where(iota < FEAT - 1, 0.0, got_head)
     else:
         got_head = jnp.where(iota < FEAT - 1, before, got_head)
-    cur0 = jnp.concatenate([own_head.astype(BF16), own_ref[SUB:half, dst]], axis=0)
-    cur1 = own_ref[half:rows, dst]
-    prev0 = jnp.concatenate([got_head.astype(BF16), got_ref[SUB:half, dst]], axis=0)
-    prev1 = got_ref[half:rows, dst]
-    rhs = jnp.concatenate(
-        [
-            jnp.concatenate([prev0, prev1], axis=1),
-            jnp.concatenate([prev1, cur0], axis=1),
-            jnp.concatenate([cur0, cur1], axis=1),
-            jnp.concatenate([cur1, cur1], axis=1),
-        ],
-        axis=0,
-    )
-    res = jnp.dot(lhs_ref[...], rhs, preferred_element_type=F32)
-    totals = []
-    for r in range(half // 8):
-        total = res[r * per * 8 : r * per * 8 + 8]
-        for g in range(1, per):
-            low = (r * per + g) * 8
-            total = jnp.where(lane_group == g, res[low : low + 8], total)
-        totals.append(total)
-    conv = jnp.concatenate([t[:, :LANES] for t in totals] + [t[:, LANES:] for t in totals], axis=0)
-    cur = jnp.concatenate([cur0, cur1], axis=0).astype(F32)
+    both = [got_head.astype(BF16)] + [got_ref[r : r + SUB, dst] for r in range(SUB, rows, SUB)]
+    both += [own_head.astype(BF16)] + [own_ref[r : r + SUB, dst] for r in range(SUB, rows, SUB)]
+    ahead = span // SUB
+    count = len(both) - ahead
+    sides = (slice(0, LANES // 2), slice(LANES // 2, LANES))
+    halves = [
+        [jnp.concatenate([both[i][:, side], both[i + ahead][:, side]], axis=1) for i in range(count)]
+        for side in sides
+    ]
+    res = []
+    for h, blocks in enumerate(halves):
+        cols = [
+            jnp.concatenate([blocks[min(w * ahead + i, count - 1)] for i in range(2 * FILT // SUB)], axis=0)
+            for w in range(0, WINDOWS, 2)
+        ]
+        lhs = lhs_ref[h * half * span : (h + 1) * half * span, :]
+        res.append(jnp.dot(lhs, jnp.concatenate(cols, axis=1), preferred_element_type=F32))
+    parts = [[] for _ in range(WINDOWS)]
+    for r in range(span // 8):
+        totals = []
+        for x in res:
+            total = x[r * half * 8 : r * half * 8 + 8]
+            for g in range(1, half):
+                at = (r * half + g) * 8
+                total = jnp.where(lane_group == g, x[at : at + 8], total)
+            totals.append(total)
+        for w in range(0, WINDOWS, 2):
+            a, b = (t[:, w // 2 * LANES : (w // 2 + 1) * LANES] for t in totals)
+            for i, side in enumerate(sides):
+                parts[w + i].append(jnp.concatenate([a[:, side], b[:, side]], axis=1))
+    conv = jnp.concatenate([x for part in parts for x in part], axis=0)
+    cur = jnp.concatenate(both[rows // SUB :], axis=0).astype(F32)
     q = q_ref[:, src].astype(F32)
     taps = taps_ref[0, :, src]
     q_feat = taps[0:1] * q
@@ -419,7 +432,7 @@
         ],
         scratch_shapes=[
             pltpu.VMEM((rows - SUB, width), BF16),
-            pltpu.VMEM((run, per * rows // 2, 2 * FILT), BF16),
+            pltpu.VMEM((run, per * rows // WINDOWS, 2 * FILT), BF16),
             pltpu.SemaphoreType.DMA((width // LANES // run,)),
         ],
         input_output_aliases={} if out is None else {len(args) - 1: 0},
@@ -499,7 +512,7 @@
             pltpu.VMEM((rows, width), BF16),
             pltpu.VMEM((SUB, first), BF16),
             pltpu.VMEM((1, full), F32),
-            pltpu.VMEM((run, per * rows // 2, 2 * FILT), BF16),
+            pltpu.VMEM((run, per * rows // WINDOWS, 2 * FILT), BF16),
             pltpu.SemaphoreType.DMA((width // LANES // run,)),
             pltpu.SemaphoreType.DMA,
         ],

time: 31.6 us -> 31.5 us (level)
  Pallas kernels: 15.6 us -> 14.2 us
  waiting for transfers between devices: 3.68 us -> 5.01 us
    ppermute x5, waiting for transfers between devices: 3.68 us -> 5.01 us  [passed_along(): lax.ppermute(shard, 'seq', [(i, i + 1) for i in range(first, length - 1,...]
    pallas_call x3, Pallas kernels: 8.46 us -> 7.14 us  [mix(): pl.pallas_call(functools.partial(mix_kernel, first, out is not None), in_...]
  transfers between devices with their start and end apart: 5 -> 5, of which waited for: 3 -> 3; matrix products, arithmetic and copies ran while one was open for 0% -> 0% of each run, Pallas kernels for 44% -> 40%
where the time goes in v5:
time: 31.5 us; the launch traced here: 31.3 us
  Pallas kernels  14.2 us (45%)
  starting transfers between devices  10.8 us (34%)
  waiting for transfers between devices  5.01 us (16%)
  local copies, waits for them, and re-layouts  1.11 us (4%)
    ppermute x5, starting transfers between devices, passed_along(): lax.ppermute(shard, 'seq', [(i, i + 1) for i in range(first, length - 1,...  10.8 us
    pallas_call x3, Pallas kernels, mix(): pl.pallas_call(functools.partial(mix_kernel, first, out is not None), in_...  7.14 us
    ppermute x5, waiting for transfers between devices, passed_along(): lax.ppermute(shard, 'seq', [(i, i + 1) for i in range(first, length - 1,...  5.01 us
    pallas_call x1, Pallas kernels, second_gate(): pl.pallas_call(functools.partial(second_gate_kernel, first), in_specs=[VM...  2.52 us
    pallas_call x1, Pallas kernels, gate(): pl.pallas_call(functools.partial(gate_kernel, firsts), in_specs=[VMEM] *...  1.7 us
    pallas_call x1, Pallas kernels, last_mix(): pl.pallas_call(functools.partial(last_mix_kernel, first, len(heads)), in_...  1.62 us
    unnamed x12, local copies, waits for them, and re-layouts  1.11 us
    pallas_call x1, Pallas kernels, last_gate(): pl.pallas_call(last_gate_kernel, in_specs=[VMEM] * 6, out_specs=[VMEM] *...  1.02 us
  transfers between devices with their start and end apart: 5, of which 3 were waited for; matrix products, arithmetic and copies ran while one was open for 0% of the time, Pallas kernels for 40%

profile of v5, /device:TPU:16, one launch (start us, length us, event | category | flops | bytes accessed | tf_op | source)
XLA Modules:
  0.0 31.3 jit_solution(7081766057635354331)
XLA Ops:
  0.0 0.0 copy-start
  0.0 0.0 copy-start.1
  0.0 0.0 copy-start.2
  0.0 0.0 copy-start.3
  0.0 0.2 gate_first.1.begun_ref
  0.2 0.0 copy-start.5
  0.2 1.6 %collective-permute-start = (bf16[144,2304]{1,0:T(8,128)(2,1)S(1)}, bf16[144,2304]{1,0:T(8,128)(2,1)S(1)}, u32[]{:S(2)}, u32[]{:S(2)}) collective-permute-start(bf16[144,2304]{1,0:T(8,128)(2,1)S(1)} %gate_first.1.begun_ref), channel_id=1, source_target_pairs={{1,2},{3,4},{5,6},{7,8},{9,10},{11,12},{13,14},{17,18},{19,20},{21... | collective-permute-start | bytes 1990664 | tf_op jit(solution)/shard_map/ppermute | solution.py:26
  1.8 0.0 copy-done
  1.8 0.5 %copy-done.1 = bf16[128,8192]{1,0:T(8,128)(2,1)S(1)} copy-done((bf16[128,8192]{1,0:T(8,128)(2,1)S(1)}, bf16[128,8192]{1,0:T(8,128)(2,1)}, u32[]{:S(2)}) %copy-start.1) | copy-done | bytes 2097176
  2.2 0.6 %copy-done.2 = bf16[128,8192]{1,0:T(8,128)(2,1)S(1)} copy-done((bf16[128,8192]{1,0:T(8,128)(2,1)S(1)}, bf16[128,8192]{1,0:T(8,128)(2,1)}, u32[]{:S(2)}) %copy-start.2) | copy-done | bytes 2097176
  2.9 0.0 copy-done.3
  2.9 2.5 %gate_second.1 = (bf16[144,2304]{1,0:T(8,128)(2,1)S(1)}, bf16[128,2560]{1,0:T(8,128)(2,1)S(1)}) custom-call(bf16[128,8192]{1,0:T(8,128)(2,1)S(1)} %copy-done.1, bf16[128,8192]{1,0:T(8,128)(2,1)S(1)} %copy-done.2, bf16[128,8192]{1,0:T(8,128)(2,1)S(1)} %copy-done, f32[3,3,8192]{2,1,0:T(4,128)S(1)} %copy-done.3, bf16[144,2304]{1,0:T(8,128)(2,1)S(1)} %gate_first.1.begun_ref), custom_call_target="tpu_custom_call" | custom-call | flops 1000 | bytes 1000 | tf_op jit(solution)/shard_map/gate_second/pallas_call | solution.py:184
  5.4 1.9 %collective-permute-start.1 = (bf16[144,2304]{1,0:T(8,128)(2,1)S(1)}, bf16[144,2304]{1,0:T(8,128)(2,1)S(1)}, u32[]{:S(2)}, u32[]{:S(2)}) collective-permute-start(bf16[144,2304]{1,0:T(8,128)(2,1)S(1)} %get-tuple-element.26.own_ref), channel_id=1, source_target_pairs={{0,1},{2,3},{4,5},{6,7},{8,9},{10,11},{12,13},{14,15},{16,17},{18,... | collective-permute-start | bytes 1990664 | tf_op jit(solution)/shard_map/ppermute | solution.py:26
  7.3 1.9 %collective-permute-start.3 = (bf16[128,2560]{1,0:T(8,128)(2,1)S(1)}, bf16[128,2560]{1,0:T(8,128)(2,1)S(1)}, u32[]{:S(2)}, u32[]{:S(2)}) collective-permute-start(bf16[128,2560]{1,0:T(8,128)(2,1)S(1)} %get-tuple-element.23._.own_ref), channel_id=1, source_target_pairs={{0,1},{1,2},{2,3},{3,4},{4,5},{5,6},{6,7},{7,8},{8,9},{9,10},{10,1... | collective-permute-start | bytes 1966088 | tf_op jit(solution)/shard_map/ppermute | solution.py:26
  9.2 0.0 copy-done.5
  9.2 1.7 %gate.1 = (f32[512,128]{1,0:T(8,128)S(1)}, bf16[64,256]{1,0:T(8,128)(2,1)S(1)}, bf16[128,2304]{1,0:T(8,128)(2,1)S(1)}, bf16[128,1024]{1,0:T(8,128)(2,1)S(1)}) custom-call(bf16[128,8192]{1,0:T(8,128)(2,1)S(1)} %copy-done.1, bf16[128,8192]{1,0:T(8,128)(2,1)S(1)} %copy-done.2, bf16[128,8192]{1,0:T(8,128)(2,1)S(1)} %copy-done, f32[3,3,8192]{2,1,0:T(4,128)S(1)} %copy-done.3, ...), custom_call_target="tpu_custom_call" | custom-call | flops 1000 | bytes 1000 | tf_op jit(solution)/shard_map/gate/pallas_call | solution.py:207
  10.9 3.5 %collective-permute-start.4 = (bf16[128,2304]{1,0:T(8,128)(2,1)S(1)}, bf16[128,2304]{1,0:T(8,128)(2,1)S(1)}, u32[]{:S(2)}, u32[]{:S(2)}) collective-permute-start(bf16[128,2304]{1,0:T(8,128)(2,1)S(1)} %get-tuple-element.34.own_ref), channel_id=1, source_target_pairs={{0,1},{1,2},{2,3},{3,4},{4,5},{5,6},{6,7},{7,8},{8,9},{9,10},{10,1... | collective-permute-start | bytes 1769480 | tf_op jit(solution)/shard_map/ppermute | solution.py:26
  14.5 0.0 collective-permute-done.in_ref
  14.5 0.0 collective-permute-done.1.near_ref
  14.5 0.0 copy-start.4
  14.5 1.0 %gate_last.1 = (bf16[136,1024]{1,0:T(8,128)(2,1)S(1)}, bf16[16,8192]{1,0:T(8,128)(2,1)S(1)}, bf16[144,2304]{1,0:T(8,128)(2,1)S(1)}) custom-call(bf16[128,8192]{1,0:T(8,128)(2,1)S(1)} %copy-done.1, bf16[128,8192]{1,0:T(8,128)(2,1)S(1)} %copy-done.2, f32[3,3,8192]{2,1,0:T(4,128)S(1)} %copy-done.3, bf16[144,2304]{1,0:T(8,128)(2,1)S(1)} %settle.1.crossed_ref, ...), custom_call_target="tpu_custom_call" | custom-call | flops 1000 | bytes 1000 | tf_op jit(solution)/shard_map/gate_last/pallas_call | solution.py:274
  15.6 1.9 %collective-permute-start.2 = (bf16[136,1024]{1,0:T(8,128)(2,1)S(1)}, bf16[136,1024]{1,0:T(8,128)(2,1)S(1)}, u32[]{:S(2)}, u32[]{:S(2)}) collective-permute-start(bf16[136,1024]{1,0:T(8,128)(2,1)S(1)} %get-tuple-element.28.own_ref), channel_id=1, source_target_pairs={{0,1},{1,2},{2,3},{3,4},{4,5},{5,6},{6,7},{7,8},{8,9},{9,10},{10,1... | collective-permute-start | bytes 835592 | tf_op jit(solution)/shard_map/ppermute | solution.py:26
  17.5 0.0 copy-done.4
  17.5 2.3 %mix.3 = (bf16[128,8192]{1,0:T(8,128)(2,1)}, f32[16,2304]{1,0:T(8,128)S(1)}, f32[8,2304]{1,0:T(8,128)S(1)}) custom-call(f32[512,128]{1,0:T(8,128)S(1)} %get-tuple-element.24.turned_ref, bf16[64,256]{1,0:T(8,128)(2,1)S(1)} %get-tuple-element.25.mask_ref, bf16[144,2304]{1,0:T(8,128)(2,1)S(1)} %get-tuple-element.26.own_ref, ...), custom_call_target="tpu_custom_call" | custom-call | flops 1000 | bytes 1000 | tf_op jit(solution)/shard_map/mix/pallas_call | solution.py:424
  19.9 0.5 %collective-permute-done.3.got_ref = bf16[128,2560]{1,0:T(8,128)(2,1)S(1)} collective-permute-done((bf16[128,2560]{1,0:T(8,128)(2,1)S(1)}, bf16[128,2560]{1,0:T(8,128)(2,1)S(1)}, u32[]{:S(2)}, u32[]{:S(2)}) %collective-permute-start.3) | collective-permute-done | bytes 655392 | tf_op jit(solution)/shard_map/ppermute | solution.py:26
  20.4 2.5 %mix.4 = (bf16[128,8192]{1,0:T(8,128)(2,1)}, f32[16,2560]{1,0:T(8,128)S(1)}, f32[8,2560]{1,0:T(8,128)S(1)}) custom-call(f32[512,128]{1,0:T(8,128)S(1)} %get-tuple-element.24.turned_ref, bf16[64,256]{1,0:T(8,128)(2,1)S(1)} %get-tuple-element.25.mask_ref, bf16[128,2560]{1,0:T(8,128)(2,1)S(1)} %get-tuple-element.23._.own_ref, ...), custom_call_target="tpu_custom_call", output_to_operand_aliasing={{0}: (8, {})} | custom-call | flops 1000 | bytes 1000 | tf_op jit(solution)/shard_map/mix/pallas_call | solution.py:424
  22.9 3.8 %collective-permute-done.4.got_ref = bf16[128,2304]{1,0:T(8,128)(2,1)S(1)} collective-permute-done((bf16[128,2304]{1,0:T(8,128)(2,1)S(1)}, bf16[128,2304]{1,0:T(8,128)(2,1)S(1)}, u32[]{:S(2)}, u32[]{:S(2)}) %collective-permute-start.4) | collective-permute-done | bytes 589856 | tf_op jit(solution)/shard_map/ppermute | solution.py:26
  26.7 2.3 %mix.5 = (bf16[128,8192]{1,0:T(8,128)(2,1)}, f32[16,2304]{1,0:T(8,128)S(1)}, f32[8,2304]{1,0:T(8,128)S(1)}) custom-call(f32[512,128]{1,0:T(8,128)S(1)} %get-tuple-element.24.turned_ref, bf16[64,256]{1,0:T(8,128)(2,1)S(1)} %get-tuple-element.25.mask_ref, bf16[128,2304]{1,0:T(8,128)(2,1)S(1)} %get-tuple-element.34.own_ref, ...), custom_call_target="tpu_custom_call", output_to_operand_aliasing={{0}: (8, {})} | custom-call | flops 1000 | bytes 1000 | tf_op jit(solution)/shard_map/mix/pallas_call | solution.py:424
  29.0 0.6 %collective-permute-done.2.got_ref = bf16[136,1024]{1,0:T(8,128)(2,1)S(1)} collective-permute-done((bf16[136,1024]{1,0:T(8,128)(2,1)S(1)}, bf16[136,1024]{1,0:T(8,128)(2,1)S(1)}, u32[]{:S(2)}, u32[]{:S(2)}) %collective-permute-start.2) | collective-permute-done | bytes 278560 | tf_op jit(solution)/shard_map/ppermute | solution.py:26
  29.7 1.6 %mix_last.1 = bf16[128,8192]{1,0:T(8,128)(2,1)} custom-call(f32[512,128]{1,0:T(8,128)S(1)} %get-tuple-element.24.turned_ref, bf16[64,256]{1,0:T(8,128)(2,1)S(1)} %get-tuple-element.25.mask_ref, bf16[136,1024]{1,0:T(8,128)(2,1)S(1)} %get-tuple-element.28.own_ref, ...), custom_call_target="tpu_custom_call", output_to_operand_aliasing={{}: (14, {})} | custom-call | flops 1000 | bytes 1000 | tf_op jit(solution)/shard_map/mix_last/pallas_call | solution.py:506
  (1 shorter events, 0.0 us)
Async XLA Ops:
  0.0 1.8 %copy-start = (bf16[128,8192]{1,0:T(8,128)(2,1)S(1)}, bf16[128,8192]{1,0:T(8,128)(2,1)}, u32[]{:S(2)}) copy-start(bf16[128,8192]{1,0:T(8,128)(2,1)} %q_ref.11) | copy-start | bytes 6291460
  0.0 2.2 %copy-start.1 = (bf16[128,8192]{1,0:T(8,128)(2,1)S(1)}, bf16[128,8192]{1,0:T(8,128)(2,1)}, u32[]{:S(2)}) copy-start(bf16[128,8192]{1,0:T(8,128)(2,1)} %k_ref.5) | copy-start | bytes 6291460
  0.0 2.9 %copy-start.2 = (bf16[128,8192]{1,0:T(8,128)(2,1)S(1)}, bf16[128,8192]{1,0:T(8,128)(2,1)}, u32[]{:S(2)}) copy-start(bf16[128,8192]{1,0:T(8,128)(2,1)} %v_ref.5) | copy-start | bytes 6291460
  0.0 2.9 %copy-start.3 = (f32[3,3,8192]{2,1,0:T(4,128)S(1)}, f32[3,3,8192]{2,1,0:T(4,128)}, u32[]{:S(2)}) copy-start(f32[3,3,8192]{2,1,0:T(4,128)} %taps_ref.13) | copy-start | bytes 884740
  0.2 9.0 %copy-start.5 = (bf16[512,128]{1,0:T(8,128)(2,1)S(1)}, bf16[512,128]{1,0:T(8,128)(2,1)}, u32[]{:S(2)}) copy-start(bf16[512,128]{1,0:T(8,128)(2,1)} %h_ref.1) | copy-start | bytes 393220
  0.2 14.3 %collective-permute-start = (bf16[144,2304]{1,0:T(8,128)(2,1)S(1)}, bf16[144,2304]{1,0:T(8,128)(2,1)S(1)}, u32[]{:S(2)}, u32[]{:S(2)}) collective-permute-start(bf16[144,2304]{1,0:T(8,128)(2,1)S(1)} %gate_first.1.begun_ref), channel_id=1, source_target_pairs={{1,2},{3,4},{5,6},{7,8},{9,10},{11,12},{13,14},{17,18},{19,20},{21... | collective-permute-start | bytes 1990664 | tf_op jit(solution)/shard_map/ppermute | solution.py:26
  5.4 9.1 %collective-permute-start.1 = (bf16[144,2304]{1,0:T(8,128)(2,1)S(1)}, bf16[144,2304]{1,0:T(8,128)(2,1)S(1)}, u32[]{:S(2)}, u32[]{:S(2)}) collective-permute-start(bf16[144,2304]{1,0:T(8,128)(2,1)S(1)} %get-tuple-element.26.own_ref), channel_id=1, source_target_pairs={{0,1},{2,3},{4,5},{6,7},{8,9},{10,11},{12,13},{14,15},{16,17},{18,... | collective-permute-start | bytes 1990664 | tf_op jit(solution)/shard_map/ppermute | solution.py:26
  7.3 13.1 %collective-permute-start.3 = (bf16[128,2560]{1,0:T(8,128)(2,1)S(1)}, bf16[128,2560]{1,0:T(8,128)(2,1)S(1)}, u32[]{:S(2)}, u32[]{:S(2)}) collective-permute-start(bf16[128,2560]{1,0:T(8,128)(2,1)S(1)} %get-tuple-element.23._.own_ref), channel_id=1, source_target_pairs={{0,1},{1,2},{2,3},{3,4},{4,5},{5,6},{6,7},{7,8},{8,9},{9,10},{10,1... | collective-permute-start | bytes 1966088 | tf_op jit(solution)/shard_map/ppermute | solution.py:26
  10.9 15.8 %collective-permute-start.4 = (bf16[128,2304]{1,0:T(8,128)(2,1)S(1)}, bf16[128,2304]{1,0:T(8,128)(2,1)S(1)}, u32[]{:S(2)}, u32[]{:S(2)}) collective-permute-start(bf16[128,2304]{1,0:T(8,128)(2,1)S(1)} %get-tuple-element.34.own_ref), channel_id=1, source_target_pairs={{0,1},{1,2},{2,3},{3,4},{4,5},{5,6},{6,7},{7,8},{8,9},{9,10},{10,1... | collective-permute-start | bytes 1769480 | tf_op jit(solution)/shard_map/ppermute | solution.py:26
  14.5 3.0 %copy-start.4 = (f32[8192]{0:T(1024)S(1)}, f32[8192]{0:T(1024)}, u32[]{:S(2)}) copy-start(f32[8192]{0:T(1024)} %param.11) | copy-start | bytes 98308
  15.6 14.1 %collective-permute-start.2 = (bf16[136,1024]{1,0:T(8,128)(2,1)S(1)}, bf16[136,1024]{1,0:T(8,128)(2,1)S(1)}, u32[]{:S(2)}, u32[]{:S(2)}) collective-permute-start(bf16[136,1024]{1,0:T(8,128)(2,1)S(1)} %get-tuple-element.28.own_ref), channel_id=1, source_target_pairs={{0,1},{1,2},{2,3},{3,4},{4,5},{5,6},{6,7},{7,8},{8,9},{9,10},{10,1... | collective-permute-start | bytes 835592 | tf_op jit(solution)/shard_map/ppermute | solution.py:26

commit v6 on v5

--- a/solution.py
+++ b/solution.py
@@ -301,14 +301,10 @@
     mask_ref[...] = jnp.where((m > b) & (m <= b + FILT), 1.0, 0.0).astype(BF16)
 
 
-def mix_tile(turned_ref, mask_ref, lhs_ref, own_ref, got_ref, edge_ref, q_ref, taps_ref, skip_ref, before, src, dst, c):
-    rows = q_ref.shape[0]
-    span = rows // WINDOWS
+def toeplitz_rows(turned, mask_ref, lhs_ref):
+    span = mask_ref.shape[0] // 2
     per = LANES // GROUP_CH
     half = per // 2
-    iota = rows_iota((SUB, LANES))
-    lane_group = lax.broadcasted_iota(jnp.int32, (8, 2 * LANES), 1) % (LANES // 2) // GROUP_CH
-    turned = turned_ref[pl.ds(pl.multiple_of(c * per, per), per), :]
     rings = []
     for g in range(per):
         row = jnp.broadcast_to(turned[g : g + 1], (span, FILT))
@@ -322,6 +318,67 @@
                 pair = pair.astype(BF16)
                 lhs_ref[low : low + SUB, :] = jnp.concatenate([pair, pair], axis=1) * mask
                 low += SUB
+
+
+def own_feature(q, taps):
+    iota = rows_iota((SUB, LANES))
+    total = taps[0:1] * q
+    for d in range(1, FEAT):
+        moved = pltpu.roll(q, d, 0)
+        head = jnp.where(iota < d, 0.0, moved[:SUB])
+        total = total + taps[d : d + 1] * jnp.concatenate([head, moved[SUB:]], axis=0)
+    return total
+
+
+def prepare_kernel(firsts, turned_ref, mask_ref, q_ref, taps_ref, *out_refs):
+    per = LANES // GROUP_CH
+    for i, first in enumerate(firsts):
+        lhs_ref, feat_ref = out_refs[2 * i : 2 * i + 2]
+        tiles = lhs_ref.shape[0]
+
+        @pl.loop(0, tiles, unroll=run_of(tiles, 4))
+        def _(c):
+            c_all = c + first // LANES
+            src = lanes_at(c_all)
+            toeplitz_rows(turned_ref[pl.ds(pl.multiple_of(c_all * per, per), per), :], mask_ref, lhs_ref.at[c])
+            feat_ref[:, lanes_at(c)] = own_feature(q_ref[:, src].astype(F32), taps_ref[0, :, src])
+
+
+def prepare(turned, mask, q, taps, firsts, widths):
+    rows = q.shape[0]
+    lhs = LANES // GROUP_CH * rows // WINDOWS
+    return pl.pallas_call(
+        functools.partial(prepare_kernel, firsts),
+        in_specs=[VMEM] * 4,
+        out_specs=[VMEM] * (2 * len(widths)),
+        out_shape=[
+            shape
+            for w in widths
+            for shape in (
+                jax.ShapeDtypeStruct((w // LANES, lhs, 2 * FILT), BF16),
+                jax.ShapeDtypeStruct((rows, w), F32),
+            )
+        ],
+        compiler_params=params(12),
+        cost_estimate=COST,
+        name="prepare",
+    )(turned, mask, q, taps)
+
+
+def mix_tile(turned_ref, mask_ref, lhs_ref, feat_ref, own_ref, got_ref, edge_ref, q_ref, taps_ref, skip_ref, before, src, dst, c):
+    rows = q_ref.shape[0]
+    span = rows // WINDOWS
+    per = LANES // GROUP_CH
+    half = per // 2
+    iota = rows_iota((SUB, LANES))
+    lane_group = lax.broadcasted_iota(jnp.int32, (8, 2 * LANES), 1) % (LANES // 2) // GROUP_CH
+    turned = turned_ref[pl.ds(c * per if isinstance(c, int) else pl.multiple_of(c * per, per), per), :]
+    taps = taps_ref[0, :, src]
+    if feat_ref is None:
+        toeplitz_rows(turned, mask_ref, lhs_ref)
+        q_feat = own_feature(q_ref[:, src].astype(F32), taps)
+    else:
+        q_feat = feat_ref[:, dst]
     own_head = jnp.where(iota < FEAT - 1, edge_ref[:, src].astype(F32), own_ref[:SUB, dst].astype(F32))
     got_head = got_ref[:SUB, dst].astype(F32)
     q_rim = got_head
@@ -361,20 +418,21 @@
                 parts[w + i].append(jnp.concatenate([a[:, side], b[:, side]], axis=1))
     conv = jnp.concatenate([x for part in parts for x in part], axis=0)
     cur = jnp.concatenate(both[rows // SUB :], axis=0).astype(F32)
-    q = q_ref[:, src].astype(F32)
-    taps = taps_ref[0, :, src]
-    q_feat = taps[0:1] * q
+    head = q_feat[:SUB]
     for d in range(1, FEAT):
-        moved = pltpu.roll(q, d, 0)
         shifted = pltpu.roll(q_rim, (d - (FEAT - 1)) % SUB, 0)
-        head = jnp.where(iota < d, shifted, moved[:SUB])
-        q_feat = q_feat + taps[d : d + 1] * jnp.concatenate([head, moved[SUB:]], axis=0)
+        head = head + taps[d : d + 1] * jnp.where(iota < d, shifted, 0.0)
+    q_feat = jnp.concatenate([head, q_feat[SUB:]], axis=0)
     return q_feat * (conv + skip_ref[:, src] * cur), q_feat, turned
 
 
-def mix_kernel(first, has_out, turned_ref, mask_ref, own_ref, got_ref, edge_ref, q_ref, taps_ref, skip_ref, *refs):
-    refs = refs[1:] if has_out else refs
-    out_hbm, head_ref, slope_ref, res_ref, lhs_ref, sems = refs
+def mix_kernel(first, has_out, has_ready, has_after, turned_ref, mask_ref, own_ref, got_ref, edge_ref, q_ref, taps_ref, skip_ref, *refs):
+    refs = refs[has_out + has_after :]
+    feat_ref = None
+    if has_ready:
+        lhs_ref, feat_ref, *refs = refs
+    out_hbm, head_ref, slope_ref, res_ref, *lhs, sems = refs
+    lhs_ref = lhs_ref if has_ready else lhs[0]
     rows = q_ref.shape[0]
     width = res_ref.shape[1]
     per = LANES // GROUP_CH
@@ -398,12 +456,26 @@
             dst = lanes_at(c)
             src = lanes_at(c + first // LANES)
             mixed, q_feat, turned = mix_tile(
-                turned_ref, mask_ref, lhs_ref.at[u], own_ref, got_ref, edge_ref, q_ref, taps_ref, skip_ref, None, src, dst, c + first // LANES
+                turned_ref,
+                mask_ref,
+                lhs_ref.at[c if has_ready else u],
+                feat_ref,
+                own_ref,
+                got_ref,
+                edge_ref,
+                q_ref,
+                taps_ref,
+                skip_ref,
+                None,
+                src,
+                dst,
+                c + first // LANES,
             )
             res_ref[:, dst] = mixed[SUB:].astype(BF16)
             head_ref[:, dst] = mixed[:SUB]
             last_tap = jnp.where(row_group == lane_group, jnp.broadcast_to(turned[:, 1:2], (per, LANES)), 0.0)
-            slope_ref[:, dst] = q_feat[:8] * jnp.sum(last_tap, axis=0, keepdims=True)
+            slope = q_feat[:8] * jnp.sum(last_tap, axis=0, keepdims=True)
+            slope_ref[:, dst] = jnp.where(rows_iota((8, LANES)) == 0, slope, 0.0)
         store(p).start()
 
     @pl.loop(0, runs)
@@ -411,18 +483,26 @@
         store(p).wait()
 
 
-def mix(turned, mask, own, got, edges, q, taps, skip, out, first):
+def mix(turned, mask, own, got, edges, q, taps, skip, out, first, ready=(), after=None):
     rows, full = q.shape
     width = own.shape[1]
     run = run_of(width // LANES)
     per = LANES // GROUP_CH
     args = [turned, mask, own, got, edges, q, taps, skip]
     in_specs = [VMEM] * len(args)
+    aliases = {}
     if out is not None:
+        aliases = {len(args): 0}
         in_specs.append(HBM)
         args.append(out)
-    return pl.pallas_call(
-        functools.partial(mix_kernel, first, out is not None),
+    if after is not None:
+        in_specs.append(pl.BlockSpec(memory_space=pl.ANY))
+        args.append(after)
+    in_specs += [VMEM] * len(ready)
+    args += ready
+    scratch = [] if ready else [pltpu.VMEM((run, per * rows // WINDOWS, 2 * FILT), BF16)]
+    return pl.pallas_call(
+        functools.partial(mix_kernel, first, out is not None, len(ready) > 0, after is not None),
         in_specs=in_specs,
         out_specs=[HBM, VMEM, VMEM],
         out_shape=[
@@ -432,10 +512,10 @@
         ],
         scratch_shapes=[
             pltpu.VMEM((rows - SUB, width), BF16),
-            pltpu.VMEM((run, per * rows // WINDOWS, 2 * FILT), BF16),
+            *scratch,
             pltpu.SemaphoreType.DMA((width // LANES // run,)),
         ],
-        input_output_aliases={} if out is None else {len(args) - 1: 0},
+        input_output_aliases=aliases,
         compiler_params=params(12),
         cost_estimate=COST,
         name="mix",
@@ -444,65 +524,54 @@
 
 def last_mix_kernel(first, parts, turned_ref, mask_ref, own_ref, got_ref, edge_ref, q_ref, taps_ref, skip_ref, *refs):
     heads, slopes = refs[:parts], refs[parts : 2 * parts]
-    _, out_hbm, res_ref, top_ref, before_ref, lhs_ref, sems, top_sem = refs[2 * parts :]
-    rows, full = q_ref.shape
-    width = res_ref.shape[1]
-    iota = rows_iota((SUB, LANES))
-
-    for b in range(pl.cdiv(full, width)):
-        count = min(width, full - b * width)
-        before_ref[:, b * width : b * width + count] = got_ref[rows:, :count].astype(F32)[b : b + 1]
-
-    at_first = 0
+    lhs_ref, feat_ref, _, out_hbm, res_ref, top_ref, sems = refs[2 * parts :]
+    rows = q_ref.shape[0]
+    tiles = res_ref.shape[1] // LANES
+    mine = first // LANES
+    before = [got_ref[rows:, lanes_at(c)].astype(F32) for c in range(tiles)]
+
+    def before_at(c_all):
+        return before[c_all % tiles][c_all // tiles : c_all // tiles + 1]
+
+    c_all = 0
     for head_ref, slope_ref in zip(heads, slopes):
-        wide = head_ref.shape[1]
-
-        @pl.loop(0, wide // LANES, unroll=run_of(wide // LANES))
-        def _(c):
-            c_all = c + at_first // LANES
-            head = head_ref[:, lanes_at(c)]
-            more = slope_ref[:, lanes_at(c)] * before_ref[:, lanes_at(c_all)]
-            more = jnp.concatenate([more, jnp.zeros_like(more)], axis=0)
-            top_ref[:, lanes_at(c_all)] = jnp.where(iota == 0, head + more, head).astype(BF16)
-
-        at_first += wide
-    top = pltpu.make_async_copy(top_ref, out_hbm.at[pl.ds(0, SUB), pl.ds(0, first)], top_sem)
+        for c in range(head_ref.shape[1] // LANES):
+            at = lanes_at(c)
+            head = head_ref[:, at]
+            changed = head[:8] + slope_ref[:, at] * before_at(c_all)
+            top_ref[:, lanes_at(c_all)] = jnp.concatenate([changed, head[8:]], axis=0).astype(BF16)
+            c_all += 1
+    top = pltpu.make_async_copy(top_ref, out_hbm.at[pl.ds(0, SUB), pl.ds(0, first)], sems.at[0])
     top.start()
-
-    run = run_of(width // LANES)
-    runs = width // LANES // run
-
-    def store(p):
-        here = pl.ds(pl.multiple_of(p * run * LANES, LANES), run * LANES)
-        there = pl.ds(pl.multiple_of(first + p * run * LANES, LANES), run * LANES)
-        return pltpu.make_async_copy(res_ref.at[:, here], out_hbm.at[:, there], sems.at[p])
-
-    @pl.loop(0, runs)
-    def _(p):
-        for u in range(run):
-            c = p * run + u
-            dst = lanes_at(c)
-            src = lanes_at(c + first // LANES)
-            before = before_ref[:, src]
-            mixed, _, _ = mix_tile(
-                turned_ref, mask_ref, lhs_ref.at[u], own_ref, got_ref, edge_ref, q_ref, taps_ref, skip_ref, before, src, dst, c + first // LANES
-            )
-            res_ref[:, dst] = mixed.astype(BF16)
-        store(p).start()
-
-    @pl.loop(0, runs)
-    def _(p):
-        store(p).wait()
-
+    for c in range(tiles):
+        dst = lanes_at(c)
+        mixed, _, _ = mix_tile(
+            turned_ref,
+            mask_ref,
+            lhs_ref.at[c],
+            feat_ref,
+            own_ref,
+            got_ref,
+            edge_ref,
+            q_ref,
+            taps_ref,
+            skip_ref,
+            before_at(c + mine),
+            lanes_at(c + mine),
+            dst,
+            c + mine,
+        )
+        res_ref[:, dst] = mixed.astype(BF16)
+    copy = pltpu.make_async_copy(res_ref, out_hbm.at[:, pl.ds(first, tiles * LANES)], sems.at[1])
+    copy.start()
     top.wait()
-
-
-def last_mix(turned, mask, own, got, edges, q, taps, skip, heads, slopes, out, first):
+    copy.wait()
+
+
+def last_mix(turned, mask, own, got, edges, q, taps, skip, heads, slopes, ready, out, first):
     rows, full = q.shape
     width = own.shape[1]
-    run = run_of(width // LANES)
-    per = LANES // GROUP_CH
-    args = [turned, mask, own, got, edges, q, taps, skip, *heads, *slopes, out]
+    args = [turned, mask, own, got, edges, q, taps, skip, *heads, *slopes, *ready, out]
     return pl.pallas_call(
         functools.partial(last_mix_kernel, first, len(heads)),
         in_specs=[VMEM] * (len(args) - 1) + [HBM],
@@ -511,10 +580,7 @@
         scratch_shapes=[
             pltpu.VMEM((rows, width), BF16),
             pltpu.VMEM((SUB, first), BF16),
-            pltpu.VMEM((1, full), F32),
-            pltpu.VMEM((run, per * rows // WINDOWS, 2 * FILT), BF16),
-            pltpu.SemaphoreType.DMA((width // LANES // run,)),
-            pltpu.SemaphoreType.DMA,
+            pltpu.SemaphoreType.DMA((2,)),
         ],
         input_output_aliases={len(args) - 1: 0},
         compiler_params=params(12),
@@ -541,16 +607,17 @@
     last, edges, got[0] = last_gate(k_stream, v_stream, feat_filter, settle(crossed), near, last)
     own.append(last)
     got.append(passed_along(last))
+    ready = prepare(turned, mask, q_stream, feat_filter, starts[2:], sizes[2:])
+    rest = (edges, q_stream, feat_filter, skip)
     out = None
     heads = []
     slopes = []
-    for first, a, b in zip(starts[:3], own, got):
-        out, head, slope = mix(turned, mask, a, b, edges, q_stream, feat_filter, skip, out, first)
+    more = ({}, {"after": ready[3]}, {"ready": ready[:2]})
+    for first, a, b, m in zip(starts[:3], own, got, more):
+        out, head, slope = mix(turned, mask, a, b, *rest, out, first, **m)
         heads.append(head)
         slopes.append(slope)
-    return last_mix(
-        turned, mask, own[3], got[3], edges, q_stream, feat_filter, skip, heads, slopes, out, starts[3]
-    )
+    return last_mix(turned, mask, own[3], got[3], *rest, heads, slopes, ready[2:], out, starts[3])
 
 
 def solution(mesh):

time: 31.5 us -> 31.3 us (level)
  waiting for transfers between devices: 5.01 us -> 3.77 us
  Pallas kernels: 14.2 us -> 15.2 us
    ppermute x5, waiting for transfers between devices: 5.01 us -> 3.77 us  [passed_along(): lax.ppermute(shard, 'seq', [(i, i + 1) for i in range(first, length - 1,...]
    pallas_call x3 -> x4, Pallas kernels: 7.14 us -> 8.36 us  [the longest x3 6.91 us: mix(): pl.pallas_call(functools.partial(mix_kernel, first, out is not None, len(...]
  transfers between devices with their start and end apart: 5 -> 5, of which waited for: 3 -> 2; matrix products, arithmetic and copies ran while one was open for 0% -> 0% of each run, Pallas kernels for 40% -> 44%
where the time goes in v6:
time: 31.3 us; the launch traced here: 31 us
  Pallas kernels  15.2 us (49%)
  starting transfers between devices  10.8 us (35%)
  waiting for transfers between devices  3.77 us (12%)
  local copies, waits for them, and re-layouts  1.11 us (4%)
    ppermute x5, starting transfers between devices, passed_along(): lax.ppermute(shard, 'seq', [(i, i + 1) for i in range(first, length - 1,...  10.8 us
    pallas_call x3, Pallas kernels, mix(): pl.pallas_call(functools.partial(mix_kernel, first, out is not None, len(...  6.91 us
    ppermute x5, waiting for transfers between devices, passed_along(): lax.ppermute(shard, 'seq', [(i, i + 1) for i in range(first, length - 1,...  3.77 us
    pallas_call x1, Pallas kernels, second_gate(): pl.pallas_call(functools.partial(second_gate_kernel, first), in_specs=[VM...  2.52 us
    pallas_call x1, Pallas kernels, gate(): pl.pallas_call(functools.partial(gate_kernel, firsts), in_specs=[VMEM] *...  1.7 us
    pallas_call x1, Pallas kernels, prepare(): pl.pallas_call(functools.partial(prepare_kernel, firsts), in_specs=[VMEM]...  1.46 us
    pallas_call x1, Pallas kernels, last_mix(): pl.pallas_call(functools.partial(last_mix_kernel, first, len(heads)), in_...  1.37 us
    unnamed x12, local copies, waits for them, and re-layouts  1.11 us
  transfers between devices with their start and end apart: 5, of which 2 were waited for; matrix products, arithmetic and copies ran while one was open for 0% of the time, Pallas kernels for 44%

profile of v6, /device:TPU:16, one launch (start us, length us, event | category | flops | bytes accessed | tf_op | source)
XLA Modules:
  0.0 31.0 jit_solution(10672413639142892977)
XLA Ops:
  0.0 0.0 copy-start
  0.0 0.0 copy-start.1
  0.0 0.0 copy-start.2
  0.0 0.0 copy-start.3
  0.0 0.2 gate_first.1.begun_ref
  0.2 0.0 copy-start.5
  0.2 1.6 %collective-permute-start = (bf16[144,2304]{1,0:T(8,128)(2,1)S(1)}, bf16[144,2304]{1,0:T(8,128)(2,1)S(1)}, u32[]{:S(2)}, u32[]{:S(2)}) collective-permute-start(bf16[144,2304]{1,0:T(8,128)(2,1)S(1)} %gate_first.1.begun_ref), channel_id=1, source_target_pairs={{1,2},{3,4},{5,6},{7,8},{9,10},{11,12},{13,14},{17,18},{19,20},{21... | collective-permute-start | bytes 1990664 | tf_op jit(solution)/shard_map/ppermute | solution.py:26
  1.8 0.0 copy-done
  1.8 0.5 %copy-done.1 = bf16[128,8192]{1,0:T(8,128)(2,1)S(1)} copy-done((bf16[128,8192]{1,0:T(8,128)(2,1)S(1)}, bf16[128,8192]{1,0:T(8,128)(2,1)}, u32[]{:S(2)}) %copy-start.1) | copy-done | bytes 2097176
  2.2 0.6 %copy-done.2 = bf16[128,8192]{1,0:T(8,128)(2,1)S(1)} copy-done((bf16[128,8192]{1,0:T(8,128)(2,1)S(1)}, bf16[128,8192]{1,0:T(8,128)(2,1)}, u32[]{:S(2)}) %copy-start.2) | copy-done | bytes 2097176
  2.9 0.0 copy-done.3
  2.9 2.5 %gate_second.1 = (bf16[144,2304]{1,0:T(8,128)(2,1)S(1)}, bf16[128,2560]{1,0:T(8,128)(2,1)S(1)}) custom-call(bf16[128,8192]{1,0:T(8,128)(2,1)S(1)} %copy-done.1, bf16[128,8192]{1,0:T(8,128)(2,1)S(1)} %copy-done.2, bf16[128,8192]{1,0:T(8,128)(2,1)S(1)} %copy-done, f32[3,3,8192]{2,1,0:T(4,128)S(1)} %copy-done.3, bf16[144,2304]{1,0:T(8,128)(2,1)S(1)} %gate_first.1.begun_ref), custom_call_target="tpu_custom_call" | custom-call | flops 1000 | bytes 1000 | tf_op jit(solution)/shard_map/gate_second/pallas_call | solution.py:184
  5.4 1.9 %collective-permute-start.1 = (bf16[144,2304]{1,0:T(8,128)(2,1)S(1)}, bf16[144,2304]{1,0:T(8,128)(2,1)S(1)}, u32[]{:S(2)}, u32[]{:S(2)}) collective-permute-start(bf16[144,2304]{1,0:T(8,128)(2,1)S(1)} %get-tuple-element.30.own_ref), channel_id=1, source_target_pairs={{0,1},{2,3},{4,5},{6,7},{8,9},{10,11},{12,13},{14,15},{16,17},{18,... | collective-permute-start | bytes 1990664 | tf_op jit(solution)/shard_map/ppermute | solution.py:26
  7.3 1.9 %collective-permute-start.3 = (bf16[128,2560]{1,0:T(8,128)(2,1)S(1)}, bf16[128,2560]{1,0:T(8,128)(2,1)S(1)}, u32[]{:S(2)}, u32[]{:S(2)}) collective-permute-start(bf16[128,2560]{1,0:T(8,128)(2,1)S(1)} %get-tuple-element.27._.own_ref), channel_id=1, source_target_pairs={{0,1},{1,2},{2,3},{3,4},{4,5},{5,6},{6,7},{7,8},{8,9},{9,10},{10,1... | collective-permute-start | bytes 1966088 | tf_op jit(solution)/shard_map/ppermute | solution.py:26
  9.2 0.0 copy-done.5
  9.2 1.7 %gate.1 = (f32[512,128]{1,0:T(8,128)S(1)}, bf16[64,256]{1,0:T(8,128)(2,1)S(1)}, bf16[128,2304]{1,0:T(8,128)(2,1)S(1)}, bf16[128,1024]{1,0:T(8,128)(2,1)S(1)}) custom-call(bf16[128,8192]{1,0:T(8,128)(2,1)S(1)} %copy-done.1, bf16[128,8192]{1,0:T(8,128)(2,1)S(1)} %copy-done.2, bf16[128,8192]{1,0:T(8,128)(2,1)S(1)} %copy-done, f32[3,3,8192]{2,1,0:T(4,128)S(1)} %copy-done.3, ...), custom_call_target="tpu_custom_call" | custom-call | flops 1000 | bytes 1000 | tf_op jit(solution)/shard_map/gate/pallas_call | solution.py:207
  10.9 3.5 %collective-permute-start.4 = (bf16[128,2304]{1,0:T(8,128)(2,1)S(1)}, bf16[128,2304]{1,0:T(8,128)(2,1)S(1)}, u32[]{:S(2)}, u32[]{:S(2)}) collective-permute-start(bf16[128,2304]{1,0:T(8,128)(2,1)S(1)} %get-tuple-element.39.own_ref), channel_id=1, source_target_pairs={{0,1},{1,2},{2,3},{3,4},{4,5},{5,6},{6,7},{7,8},{8,9},{9,10},{10,1... | collective-permute-start | bytes 1769480 | tf_op jit(solution)/shard_map/ppermute | solution.py:26
  14.5 0.0 collective-permute-done.in_ref
  14.5 0.0 collective-permute-done.1.near_ref
  14.5 1.0 %gate_last.1 = (bf16[136,1024]{1,0:T(8,128)(2,1)S(1)}, bf16[16,8192]{1,0:T(8,128)(2,1)S(1)}, bf16[144,2304]{1,0:T(8,128)(2,1)S(1)}) custom-call(bf16[128,8192]{1,0:T(8,128)(2,1)S(1)} %copy-done.1, bf16[128,8192]{1,0:T(8,128)(2,1)S(1)} %copy-done.2, f32[3,3,8192]{2,1,0:T(4,128)S(1)} %copy-done.3, bf16[144,2304]{1,0:T(8,128)(2,1)S(1)} %settle.1.crossed_ref, ...), custom_call_target="tpu_custom_call" | custom-call | flops 1000 | bytes 1000 | tf_op jit(solution)/shard_map/gate_last/pallas_call | solution.py:274
  15.6 0.0 copy-start.4
  15.6 1.9 %collective-permute-start.2 = (bf16[136,1024]{1,0:T(8,128)(2,1)S(1)}, bf16[136,1024]{1,0:T(8,128)(2,1)S(1)}, u32[]{:S(2)}, u32[]{:S(2)}) collective-permute-start(bf16[136,1024]{1,0:T(8,128)(2,1)S(1)} %get-tuple-element.32.own_ref), channel_id=1, source_target_pairs={{0,1},{1,2},{2,3},{3,4},{4,5},{5,6},{6,7},{7,8},{8,9},{9,10},{10,1... | collective-permute-start | bytes 835592 | tf_op jit(solution)/shard_map/ppermute | solution.py:26
  17.5 1.5 %prepare.1 = (bf16[18,256,256]{2,1,0:T(8,128)(2,1)S(1)}, f32[128,2304]{1,0:T(8,128)S(1)}, bf16[8,256,256]{2,1,0:T(8,128)(2,1)S(1)}, f32[128,1024]{1,0:T(8,128)S(1)}) custom-call(f32[512,128]{1,0:T(8,128)S(1)} %get-tuple-element.28.turned_ref, bf16[64,256]{1,0:T(8,128)(2,1)S(1)} %get-tuple-element.29.mask_ref, bf16[128,8192]{1,0:T(8,128)(2,1)S(1)} %copy-done, ...), custom_call_target="tpu_custom_call" | custom-call | flops 1000 | bytes 1000 | tf_op jit(solution)/shard_map/prepare/pallas_call | solution.py:350
  19.0 0.0 copy-done.4
  19.0 2.4 %mix.3 = (bf16[128,8192]{1,0:T(8,128)(2,1)}, f32[16,2304]{1,0:T(8,128)S(1)}, f32[8,2304]{1,0:T(8,128)S(1)}) custom-call(f32[512,128]{1,0:T(8,128)S(1)} %get-tuple-element.28.turned_ref, bf16[64,256]{1,0:T(8,128)(2,1)S(1)} %get-tuple-element.29.mask_ref, bf16[144,2304]{1,0:T(8,128)(2,1)S(1)} %get-tuple-element.30.own_ref, ...), custom_call_target="tpu_custom_call" | custom-call | flops 1000 | bytes 1000 | tf_op jit(solution)/shard_map/mix/pallas_call | solution.py:504
  21.4 0.0 collective-permute-done.3.got_ref
  21.4 2.5 %mix.4 = (bf16[128,8192]{1,0:T(8,128)(2,1)}, f32[16,2560]{1,0:T(8,128)S(1)}, f32[8,2560]{1,0:T(8,128)S(1)}) custom-call(f32[512,128]{1,0:T(8,128)S(1)} %get-tuple-element.28.turned_ref, bf16[64,256]{1,0:T(8,128)(2,1)S(1)} %get-tuple-element.29.mask_ref, bf16[128,2560]{1,0:T(8,128)(2,1)S(1)} %get-tuple-element.27._.own_ref, ...), custom_call_target="tpu_custom_call", output_to_operand_aliasing={{0}: (8, {})} | custom-call | flops 1000 | bytes 1000 | tf_op jit(solution)/shard_map/mix/pallas_call | solution.py:504
  23.9 2.8 %collective-permute-done.4.got_ref = bf16[128,2304]{1,0:T(8,128)(2,1)S(1)} collective-permute-done((bf16[128,2304]{1,0:T(8,128)(2,1)S(1)}, bf16[128,2304]{1,0:T(8,128)(2,1)S(1)}, u32[]{:S(2)}, u32[]{:S(2)}) %collective-permute-start.4) | collective-permute-done | bytes 589856 | tf_op jit(solution)/shard_map/ppermute | solution.py:26
  26.7 2.0 %mix.5 = (bf16[128,8192]{1,0:T(8,128)(2,1)}, f32[16,2304]{1,0:T(8,128)S(1)}, f32[8,2304]{1,0:T(8,128)S(1)}) custom-call(f32[512,128]{1,0:T(8,128)S(1)} %get-tuple-element.28.turned_ref, bf16[64,256]{1,0:T(8,128)(2,1)S(1)} %get-tuple-element.29.mask_ref, bf16[128,2304]{1,0:T(8,128)(2,1)S(1)} %get-tuple-element.39.own_ref, ...), custom_call_target="tpu_custom_call", output_to_operand_aliasing={{0}: (8, {})} | custom-call | flops 1000 | bytes 1000 | tf_op jit(solution)/shard_map/mix/pallas_call | solution.py:504
  28.7 0.9 %collective-permute-done.2.got_ref = bf16[136,1024]{1,0:T(8,128)(2,1)S(1)} collective-permute-done((bf16[136,1024]{1,0:T(8,128)(2,1)S(1)}, bf16[136,1024]{1,0:T(8,128)(2,1)S(1)}, u32[]{:S(2)}, u32[]{:S(2)}) %collective-permute-start.2) | collective-permute-done | bytes 278560 | tf_op jit(solution)/shard_map/ppermute | solution.py:26
  29.7 1.4 %mix_last.1 = bf16[128,8192]{1,0:T(8,128)(2,1)} custom-call(f32[512,128]{1,0:T(8,128)S(1)} %get-tuple-element.28.turned_ref, bf16[64,256]{1,0:T(8,128)(2,1)S(1)} %get-tuple-element.29.mask_ref, bf16[136,1024]{1,0:T(8,128)(2,1)S(1)} %get-tuple-element.32.own_ref, ...), custom_call_target="tpu_custom_call", output_to_operand_aliasing={{}: (16, {})} | custom-call | flops 1000 | bytes 1000 | tf_op jit(solution)/shard_map/mix_last/pallas_call | solution.py:575
  (1 shorter events, 0.0 us)
Async XLA Ops:
  0.0 1.8 %copy-start = (bf16[128,8192]{1,0:T(8,128)(2,1)S(1)}, bf16[128,8192]{1,0:T(8,128)(2,1)}, u32[]{:S(2)}) copy-start(bf16[128,8192]{1,0:T(8,128)(2,1)} %q_ref.13) | copy-start | bytes 6291460
  0.0 2.2 %copy-start.1 = (bf16[128,8192]{1,0:T(8,128)(2,1)S(1)}, bf16[128,8192]{1,0:T(8,128)(2,1)}, u32[]{:S(2)}) copy-start(bf16[128,8192]{1,0:T(8,128)(2,1)} %k_ref.5) | copy-start | bytes 6291460
  0.0 2.9 %copy-start.2 = (bf16[128,8192]{1,0:T(8,128)(2,1)S(1)}, bf16[128,8192]{1,0:T(8,128)(2,1)}, u32[]{:S(2)}) copy-start(bf16[128,8192]{1,0:T(8,128)(2,1)} %v_ref.5) | copy-start | bytes 6291460
  0.0 2.9 %copy-start.3 = (f32[3,3,8192]{2,1,0:T(4,128)S(1)}, f32[3,3,8192]{2,1,0:T(4,128)}, u32[]{:S(2)}) copy-start(f32[3,3,8192]{2,1,0:T(4,128)} %taps_ref.15) | copy-start | bytes 884740
  0.2 9.0 %copy-start.5 = (bf16[512,128]{1,0:T(8,128)(2,1)S(1)}, bf16[512,128]{1,0:T(8,128)(2,1)}, u32[]{:S(2)}) copy-start(bf16[512,128]{1,0:T(8,128)(2,1)} %h_ref.1) | copy-start | bytes 393220
  0.2 14.3 %collective-permute-start = (bf16[144,2304]{1,0:T(8,128)(2,1)S(1)}, bf16[144,2304]{1,0:T(8,128)(2,1)S(1)}, u32[]{:S(2)}, u32[]{:S(2)}) collective-permute-start(bf16[144,2304]{1,0:T(8,128)(2,1)S(1)} %gate_first.1.begun_ref), channel_id=1, source_target_pairs={{1,2},{3,4},{5,6},{7,8},{9,10},{11,12},{13,14},{17,18},{19,20},{21... | collective-permute-start | bytes 1990664 | tf_op jit(solution)/shard_map/ppermute | solution.py:26
  5.4 9.1 %collective-permute-start.1 = (bf16[144,2304]{1,0:T(8,128)(2,1)S(1)}, bf16[144,2304]{1,0:T(8,128)(2,1)S(1)}, u32[]{:S(2)}, u32[]{:S(2)}) collective-permute-start(bf16[144,2304]{1,0:T(8,128)(2,1)S(1)} %get-tuple-element.30.own_ref), channel_id=1, source_target_pairs={{0,1},{2,3},{4,5},{6,7},{8,9},{10,11},{12,13},{14,15},{16,17},{18,... | collective-permute-start | bytes 1990664 | tf_op jit(solution)/shard_map/ppermute | solution.py:26
  7.3 14.1 %collective-permute-start.3 = (bf16[128,2560]{1,0:T(8,128)(2,1)S(1)}, bf16[128,2560]{1,0:T(8,128)(2,1)S(1)}, u32[]{:S(2)}, u32[]{:S(2)}) collective-permute-start(bf16[128,2560]{1,0:T(8,128)(2,1)S(1)} %get-tuple-element.27._.own_ref), channel_id=1, source_target_pairs={{0,1},{1,2},{2,3},{3,4},{4,5},{5,6},{6,7},{7,8},{8,9},{9,10},{10,1... | collective-permute-start | bytes 1966088 | tf_op jit(solution)/shard_map/ppermute | solution.py:26
  10.9 15.8 %collective-permute-start.4 = (bf16[128,2304]{1,0:T(8,128)(2,1)S(1)}, bf16[128,2304]{1,0:T(8,128)(2,1)S(1)}, u32[]{:S(2)}, u32[]{:S(2)}) collective-permute-start(bf16[128,2304]{1,0:T(8,128)(2,1)S(1)} %get-tuple-element.39.own_ref), channel_id=1, source_target_pairs={{0,1},{1,2},{2,3},{3,4},{4,5},{5,6},{6,7},{7,8},{8,9},{9,10},{10,1... | collective-permute-start | bytes 1769480 | tf_op jit(solution)/shard_map/ppermute | solution.py:26
  15.6 3.4 %copy-start.4 = (f32[8192]{0:T(1024)S(1)}, f32[8192]{0:T(1024)}, u32[]{:S(2)}) copy-start(f32[8192]{0:T(1024)} %param.11) | copy-start | bytes 98308
  15.6 14.1 %collective-permute-start.2 = (bf16[136,1024]{1,0:T(8,128)(2,1)S(1)}, bf16[136,1024]{1,0:T(8,128)(2,1)S(1)}, u32[]{:S(2)}, u32[]{:S(2)}) collective-permute-start(bf16[136,1024]{1,0:T(8,128)(2,1)S(1)} %get-tuple-element.32.own_ref), channel_id=1, source_target_pairs={{0,1},{1,2},{2,3},{3,4},{4,5},{5,6},{6,7},{7,8},{8,9},{9,10},{10,1... | collective-permute-start | bytes 835592 | tf_op jit(solution)/shard_map/ppermute | solution.py:26

commit v7 on v6

--- a/solution.py
+++ b/solution.py
@@ -49,7 +49,7 @@
     return pltpu.with_memory_space_constraint(x, pltpu.HBM)
 
 
-def run_of(tiles, most=10):
+def run_of(tiles, most=12):
     return max(n for n in range(1, most + 1) if tiles % n == 0)
 
 
@@ -593,7 +593,7 @@
     rows, width = q_stream.shape
     skip = skip_gain.reshape(1, width)
     unit = width // 32
-    sizes = [9 * unit, 10 * unit, 9 * unit, 4 * unit]
+    sizes = [10 * unit, 11 * unit, 8 * unit, 3 * unit]
     starts = [sum(sizes[:i]) for i in range(len(sizes))]
     streams = (k_stream, v_stream, q_stream, feat_filter)
     begun = first_gate(*streams, sizes[0])

time: 31.3 us -> 31.3 us (level)
  waiting for transfers between devices: 3.77 us -> 4.1 us
    ppermute x5, waiting for transfers between devices: 3.77 us -> 4.1 us  [passed_along(): lax.ppermute(shard, 'seq', [(i, i + 1) for i in range(first, length - 1,...]
  transfers between devices with their start and end apart: 5 -> 5, of which waited for: 2 -> 3; matrix products, arithmetic and copies ran while one was open for 0% -> 0% of each run, Pallas kernels for 44% -> 44%
where the time goes in v7:
time: 31.3 us; the launch traced here: 31.1 us
  Pallas kernels  15 us (48%)
  starting transfers between devices  10.6 us (34%)
  waiting for transfers between devices  4.1 us (13%)
  local copies, waits for them, and re-layouts  1.15 us (4%)
    ppermute x5, starting transfers between devices, passed_along(): lax.ppermute(shard, 'seq', [(i, i + 1) for i in range(first, length - 1,...  10.6 us
    pallas_call x3, Pallas kernels, mix(): pl.pallas_call(functools.partial(mix_kernel, first, out is not None, len(...  7.06 us
    ppermute x5, waiting for transfers between devices, passed_along(): lax.ppermute(shard, 'seq', [(i, i + 1) for i in range(first, length - 1,...  4.1 us
    pallas_call x1, Pallas kernels, second_gate(): pl.pallas_call(functools.partial(second_gate_kernel, first), in_specs=[VM...  2.79 us
    pallas_call x1, Pallas kernels, gate(): pl.pallas_call(functools.partial(gate_kernel, firsts), in_specs=[VMEM] *...  1.47 us
    pallas_call x1, Pallas kernels, last_mix(): pl.pallas_call(functools.partial(last_mix_kernel, first, len(heads)), in_...  1.28 us
    pallas_call x1, Pallas kernels, prepare(): pl.pallas_call(functools.partial(prepare_kernel, firsts), in_specs=[VMEM]...  1.22 us
    unnamed x12, local copies, waits for them, and re-layouts  1.15 us
  transfers between devices with their start and end apart: 5, of which 3 were waited for; matrix products, arithmetic and copies ran while one was open for 0% of the time, Pallas kernels for 44%

profile of v7, /device:TPU:16, one launch (start us, length us, event | category | flops | bytes accessed | tf_op | source)
XLA Modules:
  0.0 31.1 jit_solution(7081584915692844592)
XLA Ops:
  0.0 0.0 copy-start
  0.0 0.0 copy-start.1
  0.0 0.0 copy-start.2
  0.0 0.0 copy-start.3
  0.0 0.1 gate_first.1.begun_ref
  0.2 0.0 copy-start.5
  0.2 1.6 %collective-permute-start = (bf16[144,2560]{1,0:T(8,128)(2,1)S(1)}, bf16[144,2560]{1,0:T(8,128)(2,1)S(1)}, u32[]{:S(2)}, u32[]{:S(2)}) collective-permute-start(bf16[144,2560]{1,0:T(8,128)(2,1)S(1)} %gate_first.1.begun_ref), channel_id=1, source_target_pairs={{1,2},{3,4},{5,6},{7,8},{9,10},{11,12},{13,14},{17,18},{19,20},{21... | collective-permute-start | bytes 2211848 | tf_op jit(solution)/shard_map/ppermute | solution.py:26
  1.7 0.0 copy-done
  1.7 0.5 %copy-done.1 = bf16[128,8192]{1,0:T(8,128)(2,1)S(1)} copy-done((bf16[128,8192]{1,0:T(8,128)(2,1)S(1)}, bf16[128,8192]{1,0:T(8,128)(2,1)}, u32[]{:S(2)}) %copy-start.1) | copy-done | bytes 2097176
  2.2 0.6 %copy-done.2 = bf16[128,8192]{1,0:T(8,128)(2,1)S(1)} copy-done((bf16[128,8192]{1,0:T(8,128)(2,1)S(1)}, bf16[128,8192]{1,0:T(8,128)(2,1)}, u32[]{:S(2)}) %copy-start.2) | copy-done | bytes 2097176
  2.9 0.0 copy-done.3
  2.9 2.8 %gate_second.1 = (bf16[144,2560]{1,0:T(8,128)(2,1)S(1)}, bf16[128,2816]{1,0:T(8,128)(2,1)S(1)}) custom-call(bf16[128,8192]{1,0:T(8,128)(2,1)S(1)} %copy-done.1, bf16[128,8192]{1,0:T(8,128)(2,1)S(1)} %copy-done.2, bf16[128,8192]{1,0:T(8,128)(2,1)S(1)} %copy-done, f32[3,3,8192]{2,1,0:T(4,128)S(1)} %copy-done.3, bf16[144,2560]{1,0:T(8,128)(2,1)S(1)} %gate_first.1.begun_ref), custom_call_target="tpu_custom_call" | custom-call | flops 1000 | bytes 1000 | tf_op jit(solution)/shard_map/gate_second/pallas_call | solution.py:184
  5.7 1.7 %collective-permute-start.1 = (bf16[144,2560]{1,0:T(8,128)(2,1)S(1)}, bf16[144,2560]{1,0:T(8,128)(2,1)S(1)}, u32[]{:S(2)}, u32[]{:S(2)}) collective-permute-start(bf16[144,2560]{1,0:T(8,128)(2,1)S(1)} %get-tuple-element.30.own_ref), channel_id=1, source_target_pairs={{0,1},{2,3},{4,5},{6,7},{8,9},{10,11},{12,13},{14,15},{16,17},{18,... | collective-permute-start | bytes 2211848 | tf_op jit(solution)/shard_map/ppermute | solution.py:26
  7.4 1.9 %collective-permute-start.3 = (bf16[128,2816]{1,0:T(8,128)(2,1)S(1)}, bf16[128,2816]{1,0:T(8,128)(2,1)S(1)}, u32[]{:S(2)}, u32[]{:S(2)}) collective-permute-start(bf16[128,2816]{1,0:T(8,128)(2,1)S(1)} %get-tuple-element.27._.own_ref), channel_id=1, source_target_pairs={{0,1},{1,2},{2,3},{3,4},{4,5},{5,6},{6,7},{7,8},{8,9},{9,10},{10,1... | collective-permute-start | bytes 2162696 | tf_op jit(solution)/shard_map/ppermute | solution.py:26
  9.3 0.0 copy-done.5
  9.3 1.5 %gate.1 = (f32[512,128]{1,0:T(8,128)S(1)}, bf16[64,256]{1,0:T(8,128)(2,1)S(1)}, bf16[128,2048]{1,0:T(8,128)(2,1)S(1)}, bf16[128,768]{1,0:T(8,128)(2,1)S(1)}) custom-call(bf16[128,8192]{1,0:T(8,128)(2,1)S(1)} %copy-done.1, bf16[128,8192]{1,0:T(8,128)(2,1)S(1)} %copy-done.2, bf16[128,8192]{1,0:T(8,128)(2,1)S(1)} %copy-done, f32[3,3,8192]{2,1,0:T(4,128)S(1)} %copy-done.3, ...), custom_call_target="tpu_custom_call" | custom-call | flops 1000 | bytes 1000 | tf_op jit(solution)/shard_map/gate/pallas_call | solution.py:207
  10.8 3.5 %collective-permute-start.4 = (bf16[128,2048]{1,0:T(8,128)(2,1)S(1)}, bf16[128,2048]{1,0:T(8,128)(2,1)S(1)}, u32[]{:S(2)}, u32[]{:S(2)}) collective-permute-start(bf16[128,2048]{1,0:T(8,128)(2,1)S(1)} %get-tuple-element.39.own_ref), channel_id=1, source_target_pairs={{0,1},{1,2},{2,3},{3,4},{4,5},{5,6},{6,7},{7,8},{8,9},{9,10},{10,1... | collective-permute-start | bytes 1572872 | tf_op jit(solution)/shard_map/ppermute | solution.py:26
  14.3 0.0 collective-permute-done.in_ref
  14.4 0.0 collective-permute-done.1.near_ref
  14.4 1.0 %gate_last.1 = (bf16[144,768]{1,0:T(8,128)(2,1)S(1)}, bf16[16,8192]{1,0:T(8,128)(2,1)S(1)}, bf16[144,2560]{1,0:T(8,128)(2,1)S(1)}) custom-call(bf16[128,8192]{1,0:T(8,128)(2,1)S(1)} %copy-done.1, bf16[128,8192]{1,0:T(8,128)(2,1)S(1)} %copy-done.2, f32[3,3,8192]{2,1,0:T(4,128)S(1)} %copy-done.3, bf16[144,2560]{1,0:T(8,128)(2,1)S(1)} %settle.1.crossed_ref, ...), custom_call_target="tpu_custom_call" | custom-call | flops 1000 | bytes 1000 | tf_op jit(solution)/shard_map/gate_last/pallas_call | solution.py:274
  15.5 0.0 copy-start.4
  15.5 1.9 %collective-permute-start.2 = (bf16[144,768]{1,0:T(8,128)(2,1)S(1)}, bf16[144,768]{1,0:T(8,128)(2,1)S(1)}, u32[]{:S(2)}, u32[]{:S(2)}) collective-permute-start(bf16[144,768]{1,0:T(8,128)(2,1)S(1)} %get-tuple-element.32.own_ref), channel_id=1, source_target_pairs={{0,1},{1,2},{2,3},{3,4},{4,5},{5,6},{6,7},{7,8},{8,9},{9,10},{10,1... | collective-permute-start | bytes 663560 | tf_op jit(solution)/shard_map/ppermute | solution.py:26
  17.4 1.2 %prepare.1 = (bf16[16,256,256]{2,1,0:T(8,128)(2,1)S(1)}, f32[128,2048]{1,0:T(8,128)S(1)}, bf16[6,256,256]{2,1,0:T(8,128)(2,1)S(1)}, f32[128,768]{1,0:T(8,128)S(1)}) custom-call(f32[512,128]{1,0:T(8,128)S(1)} %get-tuple-element.28.turned_ref, bf16[64,256]{1,0:T(8,128)(2,1)S(1)} %get-tuple-element.29.mask_ref, bf16[128,8192]{1,0:T(8,128)(2,1)S(1)} %copy-done, ...), custom_call_target="tpu_custom_call" | custom-call | flops 1000 | bytes 1000 | tf_op jit(solution)/shard_map/prepare/pallas_call | solution.py:350
  18.6 0.0 copy-done.4
  18.6 2.5 %mix.3 = (bf16[128,8192]{1,0:T(8,128)(2,1)}, f32[16,2560]{1,0:T(8,128)S(1)}, f32[8,2560]{1,0:T(8,128)S(1)}) custom-call(f32[512,128]{1,0:T(8,128)S(1)} %get-tuple-element.28.turned_ref, bf16[64,256]{1,0:T(8,128)(2,1)S(1)} %get-tuple-element.29.mask_ref, bf16[144,2560]{1,0:T(8,128)(2,1)S(1)} %get-tuple-element.30.own_ref, ...), custom_call_target="tpu_custom_call" | custom-call | flops 1000 | bytes 1000 | tf_op jit(solution)/shard_map/mix/pallas_call | solution.py:504
  21.1 0.7 %collective-permute-done.3.got_ref = bf16[128,2816]{1,0:T(8,128)(2,1)S(1)} collective-permute-done((bf16[128,2816]{1,0:T(8,128)(2,1)S(1)}, bf16[128,2816]{1,0:T(8,128)(2,1)S(1)}, u32[]{:S(2)}, u32[]{:S(2)}) %collective-permute-start.3) | collective-permute-done | bytes 720928 | tf_op jit(solution)/shard_map/ppermute | solution.py:26
  21.8 2.7 %mix.4 = (bf16[128,8192]{1,0:T(8,128)(2,1)}, f32[16,2816]{1,0:T(8,128)S(1)}, f32[8,2816]{1,0:T(8,128)S(1)}) custom-call(f32[512,128]{1,0:T(8,128)S(1)} %get-tuple-element.28.turned_ref, bf16[64,256]{1,0:T(8,128)(2,1)S(1)} %get-tuple-element.29.mask_ref, bf16[128,2816]{1,0:T(8,128)(2,1)S(1)} %get-tuple-element.27._.own_ref, ...), custom_call_target="tpu_custom_call", output_to_operand_aliasing={{0}: (8, {})} | custom-call | flops 1000 | bytes 1000 | tf_op jit(solution)/shard_map/mix/pallas_call | solution.py:504
  24.5 3.0 %collective-permute-done.4.got_ref = bf16[128,2048]{1,0:T(8,128)(2,1)S(1)} collective-permute-done((bf16[128,2048]{1,0:T(8,128)(2,1)S(1)}, bf16[128,2048]{1,0:T(8,128)(2,1)S(1)}, u32[]{:S(2)}, u32[]{:S(2)}) %collective-permute-start.4) | collective-permute-done | bytes 524320 | tf_op jit(solution)/shard_map/ppermute | solution.py:26
  27.5 1.9 %mix.5 = (bf16[128,8192]{1,0:T(8,128)(2,1)}, f32[16,2048]{1,0:T(8,128)S(1)}, f32[8,2048]{1,0:T(8,128)S(1)}) custom-call(f32[512,128]{1,0:T(8,128)S(1)} %get-tuple-element.28.turned_ref, bf16[64,256]{1,0:T(8,128)(2,1)S(1)} %get-tuple-element.29.mask_ref, bf16[128,2048]{1,0:T(8,128)(2,1)S(1)} %get-tuple-element.39.own_ref, ...), custom_call_target="tpu_custom_call", output_to_operand_aliasing={{0}: (8, {})} | custom-call | flops 1000 | bytes 1000 | tf_op jit(solution)/shard_map/mix/pallas_call | solution.py:504
  29.4 0.4 %collective-permute-done.2.got_ref = bf16[144,768]{1,0:T(8,128)(2,1)S(1)} collective-permute-done((bf16[144,768]{1,0:T(8,128)(2,1)S(1)}, bf16[144,768]{1,0:T(8,128)(2,1)S(1)}, u32[]{:S(2)}, u32[]{:S(2)}) %collective-permute-start.2) | collective-permute-done | bytes 221216 | tf_op jit(solution)/shard_map/ppermute | solution.py:26
  29.8 1.3 %mix_last.1 = bf16[128,8192]{1,0:T(8,128)(2,1)} custom-call(f32[512,128]{1,0:T(8,128)S(1)} %get-tuple-element.28.turned_ref, bf16[64,256]{1,0:T(8,128)(2,1)S(1)} %get-tuple-element.29.mask_ref, bf16[144,768]{1,0:T(8,128)(2,1)S(1)} %get-tuple-element.32.own_ref, bf16[144,768]{1,0:T(8,128)(2,1)S(1)} %collective-permute-done.2.got_ref, ...), custom_call_target="tpu_custom_call", output_to_operand_aliasing={{}: (16, {})} | custom-call | flops 1000 | bytes 1000 | tf_op jit(solution)/shard_map/mix_last/pallas_call | solution.py:575
  (1 shorter events, 0.0 us)
Async XLA Ops:
  0.0 1.7 %copy-start = (bf16[128,8192]{1,0:T(8,128)(2,1)S(1)}, bf16[128,8192]{1,0:T(8,128)(2,1)}, u32[]{:S(2)}) copy-start(bf16[128,8192]{1,0:T(8,128)(2,1)} %q_ref.13) | copy-start | bytes 6291460
  0.0 2.2 %copy-start.1 = (bf16[128,8192]{1,0:T(8,128)(2,1)S(1)}, bf16[128,8192]{1,0:T(8,128)(2,1)}, u32[]{:S(2)}) copy-start(bf16[128,8192]{1,0:T(8,128)(2,1)} %k_ref.5) | copy-start | bytes 6291460
  0.0 2.9 %copy-start.2 = (bf16[128,8192]{1,0:T(8,128)(2,1)S(1)}, bf16[128,8192]{1,0:T(8,128)(2,1)}, u32[]{:S(2)}) copy-start(bf16[128,8192]{1,0:T(8,128)(2,1)} %v_ref.5) | copy-start | bytes 6291460
  0.0 2.9 %copy-start.3 = (f32[3,3,8192]{2,1,0:T(4,128)S(1)}, f32[3,3,8192]{2,1,0:T(4,128)}, u32[]{:S(2)}) copy-start(f32[3,3,8192]{2,1,0:T(4,128)} %taps_ref.15) | copy-start | bytes 884740
  0.2 9.2 %copy-start.5 = (bf16[512,128]{1,0:T(8,128)(2,1)S(1)}, bf16[512,128]{1,0:T(8,128)(2,1)}, u32[]{:S(2)}) copy-start(bf16[512,128]{1,0:T(8,128)(2,1)} %h_ref.1) | copy-start | bytes 393220
  0.2 14.2 %collective-permute-start = (bf16[144,2560]{1,0:T(8,128)(2,1)S(1)}, bf16[144,2560]{1,0:T(8,128)(2,1)S(1)}, u32[]{:S(2)}, u32[]{:S(2)}) collective-permute-start(bf16[144,2560]{1,0:T(8,128)(2,1)S(1)} %gate_first.1.begun_ref), channel_id=1, source_target_pairs={{1,2},{3,4},{5,6},{7,8},{9,10},{11,12},{13,14},{17,18},{19,20},{21... | collective-permute-start | bytes 2211848 | tf_op jit(solution)/shard_map/ppermute | solution.py:26
  5.7 8.8 %collective-permute-start.1 = (bf16[144,2560]{1,0:T(8,128)(2,1)S(1)}, bf16[144,2560]{1,0:T(8,128)(2,1)S(1)}, u32[]{:S(2)}, u32[]{:S(2)}) collective-permute-start(bf16[144,2560]{1,0:T(8,128)(2,1)S(1)} %get-tuple-element.30.own_ref), channel_id=1, source_target_pairs={{0,1},{2,3},{4,5},{6,7},{8,9},{10,11},{12,13},{14,15},{16,17},{18,... | collective-permute-start | bytes 2211848 | tf_op jit(solution)/shard_map/ppermute | solution.py:26
  7.4 14.5 %collective-permute-start.3 = (bf16[128,2816]{1,0:T(8,128)(2,1)S(1)}, bf16[128,2816]{1,0:T(8,128)(2,1)S(1)}, u32[]{:S(2)}, u32[]{:S(2)}) collective-permute-start(bf16[128,2816]{1,0:T(8,128)(2,1)S(1)} %get-tuple-element.27._.own_ref), channel_id=1, source_target_pairs={{0,1},{1,2},{2,3},{3,4},{4,5},{5,6},{6,7},{7,8},{8,9},{9,10},{10,1... | collective-permute-start | bytes 2162696 | tf_op jit(solution)/shard_map/ppermute | solution.py:26
  10.8 16.7 %collective-permute-start.4 = (bf16[128,2048]{1,0:T(8,128)(2,1)S(1)}, bf16[128,2048]{1,0:T(8,128)(2,1)S(1)}, u32[]{:S(2)}, u32[]{:S(2)}) collective-permute-start(bf16[128,2048]{1,0:T(8,128)(2,1)S(1)} %get-tuple-element.39.own_ref), channel_id=1, source_target_pairs={{0,1},{1,2},{2,3},{3,4},{4,5},{5,6},{6,7},{7,8},{8,9},{9,10},{10,1... | collective-permute-start | bytes 1572872 | tf_op jit(solution)/shard_map/ppermute | solution.py:26
  15.5 3.2 %copy-start.4 = (f32[8192]{0:T(1024)S(1)}, f32[8192]{0:T(1024)}, u32[]{:S(2)}) copy-start(f32[8192]{0:T(1024)} %param.11) | copy-start | bytes 98308
  15.5 14.3 %collective-permute-start.2 = (bf16[144,768]{1,0:T(8,128)(2,1)S(1)}, bf16[144,768]{1,0:T(8,128)(2,1)S(1)}, u32[]{:S(2)}, u32[]{:S(2)}) collective-permute-start(bf16[144,768]{1,0:T(8,128)(2,1)S(1)} %get-tuple-element.32.own_ref), channel_id=1, source_target_pairs={{0,1},{1,2},{2,3},{3,4},{4,5},{5,6},{6,7},{7,8},{8,9},{9,10},{10,1... | collective-permute-start | bytes 663560 | tf_op jit(solution)/shard_map/ppermute | solution.py:26

commit v8 on v6

--- a/solution.py
+++ b/solution.py
@@ -330,7 +330,46 @@
     return total
 
 
-def prepare_kernel(firsts, turned_ref, mask_ref, q_ref, taps_ref, *out_refs):
+def window_conv(lhs_ref, both, depth):
+    rows = len(both) // 2 * SUB
+    span = rows // WINDOWS
+    half = LANES // GROUP_CH // 2
+    lane_group = lax.broadcasted_iota(jnp.int32, (8, 2 * LANES), 1) % (LANES // 2) // GROUP_CH
+    ahead = span // SUB
+    count = len(both) - ahead
+    sides = (slice(0, LANES // 2), slice(LANES // 2, LANES))
+    halves = [
+        [jnp.concatenate([both[i][:, side], both[i + ahead][:, side]], axis=1) for i in range(count)]
+        for side in sides
+    ]
+    res = []
+    for h, blocks in enumerate(halves):
+        cols = [
+            jnp.concatenate([blocks[min(w * ahead + i, count - 1)] for i in range(depth // SUB)], axis=0)
+            for w in range(0, WINDOWS, 2)
+        ]
+        lhs = lhs_ref[h * half * span : (h + 1) * half * span, :depth]
+        res.append(jnp.dot(lhs, jnp.concatenate(cols, axis=1), preferred_element_type=F32))
+    parts = [[] for _ in range(WINDOWS)]
+    for r in range(span // 8):
+        totals = []
+        for x in res:
+            total = x[r * half * 8 : r * half * 8 + 8]
+            for g in range(1, half):
+                at = (r * half + g) * 8
+                total = jnp.where(lane_group == g, x[at : at + 8], total)
+            totals.append(total)
+        for w in range(0, WINDOWS, 2):
+            a, b = (t[:, w // 2 * LANES : (w // 2 + 1) * LANES] for t in totals)
+            for i, side in enumerate(sides):
+                parts[w + i].append(jnp.concatenate([a[:, side], b[:, side]], axis=1))
+    return jnp.concatenate([x for part in parts for x in part], axis=0)
+
+
+def prepare_kernel(firsts, turned_ref, mask_ref, q_ref, taps_ref, own_ref, edge_ref, skip_ref, *out_refs):
+    part_ref = out_refs[-1]
+    rows = q_ref.shape[0]
+    iota = rows_iota((SUB, LANES))
     per = LANES // GROUP_CH
     for i, first in enumerate(firsts):
         lhs_ref, feat_ref = out_refs[2 * i : 2 * i + 2]
@@ -342,15 +381,22 @@
             src = lanes_at(c_all)
             toeplitz_rows(turned_ref[pl.ds(pl.multiple_of(c_all * per, per), per), :], mask_ref, lhs_ref.at[c])
             feat_ref[:, lanes_at(c)] = own_feature(q_ref[:, src].astype(F32), taps_ref[0, :, src])
-
-
-def prepare(turned, mask, q, taps, firsts, widths):
+            if i == len(firsts) - 1:
+                at = lanes_at(c)
+                head = jnp.where(iota < FEAT - 1, edge_ref[:, src].astype(F32), own_ref[:SUB, at].astype(F32))
+                own = [head.astype(BF16)] + [own_ref[r : r + SUB, at] for r in range(SUB, rows, SUB)]
+                none = [jnp.zeros((SUB, LANES), BF16)] * (rows // SUB)
+                cur = jnp.concatenate(own, axis=0).astype(F32)
+                part_ref[:, at] = window_conv(lhs_ref.at[c], none + own, 2 * FILT) + skip_ref[:, src] * cur
+
+
+def prepare(turned, mask, q, taps, own, edges, skip, firsts, widths):
     rows = q.shape[0]
     lhs = LANES // GROUP_CH * rows // WINDOWS
     return pl.pallas_call(
         functools.partial(prepare_kernel, firsts),
-        in_specs=[VMEM] * 4,
-        out_specs=[VMEM] * (2 * len(widths)),
+        in_specs=[VMEM] * 7,
+        out_specs=[VMEM] * (2 * len(widths) + 1),
         out_shape=[
             shape
             for w in widths
@@ -358,20 +404,18 @@
                 jax.ShapeDtypeStruct((w // LANES, lhs, 2 * FILT), BF16),
                 jax.ShapeDtypeStruct((rows, w), F32),
             )
-        ],
+        ]
+        + [jax.ShapeDtypeStruct((rows, widths[-1]), F32)],
         compiler_params=params(12),
         cost_estimate=COST,
         name="prepare",
-    )(turned, mask, q, taps)
-
-
-def mix_tile(turned_ref, mask_ref, lhs_ref, feat_ref, own_ref, got_ref, edge_ref, q_ref, taps_ref, skip_ref, before, src, dst, c):
+    )(turned, mask, q, taps, own, edges, skip)
+
+
+def mix_tile(turned_ref, mask_ref, lhs_ref, feat_ref, own_ref, got_ref, edge_ref, q_ref, taps_ref, skip_ref, before, src, dst, c, part_ref=None):
     rows = q_ref.shape[0]
-    span = rows // WINDOWS
     per = LANES // GROUP_CH
-    half = per // 2
     iota = rows_iota((SUB, LANES))
-    lane_group = lax.broadcasted_iota(jnp.int32, (8, 2 * LANES), 1) % (LANES // 2) // GROUP_CH
     turned = turned_ref[pl.ds(c * per if isinstance(c, int) else pl.multiple_of(c * per, per), per), :]
     taps = taps_ref[0, :, src]
     if feat_ref is None:
@@ -388,42 +432,18 @@
         got_head = jnp.where(iota < FEAT - 1, before, got_head)
     both = [got_head.astype(BF16)] + [got_ref[r : r + SUB, dst] for r in range(SUB, rows, SUB)]
     both += [own_head.astype(BF16)] + [own_ref[r : r + SUB, dst] for r in range(SUB, rows, SUB)]
-    ahead = span // SUB
-    count = len(both) - ahead
-    sides = (slice(0, LANES // 2), slice(LANES // 2, LANES))
-    halves = [
-        [jnp.concatenate([both[i][:, side], both[i + ahead][:, side]], axis=1) for i in range(count)]
-        for side in sides
-    ]
-    res = []
-    for h, blocks in enumerate(halves):
-        cols = [
-            jnp.concatenate([blocks[min(w * ahead + i, count - 1)] for i in range(2 * FILT // SUB)], axis=0)
-            for w in range(0, WINDOWS, 2)
-        ]
-        lhs = lhs_ref[h * half * span : (h + 1) * half * span, :]
-        res.append(jnp.dot(lhs, jnp.concatenate(cols, axis=1), preferred_element_type=F32))
-    parts = [[] for _ in range(WINDOWS)]
-    for r in range(span // 8):
-        totals = []
-        for x in res:
-            total = x[r * half * 8 : r * half * 8 + 8]
-            for g in range(1, half):
-                at = (r * half + g) * 8
-                total = jnp.where(lane_group == g, x[at : at + 8], total)
-            totals.append(total)
-        for w in range(0, WINDOWS, 2):
-            a, b = (t[:, w // 2 * LANES : (w // 2 + 1) * LANES] for t in totals)
-            for i, side in enumerate(sides):
-                parts[w + i].append(jnp.concatenate([a[:, side], b[:, side]], axis=1))
-    conv = jnp.concatenate([x for part in parts for x in part], axis=0)
-    cur = jnp.concatenate(both[rows // SUB :], axis=0).astype(F32)
+    if part_ref is None:
+        cur = jnp.concatenate(both[rows // SUB :], axis=0).astype(F32)
+        summed = window_conv(lhs_ref, both, 2 * FILT) + skip_ref[:, src] * cur
+    else:
+        none = [jnp.zeros((SUB, LANES), BF16)] * (rows // SUB)
+        summed = window_conv(lhs_ref, both[: rows // SUB] + none, FILT) + part_ref[:, dst]
     head = q_feat[:SUB]
     for d in range(1, FEAT):
         shifted = pltpu.roll(q_rim, (d - (FEAT - 1)) % SUB, 0)
         head = head + taps[d : d + 1] * jnp.where(iota < d, shifted, 0.0)
     q_feat = jnp.concatenate([head, q_feat[SUB:]], axis=0)
-    return q_feat * (conv + skip_ref[:, src] * cur), q_feat, turned
+    return q_feat * summed, q_feat, turned
 
 
 def mix_kernel(first, has_out, has_ready, has_after, turned_ref, mask_ref, own_ref, got_ref, edge_ref, q_ref, taps_ref, skip_ref, *refs):
@@ -524,7 +544,7 @@
 
 def last_mix_kernel(first, parts, turned_ref, mask_ref, own_ref, got_ref, edge_ref, q_ref, taps_ref, skip_ref, *refs):
     heads, slopes = refs[:parts], refs[parts : 2 * parts]
-    lhs_ref, feat_ref, _, out_hbm, res_ref, top_ref, sems = refs[2 * parts :]
+    lhs_ref, feat_ref, part_ref, _, out_hbm, res_ref, top_ref, sems = refs[2 * parts :]
     rows = q_ref.shape[0]
     tiles = res_ref.shape[1] // LANES
     mine = first // LANES
@@ -560,6 +580,7 @@
             lanes_at(c + mine),
             dst,
             c + mine,
+            part_ref,
         )
         res_ref[:, dst] = mixed.astype(BF16)
     copy = pltpu.make_async_copy(res_ref, out_hbm.at[:, pl.ds(first, tiles * LANES)], sems.at[1])
@@ -607,7 +628,7 @@
     last, edges, got[0] = last_gate(k_stream, v_stream, feat_filter, settle(crossed), near, last)
     own.append(last)
     got.append(passed_along(last))
-    ready = prepare(turned, mask, q_stream, feat_filter, starts[2:], sizes[2:])
+    ready = prepare(turned, mask, q_stream, feat_filter, own[3], edges, skip, starts[2:], sizes[2:])
     rest = (edges, q_stream, feat_filter, skip)
     out = None
     heads = []

time: 31.3 us -> 31.2 us (level)
  waiting for transfers between devices: 3.77 us -> 3.18 us
  Pallas kernels: 15.2 us -> 15.7 us
    ppermute x5, waiting for transfers between devices: 3.77 us -> 3.18 us  [passed_along(): lax.ppermute(shard, 'seq', [(i, i + 1) for i in range(first, length - 1,...]
    pallas_call x1, Pallas kernels: 1.46 us -> 2.04 us  [prepare(): pl.pallas_call(functools.partial(prepare_kernel, firsts), in_specs=[VMEM]...]
  transfers between devices with their start and end apart: 5 -> 5, of which waited for: 2 -> 2; matrix products, arithmetic and copies ran while one was open for 0% -> 0% of each run, Pallas kernels for 44% -> 46%
where the time goes in v8:
time: 31.2 us; the launch traced here: 31 us
  Pallas kernels  15.7 us (50%)
  starting transfers between devices  10.8 us (35%)
  waiting for transfers between devices  3.18 us (10%)
  local copies, waits for them, and re-layouts  1.11 us (4%)
    ppermute x5, starting transfers between devices, passed_along(): lax.ppermute(shard, 'seq', [(i, i + 1) for i in range(first, length - 1,...  10.8 us
    pallas_call x3, Pallas kernels, mix(): pl.pallas_call(functools.partial(mix_kernel, first, out is not None, len(...  6.91 us
    ppermute x5, waiting for transfers between devices, passed_along(): lax.ppermute(shard, 'seq', [(i, i + 1) for i in range(first, length - 1,...  3.18 us
    pallas_call x1, Pallas kernels, second_gate(): pl.pallas_call(functools.partial(second_gate_kernel, first), in_specs=[VM...  2.52 us
    pallas_call x1, Pallas kernels, prepare(): pl.pallas_call(functools.partial(prepare_kernel, firsts), in_specs=[VMEM]...  2.04 us
    pallas_call x1, Pallas kernels, gate(): pl.pallas_call(functools.partial(gate_kernel, firsts), in_specs=[VMEM] *...  1.7 us
    pallas_call x1, Pallas kernels, last_mix(): pl.pallas_call(functools.partial(last_mix_kernel, first, len(heads)), in_...  1.33 us
    unnamed x12, local copies, waits for them, and re-layouts  1.11 us
  transfers between devices with their start and end apart: 5, of which 2 were waited for; matrix products, arithmetic and copies ran while one was open for 0% of the time, Pallas kernels for 46%

profile of v8, /device:TPU:16, one launch (start us, length us, event | category | flops | bytes accessed | tf_op | source)
XLA Modules:
  0.0 31.0 jit_solution(1695253289886747232)
XLA Ops:
  0.0 0.0 copy-start
  0.0 0.0 copy-start.1
  0.0 0.0 copy-start.2
  0.0 0.0 copy-start.3
  0.0 0.2 gate_first.1.begun_ref
  0.2 0.0 copy-start.5
  0.2 1.6 %collective-permute-start = (bf16[144,2304]{1,0:T(8,128)(2,1)S(1)}, bf16[144,2304]{1,0:T(8,128)(2,1)S(1)}, u32[]{:S(2)}, u32[]{:S(2)}) collective-permute-start(bf16[144,2304]{1,0:T(8,128)(2,1)S(1)} %gate_first.1.begun_ref), channel_id=1, source_target_pairs={{1,2},{3,4},{5,6},{7,8},{9,10},{11,12},{13,14},{17,18},{19,20},{21... | collective-permute-start | bytes 1990664 | tf_op jit(solution)/shard_map/ppermute | solution.py:26
  1.8 0.0 copy-done
  1.8 0.5 %copy-done.1 = bf16[128,8192]{1,0:T(8,128)(2,1)S(1)} copy-done((bf16[128,8192]{1,0:T(8,128)(2,1)S(1)}, bf16[128,8192]{1,0:T(8,128)(2,1)}, u32[]{:S(2)}) %copy-start.1) | copy-done | bytes 2097176
  2.2 0.6 %copy-done.2 = bf16[128,8192]{1,0:T(8,128)(2,1)S(1)} copy-done((bf16[128,8192]{1,0:T(8,128)(2,1)S(1)}, bf16[128,8192]{1,0:T(8,128)(2,1)}, u32[]{:S(2)}) %copy-start.2) | copy-done | bytes 2097176
  2.9 0.0 copy-done.3
  2.9 2.5 %gate_second.1 = (bf16[144,2304]{1,0:T(8,128)(2,1)S(1)}, bf16[128,2560]{1,0:T(8,128)(2,1)S(1)}) custom-call(bf16[128,8192]{1,0:T(8,128)(2,1)S(1)} %copy-done.1, bf16[128,8192]{1,0:T(8,128)(2,1)S(1)} %copy-done.2, bf16[128,8192]{1,0:T(8,128)(2,1)S(1)} %copy-done, f32[3,3,8192]{2,1,0:T(4,128)S(1)} %copy-done.3, bf16[144,2304]{1,0:T(8,128)(2,1)S(1)} %gate_first.1.begun_ref), custom_call_target="tpu_custom_call" | custom-call | flops 1000 | bytes 1000 | tf_op jit(solution)/shard_map/gate_second/pallas_call | solution.py:184
  5.4 1.9 %collective-permute-start.1 = (bf16[144,2304]{1,0:T(8,128)(2,1)S(1)}, bf16[144,2304]{1,0:T(8,128)(2,1)S(1)}, u32[]{:S(2)}, u32[]{:S(2)}) collective-permute-start(bf16[144,2304]{1,0:T(8,128)(2,1)S(1)} %get-tuple-element.31.own_ref), channel_id=1, source_target_pairs={{0,1},{2,3},{4,5},{6,7},{8,9},{10,11},{12,13},{14,15},{16,17},{18,... | collective-permute-start | bytes 1990664 | tf_op jit(solution)/shard_map/ppermute | solution.py:26
  7.3 1.9 %collective-permute-start.3 = (bf16[128,2560]{1,0:T(8,128)(2,1)S(1)}, bf16[128,2560]{1,0:T(8,128)(2,1)S(1)}, u32[]{:S(2)}, u32[]{:S(2)}) collective-permute-start(bf16[128,2560]{1,0:T(8,128)(2,1)S(1)} %get-tuple-element.28._.own_ref), channel_id=1, source_target_pairs={{0,1},{1,2},{2,3},{3,4},{4,5},{5,6},{6,7},{7,8},{8,9},{9,10},{10,1... | collective-permute-start | bytes 1966088 | tf_op jit(solution)/shard_map/ppermute | solution.py:26
  9.2 0.0 copy-done.5
  9.2 1.7 %gate.1 = (f32[512,128]{1,0:T(8,128)S(1)}, bf16[64,256]{1,0:T(8,128)(2,1)S(1)}, bf16[128,2304]{1,0:T(8,128)(2,1)S(1)}, bf16[128,1024]{1,0:T(8,128)(2,1)S(1)}) custom-call(bf16[128,8192]{1,0:T(8,128)(2,1)S(1)} %copy-done.1, bf16[128,8192]{1,0:T(8,128)(2,1)S(1)} %copy-done.2, bf16[128,8192]{1,0:T(8,128)(2,1)S(1)} %copy-done, f32[3,3,8192]{2,1,0:T(4,128)S(1)} %copy-done.3, ...), custom_call_target="tpu_custom_call" | custom-call | flops 1000 | bytes 1000 | tf_op jit(solution)/shard_map/gate/pallas_call | solution.py:207
  10.9 3.5 %collective-permute-start.4 = (bf16[128,2304]{1,0:T(8,128)(2,1)S(1)}, bf16[128,2304]{1,0:T(8,128)(2,1)S(1)}, u32[]{:S(2)}, u32[]{:S(2)}) collective-permute-start(bf16[128,2304]{1,0:T(8,128)(2,1)S(1)} %get-tuple-element.40.own_ref), channel_id=1, source_target_pairs={{0,1},{1,2},{2,3},{3,4},{4,5},{5,6},{6,7},{7,8},{8,9},{9,10},{10,1... | collective-permute-start | bytes 1769480 | tf_op jit(solution)/shard_map/ppermute | solution.py:26
  14.5 0.0 collective-permute-done.in_ref
  14.5 0.0 collective-permute-done.1.near_ref
  14.5 0.0 copy-start.4
  14.5 1.0 %gate_last.1 = (bf16[136,1024]{1,0:T(8,128)(2,1)S(1)}, bf16[16,8192]{1,0:T(8,128)(2,1)S(1)}, bf16[144,2304]{1,0:T(8,128)(2,1)S(1)}) custom-call(bf16[128,8192]{1,0:T(8,128)(2,1)S(1)} %copy-done.1, bf16[128,8192]{1,0:T(8,128)(2,1)S(1)} %copy-done.2, f32[3,3,8192]{2,1,0:T(4,128)S(1)} %copy-done.3, bf16[144,2304]{1,0:T(8,128)(2,1)S(1)} %settle.1.crossed_ref, ...), custom_call_target="tpu_custom_call" | custom-call | flops 1000 | bytes 1000 | tf_op jit(solution)/shard_map/gate_last/pallas_call | solution.py:274
  15.6 1.9 %collective-permute-start.2 = (bf16[136,1024]{1,0:T(8,128)(2,1)S(1)}, bf16[136,1024]{1,0:T(8,128)(2,1)S(1)}, u32[]{:S(2)}, u32[]{:S(2)}) collective-permute-start(bf16[136,1024]{1,0:T(8,128)(2,1)S(1)} %get-tuple-element.33.own_ref), channel_id=1, source_target_pairs={{0,1},{1,2},{2,3},{3,4},{4,5},{5,6},{6,7},{7,8},{8,9},{9,10},{10,1... | collective-permute-start | bytes 835592 | tf_op jit(solution)/shard_map/ppermute | solution.py:26
  17.5 0.0 copy-done.4
  17.5 2.0 %prepare.1 = (bf16[18,256,256]{2,1,0:T(8,128)(2,1)S(1)}, f32[128,2304]{1,0:T(8,128)S(1)}, bf16[8,256,256]{2,1,0:T(8,128)(2,1)S(1)}, f32[128,1024]{1,0:T(8,128)S(1)}, f32[128,1024]{1,0:T(8,128)S(1)}) custom-call(f32[512,128]{1,0:T(8,128)S(1)} %get-tuple-element.29.turned_ref, bf16[64,256]{1,0:T(8,128)(2,1)S(1)} %get-tuple-element.30.mask_ref, ...), custom_call_target="tpu_custom_call" | custom-call | flops 1000 | bytes 1000 | tf_op jit(solution)/shard_map/prepare/pallas_call | solution.py:396
  19.6 2.4 %mix.3 = (bf16[128,8192]{1,0:T(8,128)(2,1)}, f32[16,2304]{1,0:T(8,128)S(1)}, f32[8,2304]{1,0:T(8,128)S(1)}) custom-call(f32[512,128]{1,0:T(8,128)S(1)} %get-tuple-element.29.turned_ref, bf16[64,256]{1,0:T(8,128)(2,1)S(1)} %get-tuple-element.30.mask_ref, bf16[144,2304]{1,0:T(8,128)(2,1)S(1)} %get-tuple-element.31.own_ref, ...), custom_call_target="tpu_custom_call" | custom-call | flops 1000 | bytes 1000 | tf_op jit(solution)/shard_map/mix/pallas_call | solution.py:524
  21.9 0.0 collective-permute-done.3.got_ref
  21.9 2.5 %mix.4 = (bf16[128,8192]{1,0:T(8,128)(2,1)}, f32[16,2560]{1,0:T(8,128)S(1)}, f32[8,2560]{1,0:T(8,128)S(1)}) custom-call(f32[512,128]{1,0:T(8,128)S(1)} %get-tuple-element.29.turned_ref, bf16[64,256]{1,0:T(8,128)(2,1)S(1)} %get-tuple-element.30.mask_ref, bf16[128,2560]{1,0:T(8,128)(2,1)S(1)} %get-tuple-element.28._.own_ref, ...), custom_call_target="tpu_custom_call", output_to_operand_aliasing={{0}: (8, {})} | custom-call | flops 1000 | bytes 1000 | tf_op jit(solution)/shard_map/mix/pallas_call | solution.py:524
  24.5 2.2 %collective-permute-done.4.got_ref = bf16[128,2304]{1,0:T(8,128)(2,1)S(1)} collective-permute-done((bf16[128,2304]{1,0:T(8,128)(2,1)S(1)}, bf16[128,2304]{1,0:T(8,128)(2,1)S(1)}, u32[]{:S(2)}, u32[]{:S(2)}) %collective-permute-start.4) | collective-permute-done | bytes 589856 | tf_op jit(solution)/shard_map/ppermute | solution.py:26
  26.7 2.0 %mix.5 = (bf16[128,8192]{1,0:T(8,128)(2,1)}, f32[16,2304]{1,0:T(8,128)S(1)}, f32[8,2304]{1,0:T(8,128)S(1)}) custom-call(f32[512,128]{1,0:T(8,128)S(1)} %get-tuple-element.29.turned_ref, bf16[64,256]{1,0:T(8,128)(2,1)S(1)} %get-tuple-element.30.mask_ref, bf16[128,2304]{1,0:T(8,128)(2,1)S(1)} %get-tuple-element.40.own_ref, ...), custom_call_target="tpu_custom_call", output_to_operand_aliasing={{0}: (8, {})} | custom-call | flops 1000 | bytes 1000 | tf_op jit(solution)/shard_map/mix/pallas_call | solution.py:524
  28.7 0.9 %collective-permute-done.2.got_ref = bf16[136,1024]{1,0:T(8,128)(2,1)S(1)} collective-permute-done((bf16[136,1024]{1,0:T(8,128)(2,1)S(1)}, bf16[136,1024]{1,0:T(8,128)(2,1)S(1)}, u32[]{:S(2)}, u32[]{:S(2)}) %collective-permute-start.2) | collective-permute-done | bytes 278560 | tf_op jit(solution)/shard_map/ppermute | solution.py:26
  29.7 1.3 %mix_last.1 = bf16[128,8192]{1,0:T(8,128)(2,1)} custom-call(f32[512,128]{1,0:T(8,128)S(1)} %get-tuple-element.29.turned_ref, bf16[64,256]{1,0:T(8,128)(2,1)S(1)} %get-tuple-element.30.mask_ref, bf16[136,1024]{1,0:T(8,128)(2,1)S(1)} %get-tuple-element.33.own_ref, ...), custom_call_target="tpu_custom_call", output_to_operand_aliasing={{}: (17, {})} | custom-call | flops 1000 | bytes 1000 | tf_op jit(solution)/shard_map/mix_last/pallas_call | solution.py:596
  (1 shorter events, 0.0 us)
Async XLA Ops:
  0.0 1.8 %copy-start = (bf16[128,8192]{1,0:T(8,128)(2,1)S(1)}, bf16[128,8192]{1,0:T(8,128)(2,1)}, u32[]{:S(2)}) copy-start(bf16[128,8192]{1,0:T(8,128)(2,1)} %q_ref.13) | copy-start | bytes 6291460
  0.0 2.2 %copy-start.1 = (bf16[128,8192]{1,0:T(8,128)(2,1)S(1)}, bf16[128,8192]{1,0:T(8,128)(2,1)}, u32[]{:S(2)}) copy-start(bf16[128,8192]{1,0:T(8,128)(2,1)} %k_ref.5) | copy-start | bytes 6291460
  0.0 2.9 %copy-start.2 = (bf16[128,8192]{1,0:T(8,128)(2,1)S(1)}, bf16[128,8192]{1,0:T(8,128)(2,1)}, u32[]{:S(2)}) copy-start(bf16[128,8192]{1,0:T(8,128)(2,1)} %v_ref.5) | copy-start | bytes 6291460
  0.0 2.9 %copy-start.3 = (f32[3,3,8192]{2,1,0:T(4,128)S(1)}, f32[3,3,8192]{2,1,0:T(4,128)}, u32[]{:S(2)}) copy-start(f32[3,3,8192]{2,1,0:T(4,128)} %taps_ref.15) | copy-start | bytes 884740
  0.2 9.0 %copy-start.5 = (bf16[512,128]{1,0:T(8,128)(2,1)S(1)}, bf16[512,128]{1,0:T(8,128)(2,1)}, u32[]{:S(2)}) copy-start(bf16[512,128]{1,0:T(8,128)(2,1)} %h_ref.1) | copy-start | bytes 393220
  0.2 14.3 %collective-permute-start = (bf16[144,2304]{1,0:T(8,128)(2,1)S(1)}, bf16[144,2304]{1,0:T(8,128)(2,1)S(1)}, u32[]{:S(2)}, u32[]{:S(2)}) collective-permute-start(bf16[144,2304]{1,0:T(8,128)(2,1)S(1)} %gate_first.1.begun_ref), channel_id=1, source_target_pairs={{1,2},{3,4},{5,6},{7,8},{9,10},{11,12},{13,14},{17,18},{19,20},{21... | collective-permute-start | bytes 1990664 | tf_op jit(solution)/shard_map/ppermute | solution.py:26
  5.4 9.1 %collective-permute-start.1 = (bf16[144,2304]{1,0:T(8,128)(2,1)S(1)}, bf16[144,2304]{1,0:T(8,128)(2,1)S(1)}, u32[]{:S(2)}, u32[]{:S(2)}) collective-permute-start(bf16[144,2304]{1,0:T(8,128)(2,1)S(1)} %get-tuple-element.31.own_ref), channel_id=1, source_target_pairs={{0,1},{2,3},{4,5},{6,7},{8,9},{10,11},{12,13},{14,15},{16,17},{18,... | collective-permute-start | bytes 1990664 | tf_op jit(solution)/shard_map/ppermute | solution.py:26
  7.3 14.7 %collective-permute-start.3 = (bf16[128,2560]{1,0:T(8,128)(2,1)S(1)}, bf16[128,2560]{1,0:T(8,128)(2,1)S(1)}, u32[]{:S(2)}, u32[]{:S(2)}) collective-permute-start(bf16[128,2560]{1,0:T(8,128)(2,1)S(1)} %get-tuple-element.28._.own_ref), channel_id=1, source_target_pairs={{0,1},{1,2},{2,3},{3,4},{4,5},{5,6},{6,7},{7,8},{8,9},{9,10},{10,1... | collective-permute-start | bytes 1966088 | tf_op jit(solution)/shard_map/ppermute | solution.py:26
  10.9 15.8 %collective-permute-start.4 = (bf16[128,2304]{1,0:T(8,128)(2,1)S(1)}, bf16[128,2304]{1,0:T(8,128)(2,1)S(1)}, u32[]{:S(2)}, u32[]{:S(2)}) collective-permute-start(bf16[128,2304]{1,0:T(8,128)(2,1)S(1)} %get-tuple-element.40.own_ref), channel_id=1, source_target_pairs={{0,1},{1,2},{2,3},{3,4},{4,5},{5,6},{6,7},{7,8},{8,9},{9,10},{10,1... | collective-permute-start | bytes 1769480 | tf_op jit(solution)/shard_map/ppermute | solution.py:26
  14.5 3.0 %copy-start.4 = (f32[8192]{0:T(1024)S(1)}, f32[8192]{0:T(1024)}, u32[]{:S(2)}) copy-start(f32[8192]{0:T(1024)} %param.11) | copy-start | bytes 98308
  15.6 14.1 %collective-permute-start.2 = (bf16[136,1024]{1,0:T(8,128)(2,1)S(1)}, bf16[136,1024]{1,0:T(8,128)(2,1)S(1)}, u32[]{:S(2)}, u32[]{:S(2)}) collective-permute-start(bf16[136,1024]{1,0:T(8,128)(2,1)S(1)} %get-tuple-element.33.own_ref), channel_id=1, source_target_pairs={{0,1},{1,2},{2,3},{3,4},{4,5},{5,6},{6,7},{7,8},{8,9},{9,10},{10,1... | collective-permute-start | bytes 835592 | tf_op jit(solution)/shard_map/ppermute | solution.py:26

commit v9 on v8

--- a/solution.py
+++ b/solution.py
@@ -614,7 +614,7 @@
     rows, width = q_stream.shape
     skip = skip_gain.reshape(1, width)
     unit = width // 32
-    sizes = [9 * unit, 10 * unit, 9 * unit, 4 * unit]
+    sizes = [9 * unit, 10 * unit, 10 * unit, 3 * unit]
     starts = [sum(sizes[:i]) for i in range(len(sizes))]
     streams = (k_stream, v_stream, q_stream, feat_filter)
     begun = first_gate(*streams, sizes[0])

time: 31.2 us -> 31.2 us (level)
  no operation moved by 1% of the time
where the time goes in v9:
time: 31.2 us; the launch traced here: 31 us
  Pallas kernels  15.7 us (50%)
  starting transfers between devices  10.8 us (35%)
  waiting for transfers between devices  3.21 us (10%)
  local copies, waits for them, and re-layouts  1.11 us (4%)
    ppermute x5, starting transfers between devices, passed_along(): lax.ppermute(shard, 'seq', [(i, i + 1) for i in range(first, length - 1,...  10.8 us
    pallas_call x3, Pallas kernels, mix(): pl.pallas_call(functools.partial(mix_kernel, first, out is not None, len(...  7.04 us
    ppermute x5, waiting for transfers between devices, passed_along(): lax.ppermute(shard, 'seq', [(i, i + 1) for i in range(first, length - 1,...  3.21 us
    pallas_call x1, Pallas kernels, second_gate(): pl.pallas_call(functools.partial(second_gate_kernel, first), in_specs=[VM...  2.52 us
    pallas_call x1, Pallas kernels, prepare(): pl.pallas_call(functools.partial(prepare_kernel, firsts), in_specs=[VMEM]...  1.95 us
    pallas_call x1, Pallas kernels, gate(): pl.pallas_call(functools.partial(gate_kernel, firsts), in_specs=[VMEM] *...  1.69 us
    pallas_call x1, Pallas kernels, last_mix(): pl.pallas_call(functools.partial(last_mix_kernel, first, len(heads)), in_...  1.23 us
    unnamed x12, local copies, waits for them, and re-layouts  1.11 us
  transfers between devices with their start and end apart: 5, of which 2 were waited for; matrix products, arithmetic and copies ran while one was open for 0% of the time, Pallas kernels for 46%

profile of v9, /device:TPU:16, one launch (start us, length us, event | category | flops | bytes accessed | tf_op | source)
XLA Modules:
  0.0 31.0 jit_solution(7161322626456614081)
XLA Ops:
  0.0 0.0 copy-start
  0.0 0.0 copy-start.1
  0.0 0.0 copy-start.2
  0.0 0.0 copy-start.3
  0.0 0.2 gate_first.1.begun_ref
  0.2 0.0 copy-start.5
  0.2 1.6 %collective-permute-start = (bf16[144,2304]{1,0:T(8,128)(2,1)S(1)}, bf16[144,2304]{1,0:T(8,128)(2,1)S(1)}, u32[]{:S(2)}, u32[]{:S(2)}) collective-permute-start(bf16[144,2304]{1,0:T(8,128)(2,1)S(1)} %gate_first.1.begun_ref), channel_id=1, source_target_pairs={{1,2},{3,4},{5,6},{7,8},{9,10},{11,12},{13,14},{17,18},{19,20},{21... | collective-permute-start | bytes 1990664 | tf_op jit(solution)/shard_map/ppermute | solution.py:26
  1.8 0.0 copy-done
  1.8 0.5 %copy-done.1 = bf16[128,8192]{1,0:T(8,128)(2,1)S(1)} copy-done((bf16[128,8192]{1,0:T(8,128)(2,1)S(1)}, bf16[128,8192]{1,0:T(8,128)(2,1)}, u32[]{:S(2)}) %copy-start.1) | copy-done | bytes 2097176
  2.2 0.6 %copy-done.2 = bf16[128,8192]{1,0:T(8,128)(2,1)S(1)} copy-done((bf16[128,8192]{1,0:T(8,128)(2,1)S(1)}, bf16[128,8192]{1,0:T(8,128)(2,1)}, u32[]{:S(2)}) %copy-start.2) | copy-done | bytes 2097176
  2.9 0.0 copy-done.3
  2.9 2.5 %gate_second.1 = (bf16[144,2304]{1,0:T(8,128)(2,1)S(1)}, bf16[128,2560]{1,0:T(8,128)(2,1)S(1)}) custom-call(bf16[128,8192]{1,0:T(8,128)(2,1)S(1)} %copy-done.1, bf16[128,8192]{1,0:T(8,128)(2,1)S(1)} %copy-done.2, bf16[128,8192]{1,0:T(8,128)(2,1)S(1)} %copy-done, f32[3,3,8192]{2,1,0:T(4,128)S(1)} %copy-done.3, bf16[144,2304]{1,0:T(8,128)(2,1)S(1)} %gate_first.1.begun_ref), custom_call_target="tpu_custom_call" | custom-call | flops 1000 | bytes 1000 | tf_op jit(solution)/shard_map/gate_second/pallas_call | solution.py:184
  5.4 1.9 %collective-permute-start.1 = (bf16[144,2304]{1,0:T(8,128)(2,1)S(1)}, bf16[144,2304]{1,0:T(8,128)(2,1)S(1)}, u32[]{:S(2)}, u32[]{:S(2)}) collective-permute-start(bf16[144,2304]{1,0:T(8,128)(2,1)S(1)} %get-tuple-element.31.own_ref), channel_id=1, source_target_pairs={{0,1},{2,3},{4,5},{6,7},{8,9},{10,11},{12,13},{14,15},{16,17},{18,... | collective-permute-start | bytes 1990664 | tf_op jit(solution)/shard_map/ppermute | solution.py:26
  7.3 1.9 %collective-permute-start.3 = (bf16[128,2560]{1,0:T(8,128)(2,1)S(1)}, bf16[128,2560]{1,0:T(8,128)(2,1)S(1)}, u32[]{:S(2)}, u32[]{:S(2)}) collective-permute-start(bf16[128,2560]{1,0:T(8,128)(2,1)S(1)} %get-tuple-element.28._.own_ref), channel_id=1, source_target_pairs={{0,1},{1,2},{2,3},{3,4},{4,5},{5,6},{6,7},{7,8},{8,9},{9,10},{10,1... | collective-permute-start | bytes 1966088 | tf_op jit(solution)/shard_map/ppermute | solution.py:26
  9.2 0.0 copy-done.5
  9.2 1.7 %gate.1 = (f32[512,128]{1,0:T(8,128)S(1)}, bf16[64,256]{1,0:T(8,128)(2,1)S(1)}, bf16[128,2560]{1,0:T(8,128)(2,1)S(1)}, bf16[128,768]{1,0:T(8,128)(2,1)S(1)}) custom-call(bf16[128,8192]{1,0:T(8,128)(2,1)S(1)} %copy-done.1, bf16[128,8192]{1,0:T(8,128)(2,1)S(1)} %copy-done.2, bf16[128,8192]{1,0:T(8,128)(2,1)S(1)} %copy-done, f32[3,3,8192]{2,1,0:T(4,128)S(1)} %copy-done.3, ...), custom_call_target="tpu_custom_call" | custom-call | flops 1000 | bytes 1000 | tf_op jit(solution)/shard_map/gate/pallas_call | solution.py:207
  10.9 3.5 %collective-permute-start.4 = (bf16[128,2560]{1,0:T(8,128)(2,1)S(1)}, bf16[128,2560]{1,0:T(8,128)(2,1)S(1)}, u32[]{:S(2)}, u32[]{:S(2)}) collective-permute-start(bf16[128,2560]{1,0:T(8,128)(2,1)S(1)} %get-tuple-element.40.own_ref), channel_id=1, source_target_pairs={{0,1},{1,2},{2,3},{3,4},{4,5},{5,6},{6,7},{7,8},{8,9},{9,10},{10,1... | collective-permute-start | bytes 1966088 | tf_op jit(solution)/shard_map/ppermute | solution.py:26
  14.5 0.0 collective-permute-done.in_ref
  14.5 0.0 collective-permute-done.1.near_ref
  14.5 0.0 copy-start.4
  14.5 1.0 %gate_last.1 = (bf16[144,768]{1,0:T(8,128)(2,1)S(1)}, bf16[16,8192]{1,0:T(8,128)(2,1)S(1)}, bf16[144,2304]{1,0:T(8,128)(2,1)S(1)}) custom-call(bf16[128,8192]{1,0:T(8,128)(2,1)S(1)} %copy-done.1, bf16[128,8192]{1,0:T(8,128)(2,1)S(1)} %copy-done.2, f32[3,3,8192]{2,1,0:T(4,128)S(1)} %copy-done.3, bf16[144,2304]{1,0:T(8,128)(2,1)S(1)} %settle.1.crossed_ref, ...), custom_call_target="tpu_custom_call" | custom-call | flops 1000 | bytes 1000 | tf_op jit(solution)/shard_map/gate_last/pallas_call | solution.py:274
  15.6 1.9 %collective-permute-start.2 = (bf16[144,768]{1,0:T(8,128)(2,1)S(1)}, bf16[144,768]{1,0:T(8,128)(2,1)S(1)}, u32[]{:S(2)}, u32[]{:S(2)}) collective-permute-start(bf16[144,768]{1,0:T(8,128)(2,1)S(1)} %get-tuple-element.33.own_ref), channel_id=1, source_target_pairs={{0,1},{1,2},{2,3},{3,4},{4,5},{5,6},{6,7},{7,8},{8,9},{9,10},{10,1... | collective-permute-start | bytes 663560 | tf_op jit(solution)/shard_map/ppermute | solution.py:26
  17.5 0.0 copy-done.4
  17.5 2.0 %prepare.1 = (bf16[20,256,256]{2,1,0:T(8,128)(2,1)S(1)}, f32[128,2560]{1,0:T(8,128)S(1)}, bf16[6,256,256]{2,1,0:T(8,128)(2,1)S(1)}, f32[128,768]{1,0:T(8,128)S(1)}, f32[128,768]{1,0:T(8,128)S(1)}) custom-call(f32[512,128]{1,0:T(8,128)S(1)} %get-tuple-element.29.turned_ref, bf16[64,256]{1,0:T(8,128)(2,1)S(1)} %get-tuple-element.30.mask_ref, ...), custom_call_target="tpu_custom_call" | custom-call | flops 1000 | bytes 1000 | tf_op jit(solution)/shard_map/prepare/pallas_call | solution.py:396
  19.5 2.4 %mix.3 = (bf16[128,8192]{1,0:T(8,128)(2,1)}, f32[16,2304]{1,0:T(8,128)S(1)}, f32[8,2304]{1,0:T(8,128)S(1)}) custom-call(f32[512,128]{1,0:T(8,128)S(1)} %get-tuple-element.29.turned_ref, bf16[64,256]{1,0:T(8,128)(2,1)S(1)} %get-tuple-element.30.mask_ref, bf16[144,2304]{1,0:T(8,128)(2,1)S(1)} %get-tuple-element.31.own_ref, ...), custom_call_target="tpu_custom_call" | custom-call | flops 1000 | bytes 1000 | tf_op jit(solution)/shard_map/mix/pallas_call | solution.py:524
  21.9 0.0 collective-permute-done.3.got_ref
  21.9 2.5 %mix.4 = (bf16[128,8192]{1,0:T(8,128)(2,1)}, f32[16,2560]{1,0:T(8,128)S(1)}, f32[8,2560]{1,0:T(8,128)S(1)}) custom-call(f32[512,128]{1,0:T(8,128)S(1)} %get-tuple-element.29.turned_ref, bf16[64,256]{1,0:T(8,128)(2,1)S(1)} %get-tuple-element.30.mask_ref, bf16[128,2560]{1,0:T(8,128)(2,1)S(1)} %get-tuple-element.28._.own_ref, ...), custom_call_target="tpu_custom_call", output_to_operand_aliasing={{0}: (8, {})} | custom-call | flops 1000 | bytes 1000 | tf_op jit(solution)/shard_map/mix/pallas_call | solution.py:524
  24.4 3.0 %collective-permute-done.4.got_ref = bf16[128,2560]{1,0:T(8,128)(2,1)S(1)} collective-permute-done((bf16[128,2560]{1,0:T(8,128)(2,1)S(1)}, bf16[128,2560]{1,0:T(8,128)(2,1)S(1)}, u32[]{:S(2)}, u32[]{:S(2)}) %collective-permute-start.4) | collective-permute-done | bytes 655392 | tf_op jit(solution)/shard_map/ppermute | solution.py:26
  27.4 2.2 %mix.5 = (bf16[128,8192]{1,0:T(8,128)(2,1)}, f32[16,2560]{1,0:T(8,128)S(1)}, f32[8,2560]{1,0:T(8,128)S(1)}) custom-call(f32[512,128]{1,0:T(8,128)S(1)} %get-tuple-element.29.turned_ref, bf16[64,256]{1,0:T(8,128)(2,1)S(1)} %get-tuple-element.30.mask_ref, bf16[128,2560]{1,0:T(8,128)(2,1)S(1)} %get-tuple-element.40.own_ref, ...), custom_call_target="tpu_custom_call", output_to_operand_aliasing={{0}: (8, {})} | custom-call | flops 1000 | bytes 1000 | tf_op jit(solution)/shard_map/mix/pallas_call | solution.py:524
  29.6 0.2 collective-permute-done.2.got_ref
  29.8 1.2 %mix_last.1 = bf16[128,8192]{1,0:T(8,128)(2,1)} custom-call(f32[512,128]{1,0:T(8,128)S(1)} %get-tuple-element.29.turned_ref, bf16[64,256]{1,0:T(8,128)(2,1)S(1)} %get-tuple-element.30.mask_ref, bf16[144,768]{1,0:T(8,128)(2,1)S(1)} %get-tuple-element.33.own_ref, bf16[144,768]{1,0:T(8,128)(2,1)S(1)} %collective-permute-done.2.got_ref, ...), custom_call_target="tpu_custom_call", output_to_operand_aliasing={{}: (17, {})} | custom-call | flops 1000 | bytes 1000 | tf_op jit(solution)/shard_map/mix_last/pallas_call | solution.py:596
  (1 shorter events, 0.0 us)
Async XLA Ops:
  0.0 1.8 %copy-start = (bf16[128,8192]{1,0:T(8,128)(2,1)S(1)}, bf16[128,8192]{1,0:T(8,128)(2,1)}, u32[]{:S(2)}) copy-start(bf16[128,8192]{1,0:T(8,128)(2,1)} %q_ref.13) | copy-start | bytes 6291460
  0.0 2.2 %copy-start.1 = (bf16[128,8192]{1,0:T(8,128)(2,1)S(1)}, bf16[128,8192]{1,0:T(8,128)(2,1)}, u32[]{:S(2)}) copy-start(bf16[128,8192]{1,0:T(8,128)(2,1)} %k_ref.5) | copy-start | bytes 6291460
  0.0 2.9 %copy-start.2 = (bf16[128,8192]{1,0:T(8,128)(2,1)S(1)}, bf16[128,8192]{1,0:T(8,128)(2,1)}, u32[]{:S(2)}) copy-start(bf16[128,8192]{1,0:T(8,128)(2,1)} %v_ref.5) | copy-start | bytes 6291460
  0.0 2.9 %copy-start.3 = (f32[3,3,8192]{2,1,0:T(4,128)S(1)}, f32[3,3,8192]{2,1,0:T(4,128)}, u32[]{:S(2)}) copy-start(f32[3,3,8192]{2,1,0:T(4,128)} %taps_ref.15) | copy-start | bytes 884740
  0.2 9.0 %copy-start.5 = (bf16[512,128]{1,0:T(8,128)(2,1)S(1)}, bf16[512,128]{1,0:T(8,128)(2,1)}, u32[]{:S(2)}) copy-start(bf16[512,128]{1,0:T(8,128)(2,1)} %h_ref.1) | copy-start | bytes 393220
  0.2 14.3 %collective-permute-start = (bf16[144,2304]{1,0:T(8,128)(2,1)S(1)}, bf16[144,2304]{1,0:T(8,128)(2,1)S(1)}, u32[]{:S(2)}, u32[]{:S(2)}) collective-permute-start(bf16[144,2304]{1,0:T(8,128)(2,1)S(1)} %gate_first.1.begun_ref), channel_id=1, source_target_pairs={{1,2},{3,4},{5,6},{7,8},{9,10},{11,12},{13,14},{17,18},{19,20},{21... | collective-permute-start | bytes 1990664 | tf_op jit(solution)/shard_map/ppermute | solution.py:26
  5.4 9.1 %collective-permute-start.1 = (bf16[144,2304]{1,0:T(8,128)(2,1)S(1)}, bf16[144,2304]{1,0:T(8,128)(2,1)S(1)}, u32[]{:S(2)}, u32[]{:S(2)}) collective-permute-start(bf16[144,2304]{1,0:T(8,128)(2,1)S(1)} %get-tuple-element.31.own_ref), channel_id=1, source_target_pairs={{0,1},{2,3},{4,5},{6,7},{8,9},{10,11},{12,13},{14,15},{16,17},{18,... | collective-permute-start | bytes 1990664 | tf_op jit(solution)/shard_map/ppermute | solution.py:26
  7.3 14.6 %collective-permute-start.3 = (bf16[128,2560]{1,0:T(8,128)(2,1)S(1)}, bf16[128,2560]{1,0:T(8,128)(2,1)S(1)}, u32[]{:S(2)}, u32[]{:S(2)}) collective-permute-start(bf16[128,2560]{1,0:T(8,128)(2,1)S(1)} %get-tuple-element.28._.own_ref), channel_id=1, source_target_pairs={{0,1},{1,2},{2,3},{3,4},{4,5},{5,6},{6,7},{7,8},{8,9},{9,10},{10,1... | collective-permute-start | bytes 1966088 | tf_op jit(solution)/shard_map/ppermute | solution.py:26
  10.9 16.5 %collective-permute-start.4 = (bf16[128,2560]{1,0:T(8,128)(2,1)S(1)}, bf16[128,2560]{1,0:T(8,128)(2,1)S(1)}, u32[]{:S(2)}, u32[]{:S(2)}) collective-permute-start(bf16[128,2560]{1,0:T(8,128)(2,1)S(1)} %get-tuple-element.40.own_ref), channel_id=1, source_target_pairs={{0,1},{1,2},{2,3},{3,4},{4,5},{5,6},{6,7},{7,8},{8,9},{9,10},{10,1... | collective-permute-start | bytes 1966088 | tf_op jit(solution)/shard_map/ppermute | solution.py:26
  14.5 3.0 %copy-start.4 = (f32[8192]{0:T(1024)S(1)}, f32[8192]{0:T(1024)}, u32[]{:S(2)}) copy-start(f32[8192]{0:T(1024)} %param.11) | copy-start | bytes 98308
  15.6 14.2 %collective-permute-start.2 = (bf16[144,768]{1,0:T(8,128)(2,1)S(1)}, bf16[144,768]{1,0:T(8,128)(2,1)S(1)}, u32[]{:S(2)}, u32[]{:S(2)}) collective-permute-start(bf16[144,768]{1,0:T(8,128)(2,1)S(1)} %get-tuple-element.33.own_ref), channel_id=1, source_target_pairs={{0,1},{1,2},{2,3},{3,4},{4,5},{5,6},{6,7},{7,8},{8,9},{9,10},{10,1... | collective-permute-start | bytes 663560 | tf_op jit(solution)/shard_map/ppermute | solution.py:26
